TPU v7x, 512 devices: a whole 4x4x16 slice. The times are simulated.
512 devices in a mesh: face: 8 (over x, y_lo), tile: 64 (over z, y_hi, core).
Axes of the slice: x: 4, y: 4 (y_hi: 2, y_lo: 2; y = y_hi * 2 + y_lo), z: 16, core: 2. Of those that a mesh axis runs over, the one named last changes fastest.
Arguments:
- maps: bfloat16 [4, 4, 128, 8192], P(None, None, 'face', 'tile'), may hold values from -8 to 8
- params: float32 [4, 2], replicated, may hold values from 0 to 1
- labels: int32 [4], replicated, may hold values 0 or 1
- edge_flip: int32 [8, 64], replicated, may hold values from 0 to 1
- fine_weight: float32 [3, 4, 16], replicated, may hold values from -1.75 to 1.75
- coarse_weight: float32 [3, 16, 32], replicated, may hold values from -0.875 to 0.875
- feature_weight: float32 [32, 128], replicated, may hold values from -2 to 2
- param_weight: float32 [2, 128], replicated, may hold values from -4 to 4
- out_weight: float32 [128], replicated, may hold values from -1 to 1
Outputs:
- logits: float32 [4], replicated
- saliency: float32 [4, 4, 128, 8192], P(None, None, 'face', 'tile')
- grad_fine: float32 [3, 4, 16], replicated
- grad_coarse: float32 [3, 16, 32], replicated
All inputs are finite; a program needn't handle non-finite values.
Results may differ from a plain program's by a relative error of at most 0.0003.
Values sent between devices are 32-bit elements; how exact they have to be, the bound alone decides.
No kernel may reach another device: no remote copies, remote signals or barrier semaphores. Data moves between devices by JAX's collectives and lax.ppermute only.
A program may use at most 64 MiB of HBM per device.

v0:
```python
import jax
import jax.numpy as jnp
from jax import lax
from jax.sharding import PartitionSpec as P

exact = lax.Precision.HIGHEST


def with_halo(block, sides, width):
    for axis, dim in sides:
        count = lax.axis_size(axis)
        forward = [(i, i + 1) for i in range(count - 1)]
        forward.append((count - 1, 0))
        backward = [(target, source) for source, target in forward]
        low = lax.ppermute(
            lax.slice_in_dim(block, block.shape[dim] - width, None, axis=dim), axis, forward
        )
        high = lax.ppermute(lax.slice_in_dim(block, 0, width, axis=dim), axis, backward)
        block = jnp.concatenate([low, block, high], axis=dim)
    return block


def turn_blocks(edge_row, width):
    lead = edge_row.shape[:-1]
    return edge_row.reshape(lead + (-1, width))[..., ::-1].reshape(edge_row.shape)


def face_flags(edge_flip):
    position = lax.axis_index("face")
    faces = edge_flip.shape[0]
    return (edge_flip[position] == 1, edge_flip[(position + 1) % faces] == 1)


def tile_flags(flags):
    tiles = flags[0].shape[0]
    spot = lax.axis_index("tile") % tiles
    return (flags[0][spot], flags[1][spot])


def stencil(padded, flags, width):
    top_flag, bottom_flag = tile_flags(flags)
    left = padded[..., 1:-1, :-2]
    right = padded[..., 1:-1, 2:]
    upper = padded[..., :-2, 1:-1]
    lower = padded[..., 2:, 1:-1]
    top_row = upper[..., 0, :]
    upper = upper.at[..., 0, :].set(jnp.where(top_flag, turn_blocks(top_row, width), top_row))
    bottom_row = lower[..., -1, :]
    lower = lower.at[..., -1, :].set(
        jnp.where(bottom_flag, turn_blocks(bottom_row, width), bottom_row)
    )
    return -0.25 * (upper + lower + left + right)


def fine_apply(field, flags):
    padded = with_halo(field, (("face", 2), ("tile", 3)), 1)
    return stencil(padded, flags, field.shape[-1])


def coarse_apply(field, flags):
    padded = with_halo(field, (("face", 2), ("tile", 3)), 1)
    return stencil(padded, flags, field.shape[-1])


def coarse_terms(field, flags):
    first = coarse_apply(field, flags)
    second = 2.0 * coarse_apply(first, flags) - field
    return (first, second)


def coarse_adjoint(parts, flags):
    inner = coarse_apply(parts[2], flags)
    outer = coarse_apply(parts[1] + 2.0 * inner, flags)
    return parts[0] - parts[2] + outer


def on_device(
    maps,
    params,
    labels,
    edge_flip,
    fine_weight,
    coarse_weight,
    feature_weight,
    param_weight,
    out_weight,
):
    flags = face_flags(edge_flip)
    field0 = maps.astype(jnp.float32)
    first0 = fine_apply(field0, flags)
    second0 = 2.0 * fine_apply(first0, flags) - field0
    terms0 = jnp.stack([field0, first0, second0])
    pre0 = jnp.einsum("kio,kbirc->borc", fine_weight, terms0, precision=exact)
    act0 = jax.nn.softplus(pre0)
    nmaps, nchan, nrows, ncols = act0.shape
    field1 = act0.reshape(nmaps, nchan, nrows // 2, 2, ncols // 2, 2).mean(axis=(3, 5))
    first1, second1 = coarse_terms(field1, flags)
    terms1 = jnp.stack([field1, first1, second1])
    pre1 = jnp.einsum("kio,kbirc->borc", coarse_weight, terms1, precision=exact)
    act1 = jax.nn.softplus(pre1)
    pooled_count = nrows // 2 * lax.axis_size("face") * (ncols // 2) * lax.axis_size("tile")
    features = lax.psum(act1.sum(axis=(2, 3)), ("face", "tile")) / pooled_count
    hidden = jnp.tanh(
        jnp.dot(features, feature_weight, precision=exact)
        + jnp.dot(params, param_weight, precision=exact)
    )
    logits = jnp.dot(hidden, out_weight, precision=exact)
    dlogit = jax.nn.sigmoid(logits) - labels.astype(jnp.float32)
    dhidden = dlogit[:, None] * out_weight[None, :] * (1.0 - hidden * hidden)
    dfeatures = jnp.dot(dhidden, feature_weight.T, precision=exact)
    dpre1 = (dfeatures / pooled_count)[:, :, None, None] * jax.nn.sigmoid(pre1)
    grad_c = jnp.einsum("kbirc,borc->kio", terms1, dpre1, precision=exact)
    parts1 = jnp.einsum("kio,borc->kbirc", coarse_weight, dpre1, precision=exact)
    dfield1 = coarse_adjoint(parts1, flags)
    spread = jnp.broadcast_to(
        dfield1[:, :, :, None, :, None], (nmaps, nchan, nrows // 2, 2, ncols // 2, 2)
    ).reshape(pre0.shape)
    dpre0 = 0.25 * spread * jax.nn.sigmoid(pre0)
    grad_f = jnp.einsum("kbirc,borc->kio", terms0, dpre0, precision=exact)
    parts0 = jnp.einsum("kio,borc->kbirc", fine_weight, dpre0, precision=exact)
    inner0 = fine_apply(parts0[2], flags)
    outer0 = fine_apply(parts0[1] + 2.0 * inner0, flags)
    pixel_count = nrows * lax.axis_size("face") * ncols * lax.axis_size("tile")
    saliency = (parts0[0] - parts0[2] + outer0) * pixel_count
    grad_f, grad_c = lax.psum((grad_f, grad_c), ("face", "tile"))
    return (logits, saliency, grad_f, grad_c)


def solution(mesh):
    in_specs = (P(None, None, "face", "tile"), P(), P(), P(), P(), P(), P(), P(), P())
    out_specs = (P(), P(None, None, "face", "tile"), P(), P())
    return jax.shard_map(
        on_device, mesh=mesh, in_specs=in_specs, out_specs=out_specs, check_vma=False
    )
```

profile of v0, /device:TPU:1, one launch (start us, length us, event | category | flops | bytes accessed | tf_op | source)
XLA Modules:
  0.0 429.5 jit_solution(592526183360856192)
XLA Ops:
  1.6 4.0 collective-permute-start
  5.6 4.1 collective-permute-start.1
  12.0 6.0 %collective-permute-start.2 = (f32[4,4,18,1]{3,1,2,0:T(4,128)S(1)}, f32[4,4,18,1]{3,1,2,0:T(4,128)S(1)}, u32[]{:S(2)}, u32[]{:S(2)}) collective-permute-start(f32[4,4,18,1]{3,1,2,0:T(4,128)S(1)} %get-tuple-element.242), channel_id=1, source_target_pairs={{0,1},{1,2},{2,3},{3,4},{4,5},{5,6},{6,7},{7,8},{8,9},{9,10},{10,1... | collective-permute-start | bytes 3464 | tf_op jit(solution)/shard_map/ppermute | solution.py:15
  18.1 4.5 %collective-permute-start.3 = (f32[4,4,18,1]{3,1,2,0:T(4,128)S(1)}, f32[4,4,18,1]{3,1,2,0:T(4,128)S(1)}, u32[]{:S(2)}, u32[]{:S(2)}) collective-permute-start(f32[4,4,18,1]{3,1,2,0:T(4,128)S(1)} %get-tuple-element.243), channel_id=1, source_target_pairs={{1,0},{2,1},{3,2},{4,3},{5,4},{6,5},{7,6},{8,7},{9,8},{10,9},{11,1... | collective-permute-start | bytes 3464 | tf_op jit(solution)/shard_map/ppermute | solution.py:18
  22.8 1.3 select_dynamic-update-slice_fusion.14
  24.2 1.9 collective-permute-done.3
  26.3 2.6 collective-permute-start.4
  28.9 4.8 %collective-permute-start.5 = (f32[4,4,1,128]{3,1,2,0:T(4,128)S(1)}, f32[4,4,1,128]{3,1,2,0:T(4,128)S(1)}, u32[]{:S(2)}, u32[]{:S(2)}) collective-permute-start(f32[4,4,1,128]{3,1,2,0:T(4,128)S(1)} %get-tuple-element.255), channel_id=1, source_target_pairs={{64,0},{128,64},{192,128},{256,192},{320,256},{384,320},{448,384},... | collective-permute-start | bytes 24584 | tf_op jit(solution)/shard_map/ppermute | solution.py:18
  34.7 2.9 collective-permute-start.6
  37.6 6.9 %collective-permute-start.7 = (f32[4,4,18,1]{3,1,2,0:T(4,128)S(1)}, f32[4,4,18,1]{3,1,2,0:T(4,128)S(1)}, u32[]{:S(2)}, u32[]{:S(2)}) collective-permute-start(f32[4,4,18,1]{3,1,2,0:T(4,128)S(1)} %get-tuple-element.241), channel_id=1, source_target_pairs={{1,0},{2,1},{3,2},{4,3},{5,4},{6,5},{7,6},{8,7},{9,8},{10,9},{11,1... | collective-permute-start | bytes 3464 | tf_op jit(solution)/shard_map/ppermute | solution.py:18
  46.1 1.1 fusion.37
  47.2 1.7 compare_select_fusion.1
  49.0 2.6 copy.39
  51.6 5.6 %reduce_sum.18 = f32[4,16,8,64]{1,3,2,0:T(8,128)S(1)} reduce(f32[4,16,8,2,64,2]{1,5,4,3,2,0:T(2,128)} %bitcast.121, f32[]{:T(128)} %constant.422.clone.1), dimensions={3,5}, to_apply=%region_0.1 | reduce | flops 98304 | bytes 655364 | tf_op jit(solution)/shard_map/reduce_sum | solution.py:96
  57.6 2.5 collective-permute-start.8
  60.1 5.4 %collective-permute-start.9 = (f32[4,16,1,64]{3,1,2,0:T(8,128)S(1)}, f32[4,16,1,64]{3,1,2,0:T(8,128)S(1)}, u32[]{:S(2)}, u32[]{:S(2)}) collective-permute-start(f32[4,16,1,64]{3,1,2,0:T(8,128)S(1)} %get-tuple-element.235), channel_id=1, source_target_pairs={{64,0},{128,64},{192,128},{256,192},{320,256},{384,320},{448,384},... | collective-permute-start | bytes 49160 | tf_op jit(solution)/shard_map/ppermute | solution.py:18
  66.8 2.1 collective-permute-start.10
  68.8 9.0 %collective-permute-start.11 = (f32[4,16,10,1]{3,1,2,0:T(8,128)S(1)}, f32[4,16,10,1]{3,1,2,0:T(8,128)S(1)}, u32[]{:S(2)}, u32[]{:S(2)}) collective-permute-start(f32[4,16,10,1]{3,1,2,0:T(8,128)S(1)} %get-tuple-element.217), channel_id=1, source_target_pairs={{1,0},{2,1},{3,2},{4,3},{5,4},{6,5},{7,6},{8,7},{9,8},{10,9},{11,1... | collective-permute-start | bytes 7688 | tf_op jit(solution)/shard_map/ppermute | solution.py:18
  79.8 1.9 collective-permute-start.12
  81.7 6.2 %collective-permute-start.13 = (f32[4,16,1,64]{3,1,2,0:T(8,128)S(1)}, f32[4,16,1,64]{3,1,2,0:T(8,128)S(1)}, u32[]{:S(2)}, u32[]{:S(2)}) collective-permute-start(f32[4,16,1,64]{3,1,2,0:T(8,128)S(1)} %get-tuple-element.231), channel_id=1, source_target_pairs={{64,0},{128,64},{192,128},{256,192},{320,256},{384,320},{448,384},... | collective-permute-start | bytes 49160 | tf_op jit(solution)/shard_map/ppermute | solution.py:18
  89.1 2.0 collective-permute-start.14
  91.0 11.0 %collective-permute-start.15 = (f32[4,16,10,1]{3,1,2,0:T(8,128)S(1)}, f32[4,16,10,1]{3,1,2,0:T(8,128)S(1)}, u32[]{:S(2)}, u32[]{:S(2)}) collective-permute-start(f32[4,16,10,1]{3,1,2,0:T(8,128)S(1)} %get-tuple-element.215), channel_id=1, source_target_pairs={{1,0},{2,1},{3,2},{4,3},{5,4},{6,5},{7,6},{8,7},{9,8},{10,9},{11,1... | collective-permute-start | bytes 7688 | tf_op jit(solution)/shard_map/ppermute | solution.py:18
  105.7 115.2 %psum.21 = f32[4,32]{1,0:T(4,128)S(1)} all-reduce(f32[4,32]{1,0:T(4,128)S(1)} %get-tuple-element.266), channel_id=1, replica_groups=mesh['face'=8,'tile'=64] {'face','tile'}, use_global_device_ids=true, to_apply=%region_2.3 | all-reduce | flops 128 | bytes 1024 | tf_op jit(solution)/shard_map/psum | solution.py:102
  223.1 1.9 collective-permute-start.16
  225.0 5.5 %collective-permute-start.17 = (f32[4,16,1,64]{3,1,2,0:T(8,128)S(1)}, f32[4,16,1,64]{3,1,2,0:T(8,128)S(1)}, u32[]{:S(2)}, u32[]{:S(2)}) collective-permute-start(f32[4,16,1,64]{3,1,2,0:T(8,128)S(1)} %get-tuple-element.225), channel_id=1, source_target_pairs={{64,0},{128,64},{192,128},{256,192},{320,256},{384,320},{448,384},... | collective-permute-start | bytes 49160 | tf_op jit(solution)/shard_map/ppermute | solution.py:18
  232.4 4.7 %collective-permute-start.18 = (f32[4,16,10,1]{3,1,2,0:T(8,128)}, f32[4,16,10,1]{3,1,2,0:T(8,128)S(1)}, u32[]{:S(2)}, u32[]{:S(2)}) collective-permute-start(f32[4,16,10,1]{3,1,2,0:T(8,128)} %get-tuple-element.212), channel_id=1, source_target_pairs={{0,1},{1,2},{2,3},{3,4},{4,5},{5,6},{6,7},{7,8},{8,9},{9,10},{10,1... | collective-permute-start | bytes 7688 | tf_op jit(solution)/shard_map/ppermute | solution.py:15
  237.1 2.1 collective-permute-start.19
  241.4 8.2 %collective-permute-done.19 = f32[4,16,10,1]{3,1,2,0:T(8,128)S(1)} collective-permute-done((f32[4,16,10,1]{3,1,2,0:T(8,128)S(1)}, f32[4,16,10,1]{3,1,2,0:T(8,128)S(1)}, u32[]{:S(2)}, u32[]{:S(2)}) %collective-permute-start.19) | collective-permute-done | bytes 2592 | tf_op jit(solution)/shard_map/ppermute | solution.py:18
  249.9 1.9 collective-permute-start.20
  251.8 6.1 %collective-permute-start.21 = (f32[4,16,1,64]{3,1,2,0:T(8,128)S(1)}, f32[4,16,1,64]{3,1,2,0:T(8,128)S(1)}, u32[]{:S(2)}, u32[]{:S(2)}) collective-permute-start(f32[4,16,1,64]{3,1,2,0:T(8,128)S(1)} %get-tuple-element.221), channel_id=1, source_target_pairs={{64,0},{128,64},{192,128},{256,192},{320,256},{384,320},{448,384},... | collective-permute-start | bytes 49160 | tf_op jit(solution)/shard_map/ppermute | solution.py:18
  259.8 3.3 collective-permute-start.22
  263.1 1.9 collective-permute-start.23
  266.6 4.3 %collective-permute-done.22 = f32[4,16,10,1]{3,1,2,0:T(8,128)S(1)} collective-permute-done((f32[4,16,10,1]{3,1,2,0:T(8,128)}, f32[4,16,10,1]{3,1,2,0:T(8,128)S(1)}, u32[]{:S(2)}, u32[]{:S(2)}) %collective-permute-start.22) | collective-permute-done | bytes 2592 | tf_op jit(solution)/shard_map/ppermute | solution.py:15
  271.0 4.1 collective-permute-done.23
  275.7 4.0 broadcast_in_dim.2
  279.7 2.8 copy.45
  283.5 1.9 collective-permute-start.24
  285.4 5.5 %collective-permute-start.25 = (f32[4,4,1,128]{3,1,2,0:T(4,128)S(1)}, f32[4,4,1,128]{3,1,2,0:T(4,128)S(1)}, u32[]{:S(2)}, u32[]{:S(2)}) collective-permute-start(f32[4,4,1,128]{3,1,2,0:T(4,128)S(1)} %get-tuple-element.251), channel_id=1, source_target_pairs={{64,0},{128,64},{192,128},{256,192},{320,256},{384,320},{448,384},... | collective-permute-start | bytes 24584 | tf_op jit(solution)/shard_map/ppermute | solution.py:18
  292.1 3.0 collective-permute-start.26
  295.1 1.9 collective-permute-start.27
  298.7 4.3 %collective-permute-done.27 = f32[4,4,18,1]{3,1,2,0:T(4,128)S(1)} collective-permute-done((f32[4,4,18,1]{3,1,2,0:T(4,128)S(1)}, f32[4,4,18,1]{3,1,2,0:T(4,128)S(1)}, u32[]{:S(2)}, u32[]{:S(2)}) %collective-permute-start.27) | collective-permute-done | bytes 1184 | tf_op jit(solution)/shard_map/ppermute | solution.py:18
  303.3 1.9 collective-permute-start.28
  305.2 5.7 %collective-permute-start.29 = (f32[4,4,1,128]{3,1,2,0:T(4,128)S(1)}, f32[4,4,1,128]{3,1,2,0:T(4,128)S(1)}, u32[]{:S(2)}, u32[]{:S(2)}) collective-permute-start(f32[4,4,1,128]{3,1,2,0:T(4,128)S(1)} %get-tuple-element.247), channel_id=1, source_target_pairs={{64,0},{128,64},{192,128},{256,192},{320,256},{384,320},{448,384},... | collective-permute-start | bytes 24584 | tf_op jit(solution)/shard_map/ppermute | solution.py:18
  311.0 1.7 convolution_bitcast_fusion.5
  312.6 103.5 %all-reduce = (f32[3,4,16]{2,1,0:T(4,128)}, f32[3,16,32]{2,1,0:T(8,128)}) all-reduce(f32[3,4,16]{2,1,0:T(4,128)S(1)} %convolution_bitcast_fusion.5, f32[3,16,32]{2,1,0:T(8,128)S(1)} %convolution_bitcast_fusion.4), channel_id=1, replica_groups=mesh['face'=8,'tile'=64] {'face','tile'}, use_global_device_ids=true, to_apply=%region_3.4 | all-reduce | flops 1728 | bytes 13824 | tf_op jit(solution)/shard_map/psum | solution.py:125
  416.4 4.2 collective-permute-start.30
  420.6 1.9 collective-permute-start.31
  424.1 4.4 %collective-permute-done.31 = f32[4,4,18,1]{3,1,2,0:T(4,128)S(1)} collective-permute-done((f32[4,4,18,1]{3,1,2,0:T(4,128)S(1)}, f32[4,4,18,1]{3,1,2,0:T(4,128)S(1)}, u32[]{:S(2)}, u32[]{:S(2)}) %collective-permute-start.31) | collective-permute-done | bytes 1184 | tf_op jit(solution)/shard_map/ppermute | solution.py:18
  (145 shorter events, 31.6 us)
Async XLA Ops:
  0.6 104.0 %copy-start = (f32[3,16,32]{2,1,0:T(8,128)S(1)}, f32[3,16,32]{2,1,0:T(8,128)}, u32[]{:S(2)}) copy-start(f32[3,16,32]{2,1,0:T(8,128)} %param.46) | copy-start | bytes 18436
  0.6 46.6 %copy-start.12 = (f32[3,4,16]{2,1,0:T(4,128)S(1)}, f32[3,4,16]{2,1,0:T(4,128)}, u32[]{:S(2)}) copy-start(f32[3,4,16]{2,1,0:T(4,128)} %param.45) | copy-start | bytes 2308
  1.6 50.0 %copy-start.7 = (f32[1,4,4,16,128]{4,2,0,3,1:T(4,128)}, f32[1,4,4,16,128]{4,2,0,3,1:T(4,128)S(1)}, u32[]{:S(2)}) copy-start(f32[1,4,4,16,128]{4,2,0,3,1:T(4,128)S(1)} %get-tuple-element.260) | copy-start | bytes 393220
  1.6 10.3 %collective-permute-start = (f32[4,4,1,128]{3,1,2,0:T(4,128)S(1)}, f32[4,4,1,128]{3,1,2,0:T(4,128)S(1)}, u32[]{:S(2)}, u32[]{:S(2)}) collective-permute-start(f32[4,4,1,128]{3,1,2,0:T(4,128)S(1)} %get-tuple-element.258), channel_id=1, source_target_pairs={{0,64},{64,128},{128,192},{192,256},{256,320},{320,384},{384,448},... | collective-permute-start | bytes 24584 | tf_op jit(solution)/shard_map/ppermute | solution.py:15
  5.6 6.2 %collective-permute-start.1 = (f32[4,4,1,128]{3,1,2,0:T(4,128)S(1)}, f32[4,4,1,128]{3,1,2,0:T(4,128)S(1)}, u32[]{:S(2)}, u32[]{:S(2)}) collective-permute-start(f32[4,4,1,128]{3,1,2,0:T(4,128)S(1)} %get-tuple-element.259), channel_id=1, source_target_pairs={{64,0},{128,64},{192,128},{256,192},{320,256},{384,320},{448,384},... | collective-permute-start | bytes 24584 | tf_op jit(solution)/shard_map/ppermute | solution.py:18
  12.0 12.1 %collective-permute-start.2 = (f32[4,4,18,1]{3,1,2,0:T(4,128)S(1)}, f32[4,4,18,1]{3,1,2,0:T(4,128)S(1)}, u32[]{:S(2)}, u32[]{:S(2)}) collective-permute-start(f32[4,4,18,1]{3,1,2,0:T(4,128)S(1)} %get-tuple-element.242), channel_id=1, source_target_pairs={{0,1},{1,2},{2,3},{3,4},{4,5},{5,6},{6,7},{7,8},{8,9},{9,10},{10,1... | collective-permute-start | bytes 3464 | tf_op jit(solution)/shard_map/ppermute | solution.py:15
  18.1 8.0 %collective-permute-start.3 = (f32[4,4,18,1]{3,1,2,0:T(4,128)S(1)}, f32[4,4,18,1]{3,1,2,0:T(4,128)S(1)}, u32[]{:S(2)}, u32[]{:S(2)}) collective-permute-start(f32[4,4,18,1]{3,1,2,0:T(4,128)S(1)} %get-tuple-element.243), channel_id=1, source_target_pairs={{1,0},{2,1},{3,2},{4,3},{5,4},{6,5},{7,6},{8,7},{9,8},{10,9},{11,1... | collective-permute-start | bytes 3464 | tf_op jit(solution)/shard_map/ppermute | solution.py:18
  26.3 7.4 %collective-permute-start.4 = (f32[4,4,1,128]{3,1,2,0:T(4,128)S(1)}, f32[4,4,1,128]{3,1,2,0:T(4,128)S(1)}, u32[]{:S(2)}, u32[]{:S(2)}) collective-permute-start(f32[4,4,1,128]{3,1,2,0:T(4,128)S(1)} %get-tuple-element.254), channel_id=1, source_target_pairs={{0,64},{64,128},{128,192},{192,256},{256,320},{320,384},{384,448},... | collective-permute-start | bytes 24584 | tf_op jit(solution)/shard_map/ppermute | solution.py:15
  28.9 5.6 %collective-permute-start.5 = (f32[4,4,1,128]{3,1,2,0:T(4,128)S(1)}, f32[4,4,1,128]{3,1,2,0:T(4,128)S(1)}, u32[]{:S(2)}, u32[]{:S(2)}) collective-permute-start(f32[4,4,1,128]{3,1,2,0:T(4,128)S(1)} %get-tuple-element.255), channel_id=1, source_target_pairs={{64,0},{128,64},{192,128},{256,192},{320,256},{384,320},{448,384},... | collective-permute-start | bytes 24584 | tf_op jit(solution)/shard_map/ppermute | solution.py:18
  34.7 11.4 %collective-permute-start.6 = (f32[4,4,18,1]{3,1,2,0:T(4,128)S(1)}, f32[4,4,18,1]{3,1,2,0:T(4,128)S(1)}, u32[]{:S(2)}, u32[]{:S(2)}) collective-permute-start(f32[4,4,18,1]{3,1,2,0:T(4,128)S(1)} %get-tuple-element.240), channel_id=1, source_target_pairs={{0,1},{1,2},{2,3},{3,4},{4,5},{5,6},{6,7},{7,8},{8,9},{9,10},{10,1... | collective-permute-start | bytes 3464 | tf_op jit(solution)/shard_map/ppermute | solution.py:15
  37.6 8.5 %collective-permute-start.7 = (f32[4,4,18,1]{3,1,2,0:T(4,128)S(1)}, f32[4,4,18,1]{3,1,2,0:T(4,128)S(1)}, u32[]{:S(2)}, u32[]{:S(2)}) collective-permute-start(f32[4,4,18,1]{3,1,2,0:T(4,128)S(1)} %get-tuple-element.241), channel_id=1, source_target_pairs={{1,0},{2,1},{3,2},{4,3},{5,4},{6,5},{7,6},{8,7},{9,8},{10,9},{11,1... | collective-permute-start | bytes 3464 | tf_op jit(solution)/shard_map/ppermute | solution.py:18
  47.2 4.4 %copy-start.5 = (f32[1,4,4,16,128]{4,2,0,3,1:T(4,128)}, f32[1,4,4,16,128]{4,2,0,3,1:T(4,128)S(1)}, u32[]{:S(2)}) copy-start(f32[1,4,4,16,128]{4,2,0,3,1:T(4,128)S(1)} %fusion.37) | copy-start | bytes 393220
  57.6 8.0 %collective-permute-start.8 = (f32[4,16,1,64]{3,1,2,0:T(8,128)S(1)}, f32[4,16,1,64]{3,1,2,0:T(8,128)S(1)}, u32[]{:S(2)}, u32[]{:S(2)}) collective-permute-start(f32[4,16,1,64]{3,1,2,0:T(8,128)S(1)} %get-tuple-element.234), channel_id=1, source_target_pairs={{0,64},{64,128},{128,192},{192,256},{256,320},{320,384},{384,448},... | collective-permute-start | bytes 49160 | tf_op jit(solution)/shard_map/ppermute | solution.py:15
  60.1 6.4 %collective-permute-start.9 = (f32[4,16,1,64]{3,1,2,0:T(8,128)S(1)}, f32[4,16,1,64]{3,1,2,0:T(8,128)S(1)}, u32[]{:S(2)}, u32[]{:S(2)}) collective-permute-start(f32[4,16,1,64]{3,1,2,0:T(8,128)S(1)} %get-tuple-element.235), channel_id=1, source_target_pairs={{64,0},{128,64},{192,128},{256,192},{320,256},{384,320},{448,384},... | collective-permute-start | bytes 49160 | tf_op jit(solution)/shard_map/ppermute | solution.py:18
  66.8 12.6 %collective-permute-start.10 = (f32[4,16,10,1]{3,1,2,0:T(8,128)S(1)}, f32[4,16,10,1]{3,1,2,0:T(8,128)S(1)}, u32[]{:S(2)}, u32[]{:S(2)}) collective-permute-start(f32[4,16,10,1]{3,1,2,0:T(8,128)S(1)} %get-tuple-element.216), channel_id=1, source_target_pairs={{0,1},{1,2},{2,3},{3,4},{4,5},{5,6},{6,7},{7,8},{8,9},{9,10},{10,1... | collective-permute-start | bytes 7688 | tf_op jit(solution)/shard_map/ppermute | solution.py:15
  68.8 10.6 %collective-permute-start.11 = (f32[4,16,10,1]{3,1,2,0:T(8,128)S(1)}, f32[4,16,10,1]{3,1,2,0:T(8,128)S(1)}, u32[]{:S(2)}, u32[]{:S(2)}) collective-permute-start(f32[4,16,10,1]{3,1,2,0:T(8,128)S(1)} %get-tuple-element.217), channel_id=1, source_target_pairs={{1,0},{2,1},{3,2},{4,3},{5,4},{6,5},{7,6},{8,7},{9,8},{10,9},{11,1... | collective-permute-start | bytes 7688 | tf_op jit(solution)/shard_map/ppermute | solution.py:18
  79.7 141.2 %copy-start.9 = (f32[32,128]{1,0:T(8,128)S(1)}, f32[32,128]{1,0:T(8,128)}, u32[]{:S(2)}) copy-start(f32[32,128]{1,0:T(8,128)} %param.47) | copy-start | bytes 49156
  79.7 141.3 %copy-start.10 = (f32[4,2]{0,1:T(2,128)S(1)}, f32[4,2]{0,1:T(2,128)}, u32[]{:S(2)}) copy-start(f32[4,2]{0,1:T(2,128)} %param.42) | copy-start | bytes 100
  79.7 141.3 %copy-start.11 = (f32[2,128]{1,0:T(2,128)S(1)}, f32[2,128]{1,0:T(2,128)}, u32[]{:S(2)}) copy-start(f32[2,128]{1,0:T(2,128)} %param.48) | copy-start | bytes 3076
  79.7 141.5 %copy-start.13 = (s32[4]{0:T(128)S(1)}, s32[4]{0:T(128)}, u32[]{:S(2)}) copy-start(s32[4]{0:T(128)} %param.43) | copy-start | bytes 52
  79.8 141.5 %copy-start.14 = (f32[128]{0:T(128)S(1)}, f32[128]{0:T(128)}, u32[]{:S(2)}) copy-start(f32[128]{0:T(128)} %param.49) | copy-start | bytes 1540
  79.8 8.1 %collective-permute-start.12 = (f32[4,16,1,64]{3,1,2,0:T(8,128)S(1)}, f32[4,16,1,64]{3,1,2,0:T(8,128)S(1)}, u32[]{:S(2)}, u32[]{:S(2)}) collective-permute-start(f32[4,16,1,64]{3,1,2,0:T(8,128)S(1)} %get-tuple-element.230), channel_id=1, source_target_pairs={{0,64},{64,128},{128,192},{192,256},{256,320},{320,384},{384,448},... | collective-permute-start | bytes 49160 | tf_op jit(solution)/shard_map/ppermute | solution.py:15
  81.7 7.2 %collective-permute-start.13 = (f32[4,16,1,64]{3,1,2,0:T(8,128)S(1)}, f32[4,16,1,64]{3,1,2,0:T(8,128)S(1)}, u32[]{:S(2)}, u32[]{:S(2)}) collective-permute-start(f32[4,16,1,64]{3,1,2,0:T(8,128)S(1)} %get-tuple-element.231), channel_id=1, source_target_pairs={{64,0},{128,64},{192,128},{256,192},{320,256},{384,320},{448,384},... | collective-permute-start | bytes 49160 | tf_op jit(solution)/shard_map/ppermute | solution.py:18
  89.1 14.6 %collective-permute-start.14 = (f32[4,16,10,1]{3,1,2,0:T(8,128)S(1)}, f32[4,16,10,1]{3,1,2,0:T(8,128)S(1)}, u32[]{:S(2)}, u32[]{:S(2)}) collective-permute-start(f32[4,16,10,1]{3,1,2,0:T(8,128)S(1)} %get-tuple-element.214), channel_id=1, source_target_pairs={{0,1},{1,2},{2,3},{3,4},{4,5},{5,6},{6,7},{7,8},{8,9},{9,10},{10,1... | collective-permute-start | bytes 7688 | tf_op jit(solution)/shard_map/ppermute | solution.py:15
  91.0 12.6 %collective-permute-start.15 = (f32[4,16,10,1]{3,1,2,0:T(8,128)S(1)}, f32[4,16,10,1]{3,1,2,0:T(8,128)S(1)}, u32[]{:S(2)}, u32[]{:S(2)}) collective-permute-start(f32[4,16,10,1]{3,1,2,0:T(8,128)S(1)} %get-tuple-element.215), channel_id=1, source_target_pairs={{1,0},{2,1},{3,2},{4,3},{5,4},{6,5},{7,6},{8,7},{9,8},{10,9},{11,1... | collective-permute-start | bytes 7688 | tf_op jit(solution)/shard_map/ppermute | solution.py:18
  104.0 0.7 copy-start.1
  104.0 1.7 copy-start.3
  223.1 7.4 %collective-permute-start.16 = (f32[4,16,1,64]{3,1,2,0:T(8,128)S(1)}, f32[4,16,1,64]{3,1,2,0:T(8,128)S(1)}, u32[]{:S(2)}, u32[]{:S(2)}) collective-permute-start(f32[4,16,1,64]{3,1,2,0:T(8,128)S(1)} %get-tuple-element.224), channel_id=1, source_target_pairs={{0,64},{64,128},{128,192},{192,256},{256,320},{320,384},{384,448},... | collective-permute-start | bytes 49160 | tf_op jit(solution)/shard_map/ppermute | solution.py:15
  225.0 6.5 %collective-permute-start.17 = (f32[4,16,1,64]{3,1,2,0:T(8,128)S(1)}, f32[4,16,1,64]{3,1,2,0:T(8,128)S(1)}, u32[]{:S(2)}, u32[]{:S(2)}) collective-permute-start(f32[4,16,1,64]{3,1,2,0:T(8,128)S(1)} %get-tuple-element.225), channel_id=1, source_target_pairs={{64,0},{128,64},{192,128},{256,192},{320,256},{384,320},{448,384},... | collective-permute-start | bytes 49160 | tf_op jit(solution)/shard_map/ppermute | solution.py:18
  232.4 9.0 %collective-permute-start.18 = (f32[4,16,10,1]{3,1,2,0:T(8,128)}, f32[4,16,10,1]{3,1,2,0:T(8,128)S(1)}, u32[]{:S(2)}, u32[]{:S(2)}) collective-permute-start(f32[4,16,10,1]{3,1,2,0:T(8,128)} %get-tuple-element.212), channel_id=1, source_target_pairs={{0,1},{1,2},{2,3},{3,4},{4,5},{5,6},{6,7},{7,8},{8,9},{9,10},{10,1... | collective-permute-start | bytes 7688 | tf_op jit(solution)/shard_map/ppermute | solution.py:15
  237.1 12.5 %collective-permute-start.19 = (f32[4,16,10,1]{3,1,2,0:T(8,128)S(1)}, f32[4,16,10,1]{3,1,2,0:T(8,128)S(1)}, u32[]{:S(2)}, u32[]{:S(2)}) collective-permute-start(f32[4,16,10,1]{3,1,2,0:T(8,128)S(1)} %get-tuple-element.213), channel_id=1, source_target_pairs={{1,0},{2,1},{3,2},{4,3},{5,4},{6,5},{7,6},{8,7},{9,8},{10,9},{11,1... | collective-permute-start | bytes 7688 | tf_op jit(solution)/shard_map/ppermute | solution.py:18
  249.9 8.0 %collective-permute-start.20 = (f32[4,16,1,64]{3,1,2,0:T(8,128)S(1)}, f32[4,16,1,64]{3,1,2,0:T(8,128)S(1)}, u32[]{:S(2)}, u32[]{:S(2)}) collective-permute-start(f32[4,16,1,64]{3,1,2,0:T(8,128)S(1)} %get-tuple-element.220), channel_id=1, source_target_pairs={{0,64},{64,128},{128,192},{192,256},{256,320},{320,384},{384,448},... | collective-permute-start | bytes 49160 | tf_op jit(solution)/shard_map/ppermute | solution.py:15
  251.8 7.1 %collective-permute-start.21 = (f32[4,16,1,64]{3,1,2,0:T(8,128)S(1)}, f32[4,16,1,64]{3,1,2,0:T(8,128)S(1)}, u32[]{:S(2)}, u32[]{:S(2)}) collective-permute-start(f32[4,16,1,64]{3,1,2,0:T(8,128)S(1)} %get-tuple-element.221), channel_id=1, source_target_pairs={{64,0},{128,64},{192,128},{256,192},{320,256},{384,320},{448,384},... | collective-permute-start | bytes 49160 | tf_op jit(solution)/shard_map/ppermute | solution.py:18
  259.8 11.1 %collective-permute-start.22 = (f32[4,16,10,1]{3,1,2,0:T(8,128)}, f32[4,16,10,1]{3,1,2,0:T(8,128)S(1)}, u32[]{:S(2)}, u32[]{:S(2)}) collective-permute-start(f32[4,16,10,1]{3,1,2,0:T(8,128)} %get-tuple-element.210), channel_id=1, source_target_pairs={{0,1},{1,2},{2,3},{3,4},{4,5},{5,6},{6,7},{7,8},{8,9},{9,10},{10,1... | collective-permute-start | bytes 7688 | tf_op jit(solution)/shard_map/ppermute | solution.py:15
  263.1 11.9 %collective-permute-start.23 = (f32[4,16,10,1]{3,1,2,0:T(8,128)S(1)}, f32[4,16,10,1]{3,1,2,0:T(8,128)S(1)}, u32[]{:S(2)}, u32[]{:S(2)}) collective-permute-start(f32[4,16,10,1]{3,1,2,0:T(8,128)S(1)} %get-tuple-element.211), channel_id=1, source_target_pairs={{1,0},{2,1},{3,2},{4,3},{5,4},{6,5},{7,6},{8,7},{9,8},{10,9},{11,1... | collective-permute-start | bytes 7688 | tf_op jit(solution)/shard_map/ppermute | solution.py:18
  275.7 6.9 %copy-start.15 = (f32[4,16,16,128]{3,1,2,0:T(8,128)S(1)}, f32[4,16,16,128]{3,1,2,0:T(8,128)}, u32[]{:S(2)}) copy-start(f32[4,16,16,128]{3,1,2,0:T(8,128)} %get-tuple-element.265) | copy-start | bytes 1572868
  279.7 11.2 %copy-start.2 = (f32[1,4,16,8,64]{4,2,0,3,1:T(8,128)S(1)}, f32[1,4,16,8,64]{4,2,0,3,1:T(8,128)}, u32[]{:S(2)}) copy-start(f32[1,4,16,8,64]{4,2,0,3,1:T(8,128)} %copy-done.1) | copy-start | bytes 393220
  279.7 11.2 %copy-start.4 = (f32[1,4,16,8,64]{4,2,0,3,1:T(8,128)S(1)}, f32[1,4,16,8,64]{4,2,0,3,1:T(8,128)}, u32[]{:S(2)}) copy-start(f32[1,4,16,8,64]{4,2,0,3,1:T(8,128)} %copy-done.3) | copy-start | bytes 393220
  282.6 28.4 %copy-start.6 = (f32[1,4,4,16,128]{4,2,0,3,1:T(4,128)S(1)}, f32[1,4,4,16,128]{4,2,0,3,1:T(4,128)}, u32[]{:S(2)}) copy-start(f32[1,4,4,16,128]{4,2,0,3,1:T(4,128)} %copy-done.5) | copy-start | bytes 393220
  282.6 28.4 %copy-start.8 = (f32[1,4,4,16,128]{4,2,0,3,1:T(4,128)S(1)}, f32[1,4,4,16,128]{4,2,0,3,1:T(4,128)}, u32[]{:S(2)}) copy-start(f32[1,4,4,16,128]{4,2,0,3,1:T(4,128)} %copy-done.7) | copy-start | bytes 393220
  283.5 8.3 %collective-permute-start.24 = (f32[4,4,1,128]{3,1,2,0:T(4,128)S(1)}, f32[4,4,1,128]{3,1,2,0:T(4,128)S(1)}, u32[]{:S(2)}, u32[]{:S(2)}) collective-permute-start(f32[4,4,1,128]{3,1,2,0:T(4,128)S(1)} %get-tuple-element.250), channel_id=1, source_target_pairs={{0,64},{64,128},{128,192},{192,256},{256,320},{320,384},{384,448},... | collective-permute-start | bytes 24584 | tf_op jit(solution)/shard_map/ppermute | solution.py:15
  285.4 6.4 %collective-permute-start.25 = (f32[4,4,1,128]{3,1,2,0:T(4,128)S(1)}, f32[4,4,1,128]{3,1,2,0:T(4,128)S(1)}, u32[]{:S(2)}, u32[]{:S(2)}) collective-permute-start(f32[4,4,1,128]{3,1,2,0:T(4,128)S(1)} %get-tuple-element.251), channel_id=1, source_target_pairs={{64,0},{128,64},{192,128},{256,192},{320,256},{384,320},{448,384},... | collective-permute-start | bytes 24584 | tf_op jit(solution)/shard_map/ppermute | solution.py:18
  292.1 6.6 %collective-permute-start.26 = (f32[4,4,18,1]{3,1,2,0:T(4,128)S(1)}, f32[4,4,18,1]{3,1,2,0:T(4,128)S(1)}, u32[]{:S(2)}, u32[]{:S(2)}) collective-permute-start(f32[4,4,18,1]{3,1,2,0:T(4,128)S(1)} %get-tuple-element.238), channel_id=1, source_target_pairs={{0,1},{1,2},{2,3},{3,4},{4,5},{5,6},{6,7},{7,8},{8,9},{9,10},{10,1... | collective-permute-start | bytes 3464 | tf_op jit(solution)/shard_map/ppermute | solution.py:15
  295.1 8.0 %collective-permute-start.27 = (f32[4,4,18,1]{3,1,2,0:T(4,128)S(1)}, f32[4,4,18,1]{3,1,2,0:T(4,128)S(1)}, u32[]{:S(2)}, u32[]{:S(2)}) collective-permute-start(f32[4,4,18,1]{3,1,2,0:T(4,128)S(1)} %get-tuple-element.239), channel_id=1, source_target_pairs={{1,0},{2,1},{3,2},{4,3},{5,4},{6,5},{7,6},{8,7},{9,8},{10,9},{11,1... | collective-permute-start | bytes 3464 | tf_op jit(solution)/shard_map/ppermute | solution.py:18
  303.3 112.9 %collective-permute-start.28 = (f32[4,4,1,128]{3,1,2,0:T(4,128)S(1)}, f32[4,4,1,128]{3,1,2,0:T(4,128)S(1)}, u32[]{:S(2)}, u32[]{:S(2)}) collective-permute-start(f32[4,4,1,128]{3,1,2,0:T(4,128)S(1)} %get-tuple-element.246), channel_id=1, source_target_pairs={{0,64},{64,128},{128,192},{192,256},{256,320},{320,384},{384,448},... | collective-permute-start | bytes 24584 | tf_op jit(solution)/shard_map/ppermute | solution.py:15
  305.2 110.9 %collective-permute-start.29 = (f32[4,4,1,128]{3,1,2,0:T(4,128)S(1)}, f32[4,4,1,128]{3,1,2,0:T(4,128)S(1)}, u32[]{:S(2)}, u32[]{:S(2)}) collective-permute-start(f32[4,4,1,128]{3,1,2,0:T(4,128)S(1)} %get-tuple-element.247), channel_id=1, source_target_pairs={{64,0},{128,64},{192,128},{256,192},{320,256},{384,320},{448,384},... | collective-permute-start | bytes 24584 | tf_op jit(solution)/shard_map/ppermute | solution.py:18
  416.4 7.7 %collective-permute-start.30 = (f32[4,4,18,1]{3,1,2,0:T(4,128)S(1)}, f32[4,4,18,1]{3,1,2,0:T(4,128)S(1)}, u32[]{:S(2)}, u32[]{:S(2)}) collective-permute-start(f32[4,4,18,1]{3,1,2,0:T(4,128)S(1)} %get-tuple-element.236), channel_id=1, source_target_pairs={{0,1},{1,2},{2,3},{3,4},{4,5},{5,6},{6,7},{7,8},{8,9},{9,10},{10,1... | collective-permute-start | bytes 3464 | tf_op jit(solution)/shard_map/ppermute | solution.py:15
  420.6 8.0 %collective-permute-start.31 = (f32[4,4,18,1]{3,1,2,0:T(4,128)S(1)}, f32[4,4,18,1]{3,1,2,0:T(4,128)S(1)}, u32[]{:S(2)}, u32[]{:S(2)}) collective-permute-start(f32[4,4,18,1]{3,1,2,0:T(4,128)S(1)} %get-tuple-element.237), channel_id=1, source_target_pairs={{1,0},{2,1},{3,2},{4,3},{5,4},{6,5},{7,6},{8,7},{9,8},{10,9},{11,1... | collective-permute-start | bytes 3464 | tf_op jit(solution)/shard_map/ppermute | solution.py:18
where the time goes:
time: 431 us; the launch traced here: 429 us
  blocking collectives  219 us (51%)
  starting transfers between devices  129 us (30%)
  waiting for transfers between devices  32.8 us (8%)
  other arithmetic  21.7 us (5%)
  local copies, waits for them, and re-layouts  17.1 us (4%)
  matrix products  8.29 us (2%)
    psum x1, blocking collectives, on_device(): features = lax.psum(act1.sum(axis=(2, 3)), ('face', 'tile')) / pooled_count  115 us
    psum x1, blocking collectives, on_device(): grad_f, grad_c = lax.psum((grad_f, grad_c), ('face', 'tile'))  104 us
    ppermute x16, starting transfers between devices, with_halo(): lax.ppermute(lax.slice_in_dim(block, 0, width, axis=dim), axis, backward)  82.5 us
    ppermute x16, starting transfers between devices, with_halo(): lax.ppermute(lax.slice_in_dim(block, block.shape[dim] - width, None, axis...  46.8 us
    ppermute x16, waiting for transfers between devices, with_halo(): lax.ppermute(lax.slice_in_dim(block, 0, width, axis=dim), axis, backward)  27.6 us
  transfers between devices with their start and end apart: 32, of which 13 were waited for; matrix products, arithmetic and copies ran while one was open for 4% of the time, Pallas kernels for 0%

commit v1 on v0

--- a/solution.py
+++ b/solution.py
@@ -74,6 +74,12 @@
     return parts[0] - parts[2] + outer
 
 
+def sum_over(rows, axes):
+    count = lax.axis_size(axes)
+    copies = jnp.broadcast_to(rows[None], (count,) + rows.shape)
+    return lax.all_to_all(copies, axes, 0, 0).sum(axis=0)
+
+
 def on_device(
     maps,
     params,
@@ -99,7 +105,8 @@
     pre1 = jnp.einsum("kio,kbirc->borc", coarse_weight, terms1, precision=exact)
     act1 = jax.nn.softplus(pre1)
     pooled_count = nrows // 2 * lax.axis_size("face") * (ncols // 2) * lax.axis_size("tile")
-    features = lax.psum(act1.sum(axis=(2, 3)), ("face", "tile")) / pooled_count
+    features = sum_over(act1.sum(axis=(2, 3)).reshape(1, -1), ("face", "tile")).reshape(nmaps, -1)
+    features = features / pooled_count
     hidden = jnp.tanh(
         jnp.dot(features, feature_weight, precision=exact)
         + jnp.dot(params, param_weight, precision=exact)
@@ -122,7 +129,13 @@
     outer0 = fine_apply(parts0[1] + 2.0 * inner0, flags)
     pixel_count = nrows * lax.axis_size("face") * ncols * lax.axis_size("tile")
     saliency = (parts0[0] - parts0[2] + outer0) * pixel_count
-    grad_f, grad_c = lax.psum((grad_f, grad_c), ("face", "tile"))
+    packed = jnp.concatenate([grad_f.reshape(-1), grad_c.reshape(-1)])
+    packed = jnp.pad(packed, (0, -packed.size % 1024)).reshape(-1, 128)
+    packed = sum_over(sum_over(packed, "face"), "tile").reshape(-1)
+    grad_f, grad_c = (
+        packed[: grad_f.size].reshape(grad_f.shape),
+        packed[grad_f.size : grad_f.size + grad_c.size].reshape(grad_c.shape),
+    )
     return (logits, saliency, grad_f, grad_c)
 
 

time: 431 us -> 285 us (0.66)
  blocking collectives: 219 us -> 51.1 us
  starting transfers between devices: 129 us -> 142 us
  waiting for transfers between devices: 32.8 us -> 37.3 us
    psum x2 -> x0, blocking collectives: 219 us -> none  [the longest x1 115 us: on_device(): features = lax.psum(act1.sum(axis=(2, 3)), ('face', 'tile')) / pooled_count]
    all_to_all x0 -> x1, blocking collectives: none -> 51.1 us  [sum_over(): return lax.all_to_all(copies, axes, 0, 0).sum(axis=0)]
    all_to_all x0 -> x2, starting transfers between devices: none -> 11.2 us  [sum_over(): return lax.all_to_all(copies, axes, 0, 0).sum(axis=0)]
    all_to_all x0 -> x2, waiting for transfers between devices: none -> 8.08 us  [sum_over(): return lax.all_to_all(copies, axes, 0, 0).sum(axis=0)]
    ppermute x16, starting transfers between devices: 46.8 us -> 51.2 us  [with_halo(): lax.ppermute(lax.slice_in_dim(block, block.shape[dim] - width, None, axis...]
  transfers between devices with their start and end apart: 32 -> 34, of which waited for: 13 -> 13; matrix products, arithmetic and copies ran while one was open for 4% -> 7% of each run, Pallas kernels for 0% -> 0%
where the time goes in v1:
time: 285 us; the launch traced here: 283 us
  starting transfers between devices  142 us (50%)
  blocking collectives  51.1 us (18%)
  waiting for transfers between devices  37.3 us (13%)
  other arithmetic  21.8 us (8%)
  local copies, waits for them, and re-layouts  19.6 us (7%)
  matrix products  9.35 us (3%)
    ppermute x16, starting transfers between devices, with_halo(): lax.ppermute(lax.slice_in_dim(block, 0, width, axis=dim), axis, backward)  80 us
    ppermute x16, starting transfers between devices, with_halo(): lax.ppermute(lax.slice_in_dim(block, block.shape[dim] - width, None, axis...  51.2 us
    all_to_all x1, blocking collectives, sum_over(): return lax.all_to_all(copies, axes, 0, 0).sum(axis=0)  51.1 us
    ppermute x16, waiting for transfers between devices, with_halo(): lax.ppermute(lax.slice_in_dim(block, 0, width, axis=dim), axis, backward)  27.4 us
    all_to_all x2, starting transfers between devices, sum_over(): return lax.all_to_all(copies, axes, 0, 0).sum(axis=0)  11.2 us
    all_to_all x2, waiting for transfers between devices, sum_over(): return lax.all_to_all(copies, axes, 0, 0).sum(axis=0)  8.08 us
    scatter x8, other arithmetic, stencil(): lower.at[..., -1, :]  5.89 us
  transfers between devices with their start and end apart: 34, of which 13 were waited for; matrix products, arithmetic and copies ran while one was open for 7% of the time, Pallas kernels for 0%

profile of v1, /device:TPU:1, one launch (start us, length us, event | category | flops | bytes accessed | tf_op | source)
XLA Modules:
  0.0 283.1 jit_solution(7585744198558361990)
XLA Ops:
  1.6 4.0 %collective-permute-start = (f32[4,4,1,128]{3,1,2,0:T(4,128)S(1)}, f32[4,4,1,128]{3,1,2,0:T(4,128)S(1)}, u32[]{:S(2)}, u32[]{:S(2)}) collective-permute-start(f32[4,4,1,128]{3,1,2,0:T(4,128)S(1)} %get-tuple-element.264), channel_id=1, source_target_pairs={{0,64},{64,128},{128,192},{192,256},{256,320},{320,384},{384,448},... | collective-permute-start | bytes 24584 | tf_op jit(solution)/shard_map/ppermute | solution.py:15
  5.6 4.1 %collective-permute-start.1 = (f32[4,4,1,128]{3,1,2,0:T(4,128)S(1)}, f32[4,4,1,128]{3,1,2,0:T(4,128)S(1)}, u32[]{:S(2)}, u32[]{:S(2)}) collective-permute-start(f32[4,4,1,128]{3,1,2,0:T(4,128)S(1)} %get-tuple-element.265), channel_id=1, source_target_pairs={{64,0},{128,64},{192,128},{256,192},{320,256},{384,320},{448,384},... | collective-permute-start | bytes 24584 | tf_op jit(solution)/shard_map/ppermute | solution.py:18
  11.9 6.0 %collective-permute-start.2 = (f32[4,4,18,1]{3,1,2,0:T(4,128)S(1)}, f32[4,4,18,1]{3,1,2,0:T(4,128)S(1)}, u32[]{:S(2)}, u32[]{:S(2)}) collective-permute-start(f32[4,4,18,1]{3,1,2,0:T(4,128)S(1)} %get-tuple-element.248), channel_id=1, source_target_pairs={{0,1},{1,2},{2,3},{3,4},{4,5},{5,6},{6,7},{7,8},{8,9},{9,10},{10,1... | collective-permute-start | bytes 3464 | tf_op jit(solution)/shard_map/ppermute | solution.py:15
  17.9 4.5 %collective-permute-start.3 = (f32[4,4,18,1]{3,1,2,0:T(4,128)S(1)}, f32[4,4,18,1]{3,1,2,0:T(4,128)S(1)}, u32[]{:S(2)}, u32[]{:S(2)}) collective-permute-start(f32[4,4,18,1]{3,1,2,0:T(4,128)S(1)} %get-tuple-element.249), channel_id=1, source_target_pairs={{1,0},{2,1},{3,2},{4,3},{5,4},{6,5},{7,6},{8,7},{9,8},{10,9},{11,1... | collective-permute-start | bytes 3464 | tf_op jit(solution)/shard_map/ppermute | solution.py:18
  22.7 1.3 select_dynamic-update-slice_fusion.14
  24.0 1.9 collective-permute-done.3
  26.2 2.7 collective-permute-start.4
  28.9 4.7 %collective-permute-start.5 = (f32[4,4,1,128]{3,1,2,0:T(4,128)S(1)}, f32[4,4,1,128]{3,1,2,0:T(4,128)S(1)}, u32[]{:S(2)}, u32[]{:S(2)}) collective-permute-start(f32[4,4,1,128]{3,1,2,0:T(4,128)S(1)} %get-tuple-element.261), channel_id=1, source_target_pairs={{64,0},{128,64},{192,128},{256,192},{320,256},{384,320},{448,384},... | collective-permute-start | bytes 24584 | tf_op jit(solution)/shard_map/ppermute | solution.py:18
  34.5 2.9 %collective-permute-start.6 = (f32[4,4,18,1]{3,1,2,0:T(4,128)S(1)}, f32[4,4,18,1]{3,1,2,0:T(4,128)S(1)}, u32[]{:S(2)}, u32[]{:S(2)}) collective-permute-start(f32[4,4,18,1]{3,1,2,0:T(4,128)S(1)} %get-tuple-element.246), channel_id=1, source_target_pairs={{0,1},{1,2},{2,3},{3,4},{4,5},{5,6},{6,7},{7,8},{8,9},{9,10},{10,1... | collective-permute-start | bytes 3464 | tf_op jit(solution)/shard_map/ppermute | solution.py:15
  37.4 6.9 %collective-permute-start.7 = (f32[4,4,18,1]{3,1,2,0:T(4,128)S(1)}, f32[4,4,18,1]{3,1,2,0:T(4,128)S(1)}, u32[]{:S(2)}, u32[]{:S(2)}) collective-permute-start(f32[4,4,18,1]{3,1,2,0:T(4,128)S(1)} %get-tuple-element.247), channel_id=1, source_target_pairs={{1,0},{2,1},{3,2},{4,3},{5,4},{6,5},{7,6},{8,7},{9,8},{10,9},{11,1... | collective-permute-start | bytes 3464 | tf_op jit(solution)/shard_map/ppermute | solution.py:18
  47.1 1.7 compare_select_fusion.1
  48.8 2.7 copy.63
  51.4 5.6 %reduce_sum.45 = f32[4,16,8,64]{1,3,2,0:T(8,128)S(1)} reduce(f32[4,16,8,2,64,2]{1,5,4,3,2,0:T(2,128)} %bitcast.126, f32[]{:T(128)} %constant.423.clone.1), dimensions={3,5}, to_apply=%region_0.1 | reduce | flops 98304 | bytes 655364 | tf_op jit(solution)/shard_map/reduce_sum | solution.py:102
  57.4 2.5 collective-permute-start.8
  60.0 5.4 %collective-permute-start.9 = (f32[4,16,1,64]{3,1,2,0:T(8,128)S(1)}, f32[4,16,1,64]{3,1,2,0:T(8,128)S(1)}, u32[]{:S(2)}, u32[]{:S(2)}) collective-permute-start(f32[4,16,1,64]{3,1,2,0:T(8,128)S(1)} %get-tuple-element.241), channel_id=1, source_target_pairs={{64,0},{128,64},{192,128},{256,192},{320,256},{384,320},{448,384},... | collective-permute-start | bytes 49160 | tf_op jit(solution)/shard_map/ppermute | solution.py:18
  66.6 2.1 collective-permute-start.10
  68.7 9.0 %collective-permute-start.11 = (f32[4,16,10,1]{3,1,2,0:T(8,128)S(1)}, f32[4,16,10,1]{3,1,2,0:T(8,128)S(1)}, u32[]{:S(2)}, u32[]{:S(2)}) collective-permute-start(f32[4,16,10,1]{3,1,2,0:T(8,128)S(1)} %get-tuple-element.223), channel_id=1, source_target_pairs={{1,0},{2,1},{3,2},{4,3},{5,4},{6,5},{7,6},{8,7},{9,8},{10,9},{11,1... | collective-permute-start | bytes 7688 | tf_op jit(solution)/shard_map/ppermute | solution.py:18
  79.6 1.9 collective-permute-start.12
  81.5 6.3 %collective-permute-start.13 = (f32[4,16,1,64]{3,1,2,0:T(8,128)S(1)}, f32[4,16,1,64]{3,1,2,0:T(8,128)S(1)}, u32[]{:S(2)}, u32[]{:S(2)}) collective-permute-start(f32[4,16,1,64]{3,1,2,0:T(8,128)S(1)} %get-tuple-element.237), channel_id=1, source_target_pairs={{64,0},{128,64},{192,128},{256,192},{320,256},{384,320},{448,384},... | collective-permute-start | bytes 49160 | tf_op jit(solution)/shard_map/ppermute | solution.py:18
  89.0 2.0 collective-permute-start.14
  91.0 11.1 %collective-permute-start.15 = (f32[4,16,10,1]{3,1,2,0:T(8,128)S(1)}, f32[4,16,10,1]{3,1,2,0:T(8,128)S(1)}, u32[]{:S(2)}, u32[]{:S(2)}) collective-permute-start(f32[4,16,10,1]{3,1,2,0:T(8,128)S(1)} %get-tuple-element.221), channel_id=1, source_target_pairs={{1,0},{2,1},{3,2},{4,3},{5,4},{6,5},{7,6},{8,7},{9,8},{10,9},{11,1... | collective-permute-start | bytes 7688 | tf_op jit(solution)/shard_map/ppermute | solution.py:18
  105.2 51.1 %all_to_all.15 = f32[512,1,128]{2,1,0:T(1,128)S(1)} all-to-all(f32[512,1,128]{2,1,0:T(1,128)S(1)} %broadcast_in_dim.13), channel_id=1, replica_groups=mesh['face'=8,'tile'=64] {'face','tile'}, dimensions={0} | all-to-all | bytes 524288 | tf_op jit(solution)/shard_map/all_to_all | solution.py:80
  158.7 1.9 collective-permute-start.16
  160.7 5.5 %collective-permute-start.17 = (f32[4,16,1,64]{3,1,2,0:T(8,128)S(1)}, f32[4,16,1,64]{3,1,2,0:T(8,128)S(1)}, u32[]{:S(2)}, u32[]{:S(2)}) collective-permute-start(f32[4,16,1,64]{3,1,2,0:T(8,128)S(1)} %get-tuple-element.231), channel_id=1, source_target_pairs={{64,0},{128,64},{192,128},{256,192},{320,256},{384,320},{448,384},... | collective-permute-start | bytes 49160 | tf_op jit(solution)/shard_map/ppermute | solution.py:18
  168.1 5.3 %collective-permute-start.18 = (f32[4,16,10,1]{3,1,2,0:T(8,128)}, f32[4,16,10,1]{3,1,2,0:T(8,128)S(1)}, u32[]{:S(2)}, u32[]{:S(2)}) collective-permute-start(f32[4,16,10,1]{3,1,2,0:T(8,128)} %get-tuple-element.218), channel_id=1, source_target_pairs={{0,1},{1,2},{2,3},{3,4},{4,5},{5,6},{6,7},{7,8},{8,9},{9,10},{10,1... | collective-permute-start | bytes 7688 | tf_op jit(solution)/shard_map/ppermute | solution.py:15
  173.3 1.9 collective-permute-start.19
  177.7 7.4 %collective-permute-done.19 = f32[4,16,10,1]{3,1,2,0:T(8,128)S(1)} collective-permute-done((f32[4,16,10,1]{3,1,2,0:T(8,128)S(1)}, f32[4,16,10,1]{3,1,2,0:T(8,128)S(1)}, u32[]{:S(2)}, u32[]{:S(2)}) %collective-permute-start.19) | collective-permute-done | bytes 2592 | tf_op jit(solution)/shard_map/ppermute | solution.py:18
  185.3 2.8 collective-permute-start.20
  188.1 5.2 %collective-permute-start.21 = (f32[4,16,1,64]{3,1,2,0:T(8,128)S(1)}, f32[4,16,1,64]{3,1,2,0:T(8,128)S(1)}, u32[]{:S(2)}, u32[]{:S(2)}) collective-permute-start(f32[4,16,1,64]{3,1,2,0:T(8,128)S(1)} %get-tuple-element.227), channel_id=1, source_target_pairs={{64,0},{128,64},{192,128},{256,192},{320,256},{384,320},{448,384},... | collective-permute-start | bytes 49160 | tf_op jit(solution)/shard_map/ppermute | solution.py:18
  193.3 1.9 convolution_bitcast_fusion.4
  196.3 2.6 collective-permute-start.22
  198.9 1.9 collective-permute-start.23
  203.2 8.0 %collective-permute-done.23 = f32[4,16,10,1]{3,1,2,0:T(8,128)S(1)} collective-permute-done((f32[4,16,10,1]{3,1,2,0:T(8,128)S(1)}, f32[4,16,10,1]{3,1,2,0:T(8,128)S(1)}, u32[]{:S(2)}, u32[]{:S(2)}) %collective-permute-start.23) | collective-permute-done | bytes 2592 | tf_op jit(solution)/shard_map/ppermute | solution.py:18
  211.9 4.1 %broadcast_in_dim.14 = f32[4,16,8,2,64,2]{1,5,4,3,2,0:T(2,128)} broadcast(f32[4,16,8,64]{1,3,2,0:T(8,128)S(1)} %copy.69), dimensions={0,1,2,4} | broadcast | bytes 655360 | tf_op jit(solution)/shard_map/broadcast_in_dim | solution.py:122
  216.0 2.8 copy.70
  218.8 1.7 convolution_bitcast_fusion.5
  221.5 1.9 collective-permute-start.24
  223.4 5.5 %collective-permute-start.25 = (f32[4,4,1,128]{3,1,2,0:T(4,128)S(1)}, f32[4,4,1,128]{3,1,2,0:T(4,128)S(1)}, u32[]{:S(2)}, u32[]{:S(2)}) collective-permute-start(f32[4,4,1,128]{3,1,2,0:T(4,128)S(1)} %get-tuple-element.257), channel_id=1, source_target_pairs={{64,0},{128,64},{192,128},{256,192},{320,256},{384,320},{448,384},... | collective-permute-start | bytes 24584 | tf_op jit(solution)/shard_map/ppermute | solution.py:18
  229.6 3.4 %all-to-all-start.1 = ((f32[8,16,128]{2,1,0:T(8,128)}), f32[8,16,128]{2,1,0:T(8,128)S(1)}, u32[]{:S(2)}, u32[]{:S(2)}) async-start(f32[8,16,128]{2,1,0:T(8,128)} %broadcast_in_dim.16), calls=%async_computation.1 | async-start | bytes 131072 | tf_op jit(solution)/shard_map/all_to_all | solution.py:80
  233.1 2.3 collective-permute-start.26
  235.5 2.0 collective-permute-start.27
  238.9 7.9 %all-to-all-start.2 = ((f32[64,16,128]{2,1,0:T(8,128)}), f32[64,16,128]{2,1,0:T(8,128)S(1)}, u32[]{:S(2)}, u32[]{:S(2)}) async-start(f32[64,16,128]{2,1,0:T(8,128)} %broadcast_in_dim.34), calls=%async_computation.2 | async-start | bytes 1048576 | tf_op jit(solution)/shard_map/all_to_all | solution.py:80
  248.5 3.5 %collective-permute-start.28 = (f32[4,4,1,128]{3,1,2,0:T(4,128)S(1)}, f32[4,4,1,128]{3,1,2,0:T(4,128)S(1)}, u32[]{:S(2)}, u32[]{:S(2)}) collective-permute-start(f32[4,4,1,128]{3,1,2,0:T(4,128)S(1)} %get-tuple-element.252), channel_id=1, source_target_pairs={{0,64},{64,128},{128,192},{192,256},{256,320},{320,384},{384,448},... | collective-permute-start | bytes 24584 | tf_op jit(solution)/shard_map/ppermute | solution.py:15
  252.0 4.1 %collective-permute-start.29 = (f32[4,4,1,128]{3,1,2,0:T(4,128)S(1)}, f32[4,4,1,128]{3,1,2,0:T(4,128)S(1)}, u32[]{:S(2)}, u32[]{:S(2)}) collective-permute-start(f32[4,4,1,128]{3,1,2,0:T(4,128)S(1)} %get-tuple-element.253), channel_id=1, source_target_pairs={{64,0},{128,64},{192,128},{256,192},{320,256},{384,320},{448,384},... | collective-permute-start | bytes 24584 | tf_op jit(solution)/shard_map/ppermute | solution.py:18
  257.0 6.7 %collective-permute-start.30 = (f32[4,4,18,1]{3,1,2,0:T(4,128)S(1)}, f32[4,4,18,1]{3,1,2,0:T(4,128)S(1)}, u32[]{:S(2)}, u32[]{:S(2)}) collective-permute-start(f32[4,4,18,1]{3,1,2,0:T(4,128)S(1)} %get-tuple-element.242), channel_id=1, source_target_pairs={{0,1},{1,2},{2,3},{3,4},{4,5},{5,6},{6,7},{7,8},{8,9},{9,10},{10,1... | collective-permute-start | bytes 3464 | tf_op jit(solution)/shard_map/ppermute | solution.py:15
  263.7 1.9 collective-permute-start.31
  267.2 5.6 %collective-permute-done.31 = f32[4,4,18,1]{3,1,2,0:T(4,128)S(1)} collective-permute-done((f32[4,4,18,1]{3,1,2,0:T(4,128)S(1)}, f32[4,4,18,1]{3,1,2,0:T(4,128)S(1)}, u32[]{:S(2)}, u32[]{:S(2)}) %collective-permute-start.31) | collective-permute-done | bytes 1184 | tf_op jit(solution)/shard_map/ppermute | solution.py:18
  273.8 7.8 %all-to-all-done.2 = f32[64,16,128]{2,1,0:T(8,128)S(1)} async-done(((f32[64,16,128]{2,1,0:T(8,128)}), f32[64,16,128]{2,1,0:T(8,128)S(1)}, u32[]{:S(2)}, u32[]{:S(2)}) %all-to-all-start.2) | async-done | bytes 524320 | tf_op jit(solution)/shard_map/all_to_all | solution.py:80
  (154 shorter events, 35.5 us)
Async XLA Ops:
  0.6 103.3 %copy-start = (f32[3,16,32]{2,1,0:T(8,128)S(1)}, f32[3,16,32]{2,1,0:T(8,128)}, u32[]{:S(2)}) copy-start(f32[3,16,32]{2,1,0:T(8,128)} %param.46) | copy-start | bytes 18436
  0.6 46.4 %copy-start.6 = (f32[3,4,16]{2,1,0:T(4,128)S(1)}, f32[3,4,16]{2,1,0:T(4,128)}, u32[]{:S(2)}) copy-start(f32[3,4,16]{2,1,0:T(4,128)} %param.45) | copy-start | bytes 2308
  1.6 49.9 %copy-start.1 = (f32[1,4,4,16,128]{4,2,0,3,1:T(4,128)}, f32[1,4,4,16,128]{4,2,0,3,1:T(4,128)S(1)}, u32[]{:S(2)}) copy-start(f32[1,4,4,16,128]{4,2,0,3,1:T(4,128)S(1)} %get-tuple-element.266) | copy-start | bytes 393220
  1.6 10.1 %collective-permute-start = (f32[4,4,1,128]{3,1,2,0:T(4,128)S(1)}, f32[4,4,1,128]{3,1,2,0:T(4,128)S(1)}, u32[]{:S(2)}, u32[]{:S(2)}) collective-permute-start(f32[4,4,1,128]{3,1,2,0:T(4,128)S(1)} %get-tuple-element.264), channel_id=1, source_target_pairs={{0,64},{64,128},{128,192},{192,256},{256,320},{320,384},{384,448},... | collective-permute-start | bytes 24584 | tf_op jit(solution)/shard_map/ppermute | solution.py:15
  5.6 6.1 %collective-permute-start.1 = (f32[4,4,1,128]{3,1,2,0:T(4,128)S(1)}, f32[4,4,1,128]{3,1,2,0:T(4,128)S(1)}, u32[]{:S(2)}, u32[]{:S(2)}) collective-permute-start(f32[4,4,1,128]{3,1,2,0:T(4,128)S(1)} %get-tuple-element.265), channel_id=1, source_target_pairs={{64,0},{128,64},{192,128},{256,192},{320,256},{384,320},{448,384},... | collective-permute-start | bytes 24584 | tf_op jit(solution)/shard_map/ppermute | solution.py:18
  11.9 12.1 %collective-permute-start.2 = (f32[4,4,18,1]{3,1,2,0:T(4,128)S(1)}, f32[4,4,18,1]{3,1,2,0:T(4,128)S(1)}, u32[]{:S(2)}, u32[]{:S(2)}) collective-permute-start(f32[4,4,18,1]{3,1,2,0:T(4,128)S(1)} %get-tuple-element.248), channel_id=1, source_target_pairs={{0,1},{1,2},{2,3},{3,4},{4,5},{5,6},{6,7},{7,8},{8,9},{9,10},{10,1... | collective-permute-start | bytes 3464 | tf_op jit(solution)/shard_map/ppermute | solution.py:15
  17.9 8.0 %collective-permute-start.3 = (f32[4,4,18,1]{3,1,2,0:T(4,128)S(1)}, f32[4,4,18,1]{3,1,2,0:T(4,128)S(1)}, u32[]{:S(2)}, u32[]{:S(2)}) collective-permute-start(f32[4,4,18,1]{3,1,2,0:T(4,128)S(1)} %get-tuple-element.249), channel_id=1, source_target_pairs={{1,0},{2,1},{3,2},{4,3},{5,4},{6,5},{7,6},{8,7},{9,8},{10,9},{11,1... | collective-permute-start | bytes 3464 | tf_op jit(solution)/shard_map/ppermute | solution.py:18
  26.2 7.4 %collective-permute-start.4 = (f32[4,4,1,128]{3,1,2,0:T(4,128)S(1)}, f32[4,4,1,128]{3,1,2,0:T(4,128)S(1)}, u32[]{:S(2)}, u32[]{:S(2)}) collective-permute-start(f32[4,4,1,128]{3,1,2,0:T(4,128)S(1)} %get-tuple-element.260), channel_id=1, source_target_pairs={{0,64},{64,128},{128,192},{192,256},{256,320},{320,384},{384,448},... | collective-permute-start | bytes 24584 | tf_op jit(solution)/shard_map/ppermute | solution.py:15
  28.9 5.5 %collective-permute-start.5 = (f32[4,4,1,128]{3,1,2,0:T(4,128)S(1)}, f32[4,4,1,128]{3,1,2,0:T(4,128)S(1)}, u32[]{:S(2)}, u32[]{:S(2)}) collective-permute-start(f32[4,4,1,128]{3,1,2,0:T(4,128)S(1)} %get-tuple-element.261), channel_id=1, source_target_pairs={{64,0},{128,64},{192,128},{256,192},{320,256},{384,320},{448,384},... | collective-permute-start | bytes 24584 | tf_op jit(solution)/shard_map/ppermute | solution.py:18
  34.5 11.4 %collective-permute-start.6 = (f32[4,4,18,1]{3,1,2,0:T(4,128)S(1)}, f32[4,4,18,1]{3,1,2,0:T(4,128)S(1)}, u32[]{:S(2)}, u32[]{:S(2)}) collective-permute-start(f32[4,4,18,1]{3,1,2,0:T(4,128)S(1)} %get-tuple-element.246), channel_id=1, source_target_pairs={{0,1},{1,2},{2,3},{3,4},{4,5},{5,6},{6,7},{7,8},{8,9},{9,10},{10,1... | collective-permute-start | bytes 3464 | tf_op jit(solution)/shard_map/ppermute | solution.py:15
  37.4 8.5 %collective-permute-start.7 = (f32[4,4,18,1]{3,1,2,0:T(4,128)S(1)}, f32[4,4,18,1]{3,1,2,0:T(4,128)S(1)}, u32[]{:S(2)}, u32[]{:S(2)}) collective-permute-start(f32[4,4,18,1]{3,1,2,0:T(4,128)S(1)} %get-tuple-element.247), channel_id=1, source_target_pairs={{1,0},{2,1},{3,2},{4,3},{5,4},{6,5},{7,6},{8,7},{9,8},{10,9},{11,1... | collective-permute-start | bytes 3464 | tf_op jit(solution)/shard_map/ppermute | solution.py:18
  57.4 8.0 %collective-permute-start.8 = (f32[4,16,1,64]{3,1,2,0:T(8,128)S(1)}, f32[4,16,1,64]{3,1,2,0:T(8,128)S(1)}, u32[]{:S(2)}, u32[]{:S(2)}) collective-permute-start(f32[4,16,1,64]{3,1,2,0:T(8,128)S(1)} %get-tuple-element.240), channel_id=1, source_target_pairs={{0,64},{64,128},{128,192},{192,256},{256,320},{320,384},{384,448},... | collective-permute-start | bytes 49160 | tf_op jit(solution)/shard_map/ppermute | solution.py:15
  60.0 6.4 %collective-permute-start.9 = (f32[4,16,1,64]{3,1,2,0:T(8,128)S(1)}, f32[4,16,1,64]{3,1,2,0:T(8,128)S(1)}, u32[]{:S(2)}, u32[]{:S(2)}) collective-permute-start(f32[4,16,1,64]{3,1,2,0:T(8,128)S(1)} %get-tuple-element.241), channel_id=1, source_target_pairs={{64,0},{128,64},{192,128},{256,192},{320,256},{384,320},{448,384},... | collective-permute-start | bytes 49160 | tf_op jit(solution)/shard_map/ppermute | solution.py:18
  66.6 12.6 %collective-permute-start.10 = (f32[4,16,10,1]{3,1,2,0:T(8,128)S(1)}, f32[4,16,10,1]{3,1,2,0:T(8,128)S(1)}, u32[]{:S(2)}, u32[]{:S(2)}) collective-permute-start(f32[4,16,10,1]{3,1,2,0:T(8,128)S(1)} %get-tuple-element.222), channel_id=1, source_target_pairs={{0,1},{1,2},{2,3},{3,4},{4,5},{5,6},{6,7},{7,8},{8,9},{9,10},{10,1... | collective-permute-start | bytes 7688 | tf_op jit(solution)/shard_map/ppermute | solution.py:15
  68.7 10.5 %collective-permute-start.11 = (f32[4,16,10,1]{3,1,2,0:T(8,128)S(1)}, f32[4,16,10,1]{3,1,2,0:T(8,128)S(1)}, u32[]{:S(2)}, u32[]{:S(2)}) collective-permute-start(f32[4,16,10,1]{3,1,2,0:T(8,128)S(1)} %get-tuple-element.223), channel_id=1, source_target_pairs={{1,0},{2,1},{3,2},{4,3},{5,4},{6,5},{7,6},{8,7},{9,8},{10,9},{11,1... | collective-permute-start | bytes 7688 | tf_op jit(solution)/shard_map/ppermute | solution.py:18
  79.6 8.3 %collective-permute-start.12 = (f32[4,16,1,64]{3,1,2,0:T(8,128)S(1)}, f32[4,16,1,64]{3,1,2,0:T(8,128)S(1)}, u32[]{:S(2)}, u32[]{:S(2)}) collective-permute-start(f32[4,16,1,64]{3,1,2,0:T(8,128)S(1)} %get-tuple-element.236), channel_id=1, source_target_pairs={{0,64},{64,128},{128,192},{192,256},{256,320},{320,384},{384,448},... | collective-permute-start | bytes 49160 | tf_op jit(solution)/shard_map/ppermute | solution.py:15
  81.5 75.1 %copy-start.3 = (f32[32,128]{1,0:T(8,128)S(1)}, f32[32,128]{1,0:T(8,128)}, u32[]{:S(2)}) copy-start(f32[32,128]{1,0:T(8,128)} %param.47) | copy-start | bytes 49156
  81.5 75.2 %copy-start.4 = (f32[4,2]{0,1:T(2,128)S(1)}, f32[4,2]{0,1:T(2,128)}, u32[]{:S(2)}) copy-start(f32[4,2]{0,1:T(2,128)} %param.42) | copy-start | bytes 100
  81.5 75.2 %copy-start.5 = (f32[2,128]{1,0:T(2,128)S(1)}, f32[2,128]{1,0:T(2,128)}, u32[]{:S(2)}) copy-start(f32[2,128]{1,0:T(2,128)} %param.48) | copy-start | bytes 3076
  81.5 75.4 %copy-start.7 = (s32[4]{0:T(128)S(1)}, s32[4]{0:T(128)}, u32[]{:S(2)}) copy-start(s32[4]{0:T(128)} %param.43) | copy-start | bytes 52
  81.5 75.4 %copy-start.8 = (f32[128]{0:T(128)S(1)}, f32[128]{0:T(128)}, u32[]{:S(2)}) copy-start(f32[128]{0:T(128)} %param.49) | copy-start | bytes 1540
  81.5 7.3 %collective-permute-start.13 = (f32[4,16,1,64]{3,1,2,0:T(8,128)S(1)}, f32[4,16,1,64]{3,1,2,0:T(8,128)S(1)}, u32[]{:S(2)}, u32[]{:S(2)}) collective-permute-start(f32[4,16,1,64]{3,1,2,0:T(8,128)S(1)} %get-tuple-element.237), channel_id=1, source_target_pairs={{64,0},{128,64},{192,128},{256,192},{320,256},{384,320},{448,384},... | collective-permute-start | bytes 49160 | tf_op jit(solution)/shard_map/ppermute | solution.py:18
  89.0 14.6 %collective-permute-start.14 = (f32[4,16,10,1]{3,1,2,0:T(8,128)S(1)}, f32[4,16,10,1]{3,1,2,0:T(8,128)S(1)}, u32[]{:S(2)}, u32[]{:S(2)}) collective-permute-start(f32[4,16,10,1]{3,1,2,0:T(8,128)S(1)} %get-tuple-element.220), channel_id=1, source_target_pairs={{0,1},{1,2},{2,3},{3,4},{4,5},{5,6},{6,7},{7,8},{8,9},{9,10},{10,1... | collective-permute-start | bytes 7688 | tf_op jit(solution)/shard_map/ppermute | solution.py:15
  91.0 12.6 %collective-permute-start.15 = (f32[4,16,10,1]{3,1,2,0:T(8,128)S(1)}, f32[4,16,10,1]{3,1,2,0:T(8,128)S(1)}, u32[]{:S(2)}, u32[]{:S(2)}) collective-permute-start(f32[4,16,10,1]{3,1,2,0:T(8,128)S(1)} %get-tuple-element.221), channel_id=1, source_target_pairs={{1,0},{2,1},{3,2},{4,3},{5,4},{6,5},{7,6},{8,7},{9,8},{10,9},{11,1... | collective-permute-start | bytes 7688 | tf_op jit(solution)/shard_map/ppermute | solution.py:18
  105.0 52.8 %copy-start.10 = (f32[4,32,8,64]{3,1,2,0:T(8,128)}, f32[4,32,8,64]{3,1,2,0:T(8,128)S(1)}, u32[]{:S(2)}) copy-start(f32[4,32,8,64]{3,1,2,0:T(8,128)S(1)} %get-tuple-element.273) | copy-start | bytes 786436
  158.7 7.4 %collective-permute-start.16 = (f32[4,16,1,64]{3,1,2,0:T(8,128)S(1)}, f32[4,16,1,64]{3,1,2,0:T(8,128)S(1)}, u32[]{:S(2)}, u32[]{:S(2)}) collective-permute-start(f32[4,16,1,64]{3,1,2,0:T(8,128)S(1)} %get-tuple-element.230), channel_id=1, source_target_pairs={{0,64},{64,128},{128,192},{192,256},{256,320},{320,384},{384,448},... | collective-permute-start | bytes 49160 | tf_op jit(solution)/shard_map/ppermute | solution.py:15
  160.7 6.5 %collective-permute-start.17 = (f32[4,16,1,64]{3,1,2,0:T(8,128)S(1)}, f32[4,16,1,64]{3,1,2,0:T(8,128)S(1)}, u32[]{:S(2)}, u32[]{:S(2)}) collective-permute-start(f32[4,16,1,64]{3,1,2,0:T(8,128)S(1)} %get-tuple-element.231), channel_id=1, source_target_pairs={{64,0},{128,64},{192,128},{256,192},{320,256},{384,320},{448,384},... | collective-permute-start | bytes 49160 | tf_op jit(solution)/shard_map/ppermute | solution.py:18
  168.1 9.6 %collective-permute-start.18 = (f32[4,16,10,1]{3,1,2,0:T(8,128)}, f32[4,16,10,1]{3,1,2,0:T(8,128)S(1)}, u32[]{:S(2)}, u32[]{:S(2)}) collective-permute-start(f32[4,16,10,1]{3,1,2,0:T(8,128)} %get-tuple-element.218), channel_id=1, source_target_pairs={{0,1},{1,2},{2,3},{3,4},{4,5},{5,6},{6,7},{7,8},{8,9},{9,10},{10,1... | collective-permute-start | bytes 7688 | tf_op jit(solution)/shard_map/ppermute | solution.py:15
  173.3 11.7 %collective-permute-start.19 = (f32[4,16,10,1]{3,1,2,0:T(8,128)S(1)}, f32[4,16,10,1]{3,1,2,0:T(8,128)S(1)}, u32[]{:S(2)}, u32[]{:S(2)}) collective-permute-start(f32[4,16,10,1]{3,1,2,0:T(8,128)S(1)} %get-tuple-element.219), channel_id=1, source_target_pairs={{1,0},{2,1},{3,2},{4,3},{5,4},{6,5},{7,6},{8,7},{9,8},{10,9},{11,1... | collective-permute-start | bytes 7688 | tf_op jit(solution)/shard_map/ppermute | solution.py:18
  185.3 10.0 %collective-permute-start.20 = (f32[4,16,1,64]{3,1,2,0:T(8,128)S(1)}, f32[4,16,1,64]{3,1,2,0:T(8,128)S(1)}, u32[]{:S(2)}, u32[]{:S(2)}) collective-permute-start(f32[4,16,1,64]{3,1,2,0:T(8,128)S(1)} %get-tuple-element.226), channel_id=1, source_target_pairs={{0,64},{64,128},{128,192},{192,256},{256,320},{320,384},{384,448},... | collective-permute-start | bytes 49160 | tf_op jit(solution)/shard_map/ppermute | solution.py:15
  188.1 7.3 %collective-permute-start.21 = (f32[4,16,1,64]{3,1,2,0:T(8,128)S(1)}, f32[4,16,1,64]{3,1,2,0:T(8,128)S(1)}, u32[]{:S(2)}, u32[]{:S(2)}) collective-permute-start(f32[4,16,1,64]{3,1,2,0:T(8,128)S(1)} %get-tuple-element.227), channel_id=1, source_target_pairs={{64,0},{128,64},{192,128},{256,192},{320,256},{384,320},{448,384},... | collective-permute-start | bytes 49160 | tf_op jit(solution)/shard_map/ppermute | solution.py:18
  196.3 6.9 %collective-permute-start.22 = (f32[4,16,10,1]{3,1,2,0:T(8,128)}, f32[4,16,10,1]{3,1,2,0:T(8,128)S(1)}, u32[]{:S(2)}, u32[]{:S(2)}) collective-permute-start(f32[4,16,10,1]{3,1,2,0:T(8,128)} %get-tuple-element.216), channel_id=1, source_target_pairs={{0,1},{1,2},{2,3},{3,4},{4,5},{5,6},{6,7},{7,8},{8,9},{9,10},{10,1... | collective-permute-start | bytes 7688 | tf_op jit(solution)/shard_map/ppermute | solution.py:15
  198.9 12.3 %collective-permute-start.23 = (f32[4,16,10,1]{3,1,2,0:T(8,128)S(1)}, f32[4,16,10,1]{3,1,2,0:T(8,128)S(1)}, u32[]{:S(2)}, u32[]{:S(2)}) collective-permute-start(f32[4,16,10,1]{3,1,2,0:T(8,128)S(1)} %get-tuple-element.217), channel_id=1, source_target_pairs={{1,0},{2,1},{3,2},{4,3},{5,4},{6,5},{7,6},{8,7},{9,8},{10,9},{11,1... | collective-permute-start | bytes 7688 | tf_op jit(solution)/shard_map/ppermute | solution.py:18
  211.9 6.9 %copy-start.2 = (f32[1,4,4,16,128]{4,2,0,3,1:T(4,128)S(1)}, f32[1,4,4,16,128]{4,2,0,3,1:T(4,128)}, u32[]{:S(2)}) copy-start(f32[1,4,4,16,128]{4,2,0,3,1:T(4,128)} %copy-done.1) | copy-start | bytes 393220
  211.9 6.9 %copy-start.9 = (f32[4,16,16,128]{3,1,2,0:T(8,128)S(1)}, f32[4,16,16,128]{3,1,2,0:T(8,128)}, u32[]{:S(2)}) copy-start(f32[4,16,16,128]{3,1,2,0:T(8,128)} %get-tuple-element.271) | copy-start | bytes 1572868
  221.5 11.5 %collective-permute-start.24 = (f32[4,4,1,128]{3,1,2,0:T(4,128)S(1)}, f32[4,4,1,128]{3,1,2,0:T(4,128)S(1)}, u32[]{:S(2)}, u32[]{:S(2)}) collective-permute-start(f32[4,4,1,128]{3,1,2,0:T(4,128)S(1)} %get-tuple-element.256), channel_id=1, source_target_pairs={{0,64},{64,128},{128,192},{192,256},{256,320},{320,384},{384,448},... | collective-permute-start | bytes 24584 | tf_op jit(solution)/shard_map/ppermute | solution.py:15
  223.4 9.6 %collective-permute-start.25 = (f32[4,4,1,128]{3,1,2,0:T(4,128)S(1)}, f32[4,4,1,128]{3,1,2,0:T(4,128)S(1)}, u32[]{:S(2)}, u32[]{:S(2)}) collective-permute-start(f32[4,4,1,128]{3,1,2,0:T(4,128)S(1)} %get-tuple-element.257), channel_id=1, source_target_pairs={{64,0},{128,64},{192,128},{256,192},{320,256},{384,320},{448,384},... | collective-permute-start | bytes 24584 | tf_op jit(solution)/shard_map/ppermute | solution.py:18
  229.6 8.5 %all-to-all-start.1 = ((f32[8,16,128]{2,1,0:T(8,128)}), f32[8,16,128]{2,1,0:T(8,128)S(1)}, u32[]{:S(2)}, u32[]{:S(2)}) async-start(f32[8,16,128]{2,1,0:T(8,128)} %broadcast_in_dim.16), calls=%async_computation.1 | async-start | bytes 131072 | tf_op jit(solution)/shard_map/all_to_all | solution.py:80
  233.1 15.0 %collective-permute-start.26 = (f32[4,4,18,1]{3,1,2,0:T(4,128)S(1)}, f32[4,4,18,1]{3,1,2,0:T(4,128)S(1)}, u32[]{:S(2)}, u32[]{:S(2)}) collective-permute-start(f32[4,4,18,1]{3,1,2,0:T(4,128)S(1)} %get-tuple-element.244), channel_id=1, source_target_pairs={{0,1},{1,2},{2,3},{3,4},{4,5},{5,6},{6,7},{7,8},{8,9},{9,10},{10,1... | collective-permute-start | bytes 3464 | tf_op jit(solution)/shard_map/ppermute | solution.py:15
  235.5 12.7 %collective-permute-start.27 = (f32[4,4,18,1]{3,1,2,0:T(4,128)S(1)}, f32[4,4,18,1]{3,1,2,0:T(4,128)S(1)}, u32[]{:S(2)}, u32[]{:S(2)}) collective-permute-start(f32[4,4,18,1]{3,1,2,0:T(4,128)S(1)} %get-tuple-element.245), channel_id=1, source_target_pairs={{1,0},{2,1},{3,2},{4,3},{5,4},{6,5},{7,6},{8,7},{9,8},{10,9},{11,1... | collective-permute-start | bytes 3464 | tf_op jit(solution)/shard_map/ppermute | solution.py:18
  238.9 42.6 %all-to-all-start.2 = ((f32[64,16,128]{2,1,0:T(8,128)}), f32[64,16,128]{2,1,0:T(8,128)S(1)}, u32[]{:S(2)}, u32[]{:S(2)}) async-start(f32[64,16,128]{2,1,0:T(8,128)} %broadcast_in_dim.34), calls=%async_computation.2 | async-start | bytes 1048576 | tf_op jit(solution)/shard_map/all_to_all | solution.py:80
  248.5 7.6 %collective-permute-start.28 = (f32[4,4,1,128]{3,1,2,0:T(4,128)S(1)}, f32[4,4,1,128]{3,1,2,0:T(4,128)S(1)}, u32[]{:S(2)}, u32[]{:S(2)}) collective-permute-start(f32[4,4,1,128]{3,1,2,0:T(4,128)S(1)} %get-tuple-element.252), channel_id=1, source_target_pairs={{0,64},{64,128},{128,192},{192,256},{256,320},{320,384},{384,448},... | collective-permute-start | bytes 24584 | tf_op jit(solution)/shard_map/ppermute | solution.py:15
  252.0 4.8 %collective-permute-start.29 = (f32[4,4,1,128]{3,1,2,0:T(4,128)S(1)}, f32[4,4,1,128]{3,1,2,0:T(4,128)S(1)}, u32[]{:S(2)}, u32[]{:S(2)}) collective-permute-start(f32[4,4,1,128]{3,1,2,0:T(4,128)S(1)} %get-tuple-element.253), channel_id=1, source_target_pairs={{64,0},{128,64},{192,128},{256,192},{320,256},{384,320},{448,384},... | collective-permute-start | bytes 24584 | tf_op jit(solution)/shard_map/ppermute | solution.py:18
  257.0 10.2 %collective-permute-start.30 = (f32[4,4,18,1]{3,1,2,0:T(4,128)S(1)}, f32[4,4,18,1]{3,1,2,0:T(4,128)S(1)}, u32[]{:S(2)}, u32[]{:S(2)}) collective-permute-start(f32[4,4,18,1]{3,1,2,0:T(4,128)S(1)} %get-tuple-element.242), channel_id=1, source_target_pairs={{0,1},{1,2},{2,3},{3,4},{4,5},{5,6},{6,7},{7,8},{8,9},{9,10},{10,1... | collective-permute-start | bytes 3464 | tf_op jit(solution)/shard_map/ppermute | solution.py:15
  263.7 9.1 %collective-permute-start.31 = (f32[4,4,18,1]{3,1,2,0:T(4,128)S(1)}, f32[4,4,18,1]{3,1,2,0:T(4,128)S(1)}, u32[]{:S(2)}, u32[]{:S(2)}) collective-permute-start(f32[4,4,18,1]{3,1,2,0:T(4,128)S(1)} %get-tuple-element.243), channel_id=1, source_target_pairs={{1,0},{2,1},{3,2},{4,3},{5,4},{6,5},{7,6},{8,7},{9,8},{10,9},{11,1... | collective-permute-start | bytes 3464 | tf_op jit(solution)/shard_map/ppermute | solution.py:18

commit v2 on v0

v2 whole, which is shorter than its diff:
```python
import jax
import jax.numpy as jnp
from jax import lax
from jax.experimental import pallas as pl
from jax.experimental.pallas import tpu as pltpu
from jax.sharding import PartitionSpec as P

exact = lax.Precision.HIGHEST
MAPS, BINS, CH0, CH1, ORDER = 4, 4, 16, 32, 3
ROWS, COLS = 16, 128
CROWS, CCOLS = ROWS // 2, COLS // 2
CI = MAPS * BINS
CA = MAPS * CH0
CB = MAPS * CH1
STRIP = 4
SLOT = 2 * STRIP
PER = 128 // SLOT
UP0 = 12
UP1 = 5
UP2 = 3
PAIRS = [(0, 4), (1, 5), (2, 6), (3, 7), (-3, 8), (-2, 9), (-1, 10)]
WHERE = {row: (q, half) for q, pair in enumerate(PAIRS) for half, row in enumerate(pair)}
bf16, f32 = jnp.bfloat16, jnp.float32


def lanes(count):
    return lax.broadcasted_iota(jnp.int32, (count, 128), 1)


def pick(value, index):
    return jnp.take_along_axis(value, index, axis=1, mode="promise_in_bounds")


def roll(value, shift):
    shift %= 128
    return value if shift == 0 else pltpu.roll(value, shift, 1)


def halves(value):
    high = value.astype(bf16)
    return high, (value - high.astype(f32)).astype(bf16)


def weight_halves(ref, start):
    high, low = halves(ref[...])
    column = lax.broadcasted_iota(jnp.int32, ref.shape, 1)
    return jnp.where(column < start, high.astype(f32), low.astype(f32)).astype(bf16)


def dot(a, b):
    return jnp.dot(a, b, preferred_element_type=f32)


def dot_nt(a, b):
    return lax.dot_general(a, b, (((1,), (1,)), ((), ())), preferred_element_type=f32)


def fine_turns(flags, count):
    lane = lanes(count)
    turns = []
    for side in range(2):
        left, own, right = (flags[3 * side + n] for n in range(3))
        block = jnp.where(own == 1, 127 - lane, lane)
        strip = jnp.where(
            lane < 64,
            jnp.where((lane < SLOT) & (right == 1), SLOT - 1 - lane, lane),
            jnp.where((lane >= 128 - SLOT) & (left == 1), 255 - SLOT - lane, lane),
        )
        turns.append((block, strip))
    return turns


def coarse_turns(flags, count):
    lane = lanes(count)
    turns = []
    for side in range(2):
        left, own, right = (flags[3 * side + n] for n in range(3))
        index = jnp.where((lane < 64) & (own == 1), 63 - lane, lane)
        index = jnp.where((lane >= 64) & (lane < 64 + SLOT) & (right == 1), 127 + SLOT - lane, index)
        index = jnp.where((lane >= 128 - SLOT) & (left == 1), 255 - SLOT - lane, index)
        turns.append(index)
    return turns


def vertical(rows, row, height, top, bottom):
    if row == 0:
        upper = pick(rows[-1], top)
    elif row == height:
        upper = pick(rows[height - 1], bottom)
    else:
        upper = rows[row - 1]
    if row == -1:
        lower = pick(rows[0], top)
    elif row == height - 1:
        lower = pick(rows[height], bottom)
    else:
        lower = rows[row + 1]
    return upper + lower


def fine_lap(block, strip, row, turns, with_strip):
    (top, top_strip), (bottom, bottom_strip) = turns
    lane = lanes(block[row].shape[0])
    first, last = lane == 0, lane == 127
    b_right, s_right = roll(block[row], 1), roll(strip[row], 1)
    b_left, s_left = roll(block[row], -1), roll(strip[row], -1)
    side = jnp.where(first, s_right, b_right) + jnp.where(last, s_left, b_left)
    out = -0.25 * (vertical(block, row, ROWS, top, bottom) + side)
    if not with_strip:
        return out
    side = jnp.where(first, b_right, s_right) + jnp.where(last, b_left, s_left)
    return out, -0.25 * (vertical(strip, row, ROWS, top_strip, bottom_strip) + side)


def coarse_lap(rows, row, turns):
    value = rows[row]
    side = roll(value, 1) + roll(value, -1)
    return -0.25 * (vertical(rows, row, CROWS, turns[0], turns[1]) + side)


def end_index(count, stride=1, width=COLS):
    j = lanes(count) % SLOT
    return jnp.where(j < STRIP, j, width - SLOT + j) * stride


def fine_strip(left, right, place):
    group, slot = place // PER, place % PER
    lane = lanes(left.shape[1])
    return jnp.where(
        lane < 64, roll(right[group], -SLOT * slot), roll(left[group], 128 - SLOT - SLOT * slot)
    )


def coarse_row(block, left, right, slot):
    lane = lanes(block.shape[0])
    strip = jnp.where(
        lane < 96, roll(right, 64 - SLOT * slot), roll(left, 128 - SLOT - SLOT * slot)
    )
    return jnp.where(lane < 64, block, strip)


def groups(count):
    return -(-count // PER)


def put_slots(out_ref, filled, count):
    lane = lanes(filled[0].shape[0])
    for group in range(groups(count)):
        value = filled[group * PER]
        for n in range(group * PER + 1, min(count, group * PER + PER)):
            value = jnp.where(lane // SLOT == n % PER, filled[n], value)
        out_ref[group] = value


def fine_rows(up_ref, own_ref, down_ref):
    rows = {}
    for row in range(-UP0, ROWS + UP0):
        if row < 0:
            rows[row] = up_ref[ROWS + row]
        elif row < ROWS:
            rows[row] = own_ref[row]
        else:
            rows[row] = down_ref[row - ROWS]
    return rows


def ends_kernel(up_ref, own_ref, down_ref, out_ref):
    index = end_index(CI)
    rows = fine_rows(up_ref, own_ref, down_ref)
    put_slots(out_ref, [pick(rows[row], index) for row in sorted(rows)], len(rows))


def fine_kernel(
    flags, up_ref, own_ref, down_ref, left_ref, right_ref, w_ref,
    x1_ref, sig_ref, terms_ref, ends_ref, t_ref,
):
    turns = fine_turns(flags, CI)
    block = fine_rows(up_ref, own_ref, down_ref)
    strip = {row: fine_strip(left_ref, right_ref, row + UP0) for row in block}
    first, first_strip = {}, {}
    for row in range(1 - UP0, ROWS + UP0 - 1):
        first[row], first_strip[row] = fine_lap(block, strip, row, turns, True)
    low, high = -2 * UP1, ROWS + 2 * UP1
    for row in range(low, high):
        second = 2.0 * fine_lap(first, first_strip, row, turns, False) - block[row]
        here = pl.ds((row - low) * 128, 128)
        one, one_low = halves(first[row])
        two, two_low = halves(second)
        for n, part in enumerate((block[row].astype(bf16), one, two, one_low, two_low)):
            t_ref[CI * n : CI * (n + 1), here] = part
        for n, part in enumerate((block[row].astype(bf16), one, two)):
            t_ref[CI * (5 + n) : CI * (6 + n), here] = part
    own = pl.ds(-low * 128, ROWS * 128)
    terms_ref[...] = t_ref[0 : 5 * CI, own]
    weights = weight_halves(w_ref, 5 * CI)
    lane = lanes(CA)
    even = 2 * (lane % 64)
    ends = end_index(CA, 2, CCOLS)
    filled = []
    for crow in range(-UP1, CROWS + UP1):
        place = crow + UP1
        pre = dot(weights, t_ref[:, place * 256 : place * 256 + 256])
        decay = jnp.exp(-jnp.abs(pre))
        act = jnp.maximum(pre, 0.0) + jnp.log(1.0 + decay)
        if -1 <= crow <= CROWS:
            inverse = 1.0 / (1.0 + decay)
            sig = jnp.where(pre >= 0, inverse, decay * inverse)
            sig_ref[2 * (crow + 1)] = sig[:, :128]
            sig_ref[2 * (crow + 1) + 1] = sig[:, 128:]
        both = act[:, :128] + act[:, 128:]
        both = 0.25 * (both + roll(both, -1))
        x1_ref[place] = pick(both, even)
        filled.append(pick(both, ends))
    put_slots(ends_ref, filled, len(filled))


def coarse_kernel(
    flags, x1_ref, left_ref, right_ref, w_ref, feat_ref, sig_ref, ends_ref, gram_ref, t_ref, s_ref
):
    turns = coarse_turns(flags, CA)
    lane = lanes(CA)
    rows = {}
    for row in range(-UP1, CROWS + UP1):
        place = row + UP1
        rows[row] = coarse_row(
            x1_ref[place], left_ref[place // PER], right_ref[place // PER], place % PER
        )
    first = {row: coarse_lap(rows, row, turns) for row in range(1 - UP1, CROWS + UP1 - 1)}
    second = {
        row: 2.0 * coarse_lap(first, row, turns) - rows[row]
        for row in range(-UP2, CROWS + UP2)
    }
    for q, (a, b) in enumerate(PAIRS):
        here = pl.ds(q * 128, 128)
        for k, term in enumerate((rows, first, second)):
            packed = jnp.where(lane < 64, term[a], roll(term[b], 64))
            high, low = halves(packed)
            for m in range(MAPS):
                chans = slice(CH0 * m, CH0 * (m + 1))
                t_ref[m, CH0 * k : CH0 * (k + 1), here] = high[chans]
                t_ref[m, CH0 * (3 + k) : CH0 * (4 + k), here] = low[chans]
                t_ref[m, CH0 * (6 + k) : CH0 * (7 + k), here] = high[chans]
    weights = weight_halves(w_ref, 2 * ORDER * CH0)
    own = 4 * 128
    j = lanes(CH1) % SLOT
    column = jnp.where(j < STRIP, j, CCOLS - SLOT + j)
    index = jnp.where(lanes(CH1) // SLOT % 2 == 0, column, 64 + column)
    sums = []
    for m in range(MAPS):
        pre = dot(weights, t_ref[m])
        decay = jnp.exp(-jnp.abs(pre))
        inverse = 1.0 / (1.0 + decay)
        sig = jnp.where(pre >= 0, inverse, decay * inverse)
        act = jnp.maximum(pre[:, :own], 0.0) + jnp.log(1.0 + decay[:, :own])
        sums.append(sum(act[:, 128 * q : 128 * (q + 1)] for q in range(4)))
        high, low = halves(sig[:, :own])
        s_ref[CH1 * m : CH1 * (m + 1)] = high
        s_ref[CB + CH1 * m : CB + CH1 * (m + 1)] = low
        chans = slice(CH1 * m, CH1 * (m + 1))
        ends = jnp.zeros((CH1, 128), f32)
        for q in range(len(PAIRS)):
            value = sig[:, 128 * q : 128 * (q + 1)]
            sig_ref[q, chans] = value
            ends = jnp.where(lanes(CH1) // (2 * SLOT) == q, pick(value, index), ends)
        ends_ref[chans] = ends
    total = jnp.sum(jnp.concatenate(sums, axis=0).T, axis=0, keepdims=True)
    feat_ref[...] = jnp.broadcast_to(total, feat_ref.shape)
    grams = [jnp.zeros((CH0, 128), f32) for _ in range(ORDER)]
    for m in range(MAPS):
        both = dot_nt(t_ref[m, : 2 * ORDER * CH0, :own], s_ref[...])
        for k in range(ORDER):
            high = both[CH0 * k : CH0 * (k + 1)]
            low = both[CH0 * (3 + k) : CH0 * (4 + k)]
            value = high[:, :CB] + high[:, CB:] + low[:, :CB]
            grams[k] = jnp.where(lanes(CH0) // CH1 == m, value, grams[k])
    for k in range(ORDER):
        gram_ref[k] = grams[k]


def back_kernel(
    flags, feat_ref, shift_ref, labels_ref, fw_ref, out_ref, w1_ref, w0_ref,
    sig1_ref, left_ref, right_ref, gram_ref, sig0_ref, terms_ref,
    logits_ref, grads_ref, g_ref, ends_ref, s_ref, d_ref,
    *, pooled,
):
    features = jnp.sum(feat_ref[...], axis=0, keepdims=True) * (1.0 / pooled)
    row8 = lax.broadcasted_iota(jnp.int32, (8, 128), 0)
    spread = jnp.where(lanes(8) // CH1 == row8, jnp.broadcast_to(features, (8, 128)), 0.0)
    fw = fw_ref[...]
    hidden = jnp.tanh(
        jnp.dot(spread, fw, precision=exact, preferred_element_type=f32) + shift_ref[...]
    )
    logits = jnp.sum(hidden * out_ref[...], axis=1, keepdims=True)
    logits_ref[...] = jnp.broadcast_to(logits, (8, 128))
    decay = jnp.exp(-jnp.abs(logits))
    dlogit = jnp.where(logits >= 0, 1.0, decay) / (1.0 + decay) - labels_ref[...]
    dhidden = dlogit * out_ref[...] * (1.0 - hidden * hidden)
    dhidden = jnp.concatenate(
        [jnp.broadcast_to(dhidden[m : m + 1], (CH1, 128)) for m in range(MAPS)], axis=0
    )
    dcol = jnp.sum(fw * dhidden, axis=1, keepdims=True) * (1.0 / pooled)
    dfull = jnp.broadcast_to(dcol, (CB, 128))
    drow = jnp.broadcast_to(dfull.T[:1], (CH0, 128))
    coarse = []
    for k in range(ORDER):
        value = gram_ref[k] * drow
        value = value + roll(value, 64)
        coarse.append(value + roll(value, 32))
    slabs = len(PAIRS) + 2
    for q in range(slabs):
        value = sig1_ref[q] if q < len(PAIRS) else (left_ref, right_ref)[q - len(PAIRS)][...]
        high, low = halves(value * dfull)
        here = pl.ds(q * 128, 128)
        for m in range(MAPS):
            chans = slice(CH1 * m, CH1 * (m + 1))
            s_ref[m, :CH1, here] = high[chans]
            s_ref[m, CH1 : 2 * CH1, here] = low[chans]
            s_ref[m, 2 * CH1 :, here] = high[chans]
    weights = weight_halves(w1_ref, 2 * CH1)
    parts = [dot(weights, s_ref[m]) for m in range(MAPS)]

    def slab(k, q):
        return jnp.concatenate(
            [part[CH0 * k : CH0 * (k + 1), 128 * q : 128 * (q + 1)] for part in parts], axis=0
        )

    def spread_rows(k, low, high, strips):
        left, right = (slab(k, slabs - 2), slab(k, slabs - 1)) if strips else (None, None)
        packed = [slab(k, q) for q in range(len(PAIRS))]
        rows = {}
        for row in range(low, high):
            q, half = WHERE[row]
            value = roll(packed[q], 64 * half)
            rows[row] = coarse_row(value, left, right, 2 * q + half) if strips else value
        return rows

    turns = coarse_turns(flags, CA)
    g0 = spread_rows(0, -1, CROWS + 1, False)
    g1 = spread_rows(1, 1 - UP2, CROWS + UP2 - 1, True)
    g2 = spread_rows(2, -UP2, CROWS + UP2, True)
    inner = {row: g1[row] + 2.0 * coarse_lap(g2, row, turns) for row in g1}
    doubled = lanes(CA) // 2
    for crow in range(-1, CROWS + 1):
        dx1 = g0[crow] - g2[crow] + coarse_lap(inner, crow, turns)
        dx1 = 0.25 * pick(dx1, doubled)
        for n in (2 * (crow + 1), 2 * (crow + 1) + 1):
            high, low = halves(dx1 * sig0_ref[n])
            here = pl.ds(n * 128, 128)
            d_ref[:CA, here] = high
            d_ref[CA : 2 * CA, here] = low
            d_ref[2 * CA :, here] = high
    both = dot_nt(terms_ref[...], d_ref[: 2 * CA, 2 * 128 : (2 + ROWS) * 128])
    lane = lanes(CI)
    row16 = lax.broadcasted_iota(jnp.int32, (CI, 128), 0)
    same = lane % CA // CH0 == row16 // BINS
    fine = []
    for k in range(ORDER):
        value = jnp.where(same, both[CI * k : CI * (k + 1)], 0.0)
        if k:
            low = both[CI * (2 + k) : CI * (3 + k)]
            value = value + jnp.where(same & (lane < CA), low, 0.0)
        for shift in (64, 32, 16):
            value = value + roll(value, shift)
        for shift in (8, 4):
            value = value + pltpu.roll(value, shift, 0)
        fine.append(value)
    value = jnp.where(row16 // BINS == 0, fine[0], jnp.where(row16 // BINS == 1, fine[1], fine[2]))
    for k in range(ORDER):
        value = jnp.where(lane // CH1 == k, coarse[k], value)
    for n in range(grads_ref.shape[0] // CI):
        grads_ref[CI * n : CI * (n + 1)] = value
    weights = weight_halves(w0_ref, 2 * CA)
    index = end_index(2 * CI)
    filled = []
    for n in range(0, ROWS + 4, 2):
        value = dot(weights, d_ref[:, n * 128 : (n + 2) * 128])
        for step in range(2):
            part = value[:, 128 * step : 128 * (step + 1)]
            g_ref[n + step] = part
            filled.append(pick(part[CI:], index))
    put_slots(ends_ref, filled, len(filled))


def saliency_kernel(flags, g_ref, left_ref, right_ref, out_ref, *, pixels):
    turns = fine_turns(flags, CI)
    g0, g1, g2, s1, s2 = {}, {}, {}, {}, {}
    for row in range(-2, ROWS + 2):
        value = g_ref[row + 2]
        g0[row], g1[row], g2[row] = (value[CI * k : CI * (k + 1)] for k in range(3))
        strip = fine_strip(left_ref, right_ref, row + 2)
        s1[row], s2[row] = strip[:CI], strip[CI:]
    inner, inner_strip = {}, {}
    for row in range(-1, ROWS + 1):
        value, strip = fine_lap(g2, s2, row, turns, True)
        inner[row] = g1[row] + 2.0 * value
        inner_strip[row] = s1[row] + 2.0 * strip
    for row in range(ROWS):
        outer = fine_lap(inner, inner_strip, row, turns, False)
        out_ref[pl.ds(row, CI, stride=ROWS), :] = (g0[row] - g2[row] + outer) * pixels


def again_kernel(in_ref, out_ref):
    value = in_ref[0:CI]
    for n in range(1, in_ref.shape[0] // CI):
        value = value + in_ref[CI * n : CI * (n + 1)]
    for n in range(out_ref.shape[0] // CI):
        out_ref[CI * n : CI * (n + 1)] = value


def last_kernel(in_ref, fine_ref, coarse_ref, tmp_ref):
    value = in_ref[0:CI]
    for n in range(1, in_ref.shape[0] // CI):
        value = value + in_ref[CI * n : CI * (n + 1)]
    for k in range(ORDER):
        coarse_ref[k] = roll(value, -CH1 * k)[:, :CH1]
    tmp_ref[...] = roll(value, -ORDER * CH1)
    for k in range(ORDER):
        fine_ref[k] = tmp_ref[BINS * k : BINS * (k + 1), :CH0]


def call(kernel, outs, *args, smem=0, scratch=()):
    in_specs = [
        pl.BlockSpec(memory_space=pltpu.SMEM if n < smem else pltpu.VMEM) for n in range(len(args))
    ]
    return pl.pallas_call(
        kernel,
        out_shape=outs,
        in_specs=in_specs,
        out_specs=jax.tree.map(lambda _: pl.BlockSpec(memory_space=pltpu.VMEM), outs),
        scratch_shapes=list(scratch),
        compiler_params=pltpu.CompilerParams(vmem_limit_bytes=32 * 2**20),
    )(*args)


def shape(*dims, dtype=f32):
    return jax.ShapeDtypeStruct(dims, dtype)


def both_ways(value, axis):
    count = lax.axis_size(axis)
    forward = [(n, (n + 1) % count) for n in range(count)]
    backward = [(target, source) for source, target in forward]
    return lax.ppermute(value, axis, forward), lax.ppermute(value, axis, backward)


def share(rows, axes):
    return lax.all_to_all(rows, axes, 0, 0, tiled=True)


def on_device(
    maps, params, labels, edge_flip,
    fine_weight, coarse_weight, feature_weight, param_weight, out_weight,
):
    faces, tiles = lax.axis_size("face"), lax.axis_size("tile")
    devices = faces * tiles
    f, t = lax.axis_index("face"), lax.axis_index("tile")
    columns = jnp.stack([(t + tiles - 1) % tiles, t, (t + 1) % tiles])
    flags = jnp.concatenate([edge_flip[f][columns], edge_flip[(f + 1) % faces][columns]])
    eye = jnp.eye(MAPS, dtype=f32)
    fine = jnp.einsum("kio,mn->monki", fine_weight, eye)
    fine = fine.transpose(0, 1, 3, 2, 4).reshape(CA, ORDER * CI)
    fine_forward = jnp.concatenate([fine, fine[:, CI:], fine], axis=1)
    fine_backward = jnp.concatenate([fine.T] * 3, axis=1)
    coarse = coarse_weight.reshape(ORDER * CH0, CH1)
    coarse_forward = jnp.concatenate([coarse.T] * 3, axis=1)
    coarse_backward = jnp.concatenate([coarse] * 3, axis=1)
    features4 = jnp.concatenate([feature_weight] * MAPS, axis=0)
    pad = [(0, 8 - MAPS), (0, 0)]
    shift = jnp.dot(jnp.pad(params, pad), param_weight, precision=exact)
    labels8 = jnp.broadcast_to(jnp.pad(labels.astype(f32)[:, None], pad), (8, 128))

    own = maps.reshape(CI, ROWS, COLS).transpose(1, 0, 2).astype(f32)
    up, down = both_ways(own, "face")
    ends0 = call(ends_kernel, shape(groups(ROWS + 2 * UP0), CI, 128), up, own, down)
    left0, right0 = both_ways(ends0, "tile")
    crows = CROWS + 2 * UP1
    x1, sig0, terms0, ends1 = call(
        fine_kernel,
        (
            shape(crows, CA, 128),
            shape(ROWS + 4, CA, 128),
            shape(5 * CI, ROWS * 128, dtype=bf16),
            shape(groups(crows), CA, 128),
        ),
        flags, up, own, down, left0, right0, fine_forward,
        smem=1,
        scratch=[pltpu.VMEM((8 * CI, 2 * crows * 128), bf16)],
    )
    left1, right1 = both_ways(ends1, "tile")
    feats, sig1, ends2, grams = call(
        coarse_kernel,
        (
            shape(devices, CB),
            shape(len(PAIRS), CB, 128),
            shape(CB, 128),
            shape(ORDER, CH0, 128),
        ),
        flags, x1, left1, right1, coarse_forward,
        smem=1,
        scratch=[
            pltpu.VMEM((MAPS, 3 * ORDER * CH0, len(PAIRS) * 128), bf16),
            pltpu.VMEM((2 * CB, 4 * 128), bf16),
        ],
    )
    left2, right2 = both_ways(ends2, "tile")
    feats = share(feats, ("face", "tile"))
    pooled = CROWS * faces * CCOLS * tiles
    logits, grads, g, ends3 = call(
        lambda *refs: back_kernel(*refs, pooled=pooled),
        (
            shape(8, 128),
            shape(faces * CI, 128),
            shape(ROWS + 4, ORDER * CI, 128),
            shape(groups(ROWS + 4), 2 * CI, 128),
        ),
        flags, feats, shift, labels8, features4, out_weight[None],
        coarse_backward, fine_backward, sig1, left2, right2, grams, sig0, terms0,
        smem=1,
        scratch=[
            pltpu.VMEM((MAPS, 3 * CH1, (len(PAIRS) + 2) * 128), bf16),
            pltpu.VMEM((3 * CA, (ROWS + 4) * 128), bf16),
        ],
    )
    left3, right3 = both_ways(ends3, "tile")
    grads = share(grads, "face")
    grads = call(again_kernel, shape(tiles * CI, 128), grads)
    grads = share(grads, "tile")
    pixels = float(ROWS * faces * COLS * tiles)
    saliency = call(
        lambda *refs: saliency_kernel(*refs, pixels=pixels),
        shape(CI * ROWS, COLS), flags, g, left3, right3,
        smem=1,
    )
    grad_f, grad_c = call(
        last_kernel, (shape(*fine_weight.shape), shape(*coarse_weight.shape)), grads,
        scratch=[pltpu.VMEM((CI, 128), f32)],
    )
    return (logits[:MAPS, 0], saliency.reshape(maps.shape), grad_f, grad_c)


def solution(mesh):
    in_specs = (P(None, None, "face", "tile"), P(), P(), P(), P(), P(), P(), P(), P())
    out_specs = (P(), P(None, None, "face", "tile"), P(), P())
    return jax.shard_map(
        on_device, mesh=mesh, in_specs=in_specs, out_specs=out_specs, check_vma=False
    )
```

time: 431 us -> 147 us (0.34)
  blocking collectives: 219 us -> 8.18 us
  starting transfers between devices: 129 us -> 74.7 us
  other arithmetic: 21.7 us -> 0.5 us
  Pallas kernels: 0 us -> 12.9 us
  local copies, waits for them, and re-layouts: 17.1 us -> 7.76 us
  waiting for transfers between devices: 32.8 us -> 41.2 us
  matrix products: 8.29 us -> 0.19 us
    psum x2 -> x0, blocking collectives: 219 us -> none  [the longest x1 115 us: on_device(): features = lax.psum(act1.sum(axis=(2, 3)), ('face', 'tile')) / pooled_count]
    ppermute x32 -> x10, starting transfers between devices: 129 us -> 43.3 us  [the longest x5 23.1 us: both_ways(): lax.ppermute(value, axis, forward)]
    all_to_all x0 -> x2, starting transfers between devices: none -> 31.4 us  [share(): return lax.all_to_all(rows, axes, 0, 0, tiled=True)]
    all_to_all x0 -> x2, waiting for transfers between devices: none -> 29 us  [share(): return lax.all_to_all(rows, axes, 0, 0, tiled=True)]
    ppermute x32 -> x10, waiting for transfers between devices: 32.8 us -> 12.2 us  [the longest x5 12.2 us: both_ways(): lax.ppermute(value, axis, backward)]
    pallas_call x0 -> x7, Pallas kernels: none -> 12.9 us  [call(): pl.pallas_call(kernel, out_shape=outs, in_specs=in_specs, out_specs=jax.t...]
    scatter x15 -> x0, other arithmetic: 10.7 us -> none  [the longest x8 6.22 us: stencil(): lower.at[..., -1, :]]
    all_to_all x0 -> x1, blocking collectives: none -> 8.18 us  [share(): return lax.all_to_all(rows, axes, 0, 0, tiled=True)]
  transfers between devices with their start and end apart: 32 -> 12, of which waited for: 13 -> 6; matrix products, arithmetic and copies ran while one was open for 4% -> 2% of each run, Pallas kernels for 0% -> 1%
where the time goes in v2:
time: 147 us; the launch traced here: 146 us
  starting transfers between devices  74.7 us (51%)
  waiting for transfers between devices  41.2 us (28%)
  Pallas kernels  12.9 us (9%)
  blocking collectives  8.18 us (6%)
  local copies, waits for them, and re-layouts  7.76 us (5%)
    all_to_all x2, starting transfers between devices, share(): return lax.all_to_all(rows, axes, 0, 0, tiled=True)  31.4 us
    all_to_all x2, waiting for transfers between devices, share(): return lax.all_to_all(rows, axes, 0, 0, tiled=True)  29 us
    ppermute x5, starting transfers between devices, both_ways(): lax.ppermute(value, axis, forward)  23.1 us
    ppermute x5, starting transfers between devices, both_ways(): lax.ppermute(value, axis, backward)  20.2 us
    pallas_call x7, Pallas kernels, call(): pl.pallas_call(kernel, out_shape=outs, in_specs=in_specs, out_specs=jax.t...  12.9 us
    ppermute x5, waiting for transfers between devices, both_ways(): lax.ppermute(value, axis, backward)  12.2 us
    all_to_all x1, blocking collectives, share(): return lax.all_to_all(rows, axes, 0, 0, tiled=True)  8.18 us
    unnamed x14, local copies, waits for them, and re-layouts  3.9 us
  transfers between devices with their start and end apart: 12, of which 6 were waited for; matrix products, arithmetic and copies ran while one was open for 2% of the time, Pallas kernels for 1%

profile of v2, /device:TPU:1, one launch (start us, length us, event | category | flops | bytes accessed | tf_op | source)
XLA Modules:
  0.0 146.4 jit_solution(9535647424171452378)
XLA Ops:
  0.6 0.9 copy.19
  1.5 4.0 %collective-permute-start = (f32[16,16,128]{2,1,0:T(8,128)S(1)}, f32[16,16,128]{2,1,0:T(8,128)S(1)}, u32[]{:S(2)}, u32[]{:S(2)}) collective-permute-start(f32[16,16,128]{2,1,0:T(8,128)S(1)} %bitcast.36), channel_id=1, source_target_pairs={{0,64},{64,128},{128,192},{192,256},{256,320},{320,384},{384,448},... | collective-permute-start | bytes 393224 | tf_op jit(solution)/shard_map/ppermute | solution.py:443
  5.6 4.1 %collective-permute-start.1 = (f32[16,16,128]{2,1,0:T(8,128)S(1)}, f32[16,16,128]{2,1,0:T(8,128)S(1)}, u32[]{:S(2)}, u32[]{:S(2)}) collective-permute-start(f32[16,16,128]{2,1,0:T(8,128)S(1)} %bitcast.37), channel_id=1, source_target_pairs={{64,0},{128,64},{192,128},{256,192},{320,256},{384,320},{448,384},... | collective-permute-start | bytes 393224 | tf_op jit(solution)/shard_map/ppermute | solution.py:443
  9.8 0.1 fusion.3
  9.8 0.6 copy-done.4
  10.4 0.1 multiply_bitcast_fusion
  10.5 0.8 dynamic-slice_bitcast_fusion.1
  11.3 0.6 gather_fusion
  11.9 0.6 gather_fusion.1
  12.6 0.1 reshape.149
  12.7 0.1 shard_map.120
  12.9 7.0 %collective-permute-start.2 = (f32[3,16,128]{2,1,0:T(8,128)S(1)}, f32[3,16,128]{2,1,0:T(8,128)S(1)}, u32[]{:S(2)}, u32[]{:S(2)}) collective-permute-start(f32[3,16,128]{2,1,0:T(8,128)S(1)} %shard_map.120), channel_id=1, source_target_pairs={{0,1},{1,2},{2,3},{3,4},{4,5},{5,6},{6,7},{7,8},{8,9},{9,10},{10,1... | collective-permute-start | bytes 73736 | tf_op jit(solution)/shard_map/ppermute | solution.py:443
  19.9 3.5 %collective-permute-start.3 = (f32[3,16,128]{2,1,0:T(8,128)S(1)}, f32[3,16,128]{2,1,0:T(8,128)S(1)}, u32[]{:S(2)}, u32[]{:S(2)}) collective-permute-start(f32[3,16,128]{2,1,0:T(8,128)S(1)} %shard_map.120), channel_id=1, source_target_pairs={{1,0},{2,1},{3,2},{4,3},{5,4},{6,5},{7,6},{8,7},{9,8},{10,9},{11,1... | collective-permute-start | bytes 73736 | tf_op jit(solution)/shard_map/ppermute | solution.py:443
  23.4 0.1 pad_add_fusion.flags.refs_0_
  23.5 0.1 copy.20.w_ref
  23.6 0.7 copy-done.2
  24.2 0.1 copy.21
  24.3 2.3 %collective-permute-done.3.right_ref = f32[3,16,128]{2,1,0:T(8,128)S(1)} collective-permute-done((f32[3,16,128]{2,1,0:T(8,128)S(1)}, f32[3,16,128]{2,1,0:T(8,128)S(1)}, u32[]{:S(2)}, u32[]{:S(2)}) %collective-permute-start.3) | collective-permute-done | bytes 24608 | tf_op jit(solution)/shard_map/ppermute | solution.py:443
  26.6 3.3 %shard_map.121 = (f32[18,64,128]{2,1,0:T(8,128)S(1)}, f32[20,64,128]{2,1,0:T(8,128)S(1)}, bf16[80,2048]{1,0:T(8,128)(2,1)S(1)}, f32[2,64,128]{2,1,0:T(8,128)S(1)}) custom-call(s32[6]{0:T(128)S(1)} %pad_add_fusion.flags.refs_0_, f32[16,16,128]{2,1,0:T(8,128)S(1)} %collective-permute-done.up_ref, f32[16,16,128]{2,1,0:T(8,128)S(1)} %bitcast.39, ...), custom_call_target="tpu_custom_call" | custom-call | tf_op jit(solution)/shard_map/pallas_call | solution.py:425
  29.9 1.9 %collective-permute-start.4 = (f32[2,64,128]{2,1,0:T(8,128)S(1)}, f32[2,64,128]{2,1,0:T(8,128)S(1)}, u32[]{:S(2)}, u32[]{:S(2)}) collective-permute-start(f32[2,64,128]{2,1,0:T(8,128)S(1)} %get-tuple-element.19), channel_id=1, source_target_pairs={{0,1},{1,2},{2,3},{3,4},{4,5},{5,6},{6,7},{7,8},{8,9},{9,10},{10,1... | collective-permute-start | bytes 196616 | tf_op jit(solution)/shard_map/ppermute | solution.py:443
  31.8 7.6 %collective-permute-start.5 = (f32[2,64,128]{2,1,0:T(8,128)S(1)}, f32[2,64,128]{2,1,0:T(8,128)S(1)}, u32[]{:S(2)}, u32[]{:S(2)}) collective-permute-start(f32[2,64,128]{2,1,0:T(8,128)S(1)} %get-tuple-element.19), channel_id=1, source_target_pairs={{1,0},{2,1},{3,2},{4,3},{5,4},{6,5},{7,6},{8,7},{9,8},{10,9},{11,1... | collective-permute-start | bytes 196616 | tf_op jit(solution)/shard_map/ppermute | solution.py:443
  39.4 0.1 pad_maximum_fusion.3.w_ref
  39.5 0.8 collective-permute-done.5.right_ref
  40.3 3.0 %shard_map.122 = (f32[512,128]{1,0:T(8,128)}, f32[7,128,128]{2,1,0:T(8,128)S(1)}, f32[128,128]{1,0:T(8,128)S(1)}, f32[3,16,128]{2,1,0:T(8,128)S(1)}) custom-call(s32[6]{0:T(128)S(1)} %pad_add_fusion.flags.refs_0_, f32[18,64,128]{2,1,0:T(8,128)S(1)} %get-tuple-element.18.x1_ref, f32[2,64,128]{2,1,0:T(8,128)S(1)} %collective-permute-done.4.left_ref, ...), custom_call_target="tpu_custom_call" | custom-call | tf_op jit(solution)/shard_map/pallas_call | solution.py:425
  43.3 22.5 %all-to-all-start = ((f32[512,1,128]{2,1,0:T(1,128)}), f32[512,1,128]{2,1,0:T(1,128)S(1)}, u32[]{:S(2)}, u32[]{:S(2)}) async-start(f32[512,1,128]{2,1,0:T(1,128)} %bitcast.14), calls=%async_computation | async-start | bytes 524288 | tf_op jit(solution)/shard_map/all_to_all | solution.py:447
  65.8 0.1 pad_maximum_fusion.4.refs_6_
  65.9 0.1 pad_maximum_fusion.2.refs_7_
  66.0 0.6 copy-done.3
  66.6 0.6 copy-done.6
  67.3 0.7 copy-done.5
  68.0 0.2 fusion.1.refs_2_
  68.1 5.1 %collective-permute-start.6 = (f32[128,128]{1,0:T(8,128)S(1)}, f32[128,128]{1,0:T(8,128)S(1)}, u32[]{:S(2)}, u32[]{:S(2)}) collective-permute-start(f32[128,128]{1,0:T(8,128)S(1)} %get-tuple-element.22), channel_id=1, source_target_pairs={{0,1},{1,2},{2,3},{3,4},{4,5},{5,6},{6,7},{7,8},{8,9},{9,10},{10,1... | collective-permute-start | bytes 196616 | tf_op jit(solution)/shard_map/ppermute | solution.py:443
  73.2 3.1 %collective-permute-start.7 = (f32[128,128]{1,0:T(8,128)S(1)}, f32[128,128]{1,0:T(8,128)S(1)}, u32[]{:S(2)}, u32[]{:S(2)}) collective-permute-start(f32[128,128]{1,0:T(8,128)S(1)} %get-tuple-element.22), channel_id=1, source_target_pairs={{1,0},{2,1},{3,2},{4,3},{5,4},{6,5},{7,6},{8,7},{9,8},{10,9},{11,1... | collective-permute-start | bytes 196616 | tf_op jit(solution)/shard_map/ppermute | solution.py:443
  76.3 4.4 %collective-permute-done.7.refs_10_ = f32[128,128]{1,0:T(8,128)S(1)} collective-permute-done((f32[128,128]{1,0:T(8,128)S(1)}, f32[128,128]{1,0:T(8,128)S(1)}, u32[]{:S(2)}, u32[]{:S(2)}) %collective-permute-start.7) | collective-permute-done | bytes 65568 | tf_op jit(solution)/shard_map/ppermute | solution.py:443
  80.8 9.2 %all-to-all-done = f32[512,1,128]{2,1,0:T(1,128)S(1)} async-done(((f32[512,1,128]{2,1,0:T(1,128)}), f32[512,1,128]{2,1,0:T(1,128)S(1)}, u32[]{:S(2)}, u32[]{:S(2)}) %all-to-all-start) | async-done | bytes 262176 | tf_op jit(solution)/shard_map/all_to_all | solution.py:447
  89.9 0.1 broadcast_in_dim.17.refs_3_
  90.0 0.7 copy-done.1
  90.6 3.1 %shard_map.123 = (f32[8,128]{1,0:T(8,128)S(1)}, f32[128,128]{1,0:T(8,128)S(1)}, f32[20,48,128]{2,1,0:T(8,128)S(1)}, f32[2,32,128]{2,1,0:T(8,128)S(1)}) custom-call(s32[6]{0:T(128)S(1)} %pad_add_fusion.flags.refs_0_, f32[512,128]{1,0:T(8,128)S(1)} %bitcast.40, f32[8,128]{1,0:T(8,128)S(1)} %fusion.1.refs_2_, f32[8,128]{1,0:T(8,128)S(1)} %broadcast_in_dim.17.refs_3_, ...), custom_call_target="tpu_custom_call" | custom-call | tf_op jit(solution)/shard_map/pallas_call | solution.py:425
  93.8 8.2 %all_to_all.33 = f32[8,16,128]{2,1,0:T(8,128)S(1)} all-to-all(f32[8,16,128]{2,1,0:T(8,128)S(1)} %bitcast.42), channel_id=1, replica_groups=mesh['face'=8,'tile'=64] {'face'}, dimensions={0} | all-to-all | bytes 131072 | tf_op jit(solution)/shard_map/all_to_all | solution.py:447
  102.0 0.8 shard_map.125
  102.8 8.9 %all-to-all-start.2 = ((f32[64,16,128]{2,1,0:T(8,128)}), f32[64,16,128]{2,1,0:T(8,128)S(1)}, u32[]{:S(2)}, u32[]{:S(2)}) async-start(f32[64,16,128]{2,1,0:T(8,128)} %bitcast.23), calls=%async_computation.2 | async-start | bytes 1048576 | tf_op jit(solution)/shard_map/all_to_all | solution.py:447
  111.7 5.0 %collective-permute-start.8 = (f32[2,32,128]{2,1,0:T(8,128)S(1)}, f32[2,32,128]{2,1,0:T(8,128)S(1)}, u32[]{:S(2)}, u32[]{:S(2)}) collective-permute-start(f32[2,32,128]{2,1,0:T(8,128)S(1)} %get-tuple-element.28), channel_id=1, source_target_pairs={{0,1},{1,2},{2,3},{3,4},{4,5},{5,6},{6,7},{7,8},{8,9},{9,10},{10,1... | collective-permute-start | bytes 98312 | tf_op jit(solution)/shard_map/ppermute | solution.py:443
  116.8 1.9 %collective-permute-start.9 = (f32[2,32,128]{2,1,0:T(8,128)S(1)}, f32[2,32,128]{2,1,0:T(8,128)S(1)}, u32[]{:S(2)}, u32[]{:S(2)}) collective-permute-start(f32[2,32,128]{2,1,0:T(8,128)S(1)} %get-tuple-element.28), channel_id=1, source_target_pairs={{1,0},{2,1},{3,2},{4,3},{5,4},{6,5},{7,6},{8,7},{9,8},{10,9},{11,1... | collective-permute-start | bytes 98312 | tf_op jit(solution)/shard_map/ppermute | solution.py:443
  118.7 0.6 slice_reduce_fusion
  119.3 4.6 %collective-permute-done.9.refs_3_ = f32[2,32,128]{2,1,0:T(8,128)S(1)} collective-permute-done((f32[2,32,128]{2,1,0:T(8,128)S(1)}, f32[2,32,128]{2,1,0:T(8,128)S(1)}, u32[]{:S(2)}, u32[]{:S(2)}) %collective-permute-start.9) | collective-permute-done | bytes 32800 | tf_op jit(solution)/shard_map/ppermute | solution.py:443
  124.0 1.8 %shard_map.124 = f32[256,128]{1,0:T(8,128)} custom-call(s32[6]{0:T(128)S(1)} %pad_add_fusion.flags.refs_0_, f32[20,48,128]{2,1,0:T(8,128)S(1)} %get-tuple-element.27.refs_1_, f32[2,32,128]{2,1,0:T(8,128)S(1)} %collective-permute-done.8.refs_2_, f32[2,32,128]{2,1,0:T(8,128)S(1)} %collective-permute-done.9.refs_3_), custom_call_target="tpu_custom_call" | custom-call | tf_op jit(solution)/shard_map/pallas_call | solution.py:425
  125.8 19.9 %all-to-all-done.2 = f32[64,16,128]{2,1,0:T(8,128)S(1)} async-done(((f32[64,16,128]{2,1,0:T(8,128)}), f32[64,16,128]{2,1,0:T(8,128)S(1)}, u32[]{:S(2)}, u32[]{:S(2)}) %all-to-all-start.2) | async-done | bytes 524320 | tf_op jit(solution)/shard_map/all_to_all | solution.py:447
  145.6 0.8 shard_map.126
  (21 shorter events, 0.1 us)
Async XLA Ops:
  0.6 66.7 %copy-start = (f32[2,128]{1,0:T(2,128)S(1)}, f32[2,128]{1,0:T(2,128)}, u32[]{:S(2)}) copy-start(f32[2,128]{1,0:T(2,128)} %param.16) | copy-start | bytes 3076
  1.5 11.2 %collective-permute-start = (f32[16,16,128]{2,1,0:T(8,128)S(1)}, f32[16,16,128]{2,1,0:T(8,128)S(1)}, u32[]{:S(2)}, u32[]{:S(2)}) collective-permute-start(f32[16,16,128]{2,1,0:T(8,128)S(1)} %bitcast.36), channel_id=1, source_target_pairs={{0,64},{64,128},{128,192},{192,256},{256,320},{320,384},{384,448},... | collective-permute-start | bytes 393224 | tf_op jit(solution)/shard_map/ppermute | solution.py:443
  5.6 7.2 %collective-permute-start.1 = (f32[16,16,128]{2,1,0:T(8,128)S(1)}, f32[16,16,128]{2,1,0:T(8,128)S(1)}, u32[]{:S(2)}, u32[]{:S(2)}) collective-permute-start(f32[16,16,128]{2,1,0:T(8,128)S(1)} %bitcast.37), channel_id=1, source_target_pairs={{64,0},{128,64},{192,128},{256,192},{320,256},{384,320},{448,384},... | collective-permute-start | bytes 393224 | tf_op jit(solution)/shard_map/ppermute | solution.py:443
  9.7 0.7 copy-start.4
  12.9 11.4 %collective-permute-start.2 = (f32[3,16,128]{2,1,0:T(8,128)S(1)}, f32[3,16,128]{2,1,0:T(8,128)S(1)}, u32[]{:S(2)}, u32[]{:S(2)}) collective-permute-start(f32[3,16,128]{2,1,0:T(8,128)S(1)} %shard_map.120), channel_id=1, source_target_pairs={{0,1},{1,2},{2,3},{3,4},{4,5},{5,6},{6,7},{7,8},{8,9},{9,10},{10,1... | collective-permute-start | bytes 73736 | tf_op jit(solution)/shard_map/ppermute | solution.py:443
  19.9 6.7 %collective-permute-start.3 = (f32[3,16,128]{2,1,0:T(8,128)S(1)}, f32[3,16,128]{2,1,0:T(8,128)S(1)}, u32[]{:S(2)}, u32[]{:S(2)}) collective-permute-start(f32[3,16,128]{2,1,0:T(8,128)S(1)} %shard_map.120), channel_id=1, source_target_pairs={{1,0},{2,1},{3,2},{4,3},{5,4},{6,5},{7,6},{8,7},{9,8},{10,9},{11,1... | collective-permute-start | bytes 73736 | tf_op jit(solution)/shard_map/ppermute | solution.py:443
  23.5 0.7 copy-start.2
  29.9 9.7 %collective-permute-start.4 = (f32[2,64,128]{2,1,0:T(8,128)S(1)}, f32[2,64,128]{2,1,0:T(8,128)S(1)}, u32[]{:S(2)}, u32[]{:S(2)}) collective-permute-start(f32[2,64,128]{2,1,0:T(8,128)S(1)} %get-tuple-element.19), channel_id=1, source_target_pairs={{0,1},{1,2},{2,3},{3,4},{4,5},{5,6},{6,7},{7,8},{8,9},{9,10},{10,1... | collective-permute-start | bytes 196616 | tf_op jit(solution)/shard_map/ppermute | solution.py:443
  31.8 8.5 %collective-permute-start.5 = (f32[2,64,128]{2,1,0:T(8,128)S(1)}, f32[2,64,128]{2,1,0:T(8,128)S(1)}, u32[]{:S(2)}, u32[]{:S(2)}) collective-permute-start(f32[2,64,128]{2,1,0:T(8,128)S(1)} %get-tuple-element.19), channel_id=1, source_target_pairs={{1,0},{2,1},{3,2},{4,3},{5,4},{6,5},{7,6},{8,7},{9,8},{10,9},{11,1... | collective-permute-start | bytes 196616 | tf_op jit(solution)/shard_map/ppermute | solution.py:443
  43.3 46.6 %all-to-all-start = ((f32[512,1,128]{2,1,0:T(1,128)}), f32[512,1,128]{2,1,0:T(1,128)S(1)}, u32[]{:S(2)}, u32[]{:S(2)}) async-start(f32[512,1,128]{2,1,0:T(1,128)} %bitcast.14), calls=%async_computation | async-start | bytes 524288 | tf_op jit(solution)/shard_map/all_to_all | solution.py:447
  65.9 0.7 copy-start.3
  66.6 0.7 copy-start.6
  67.3 0.7 copy-start.5
  68.1 8.2 %collective-permute-start.6 = (f32[128,128]{1,0:T(8,128)S(1)}, f32[128,128]{1,0:T(8,128)S(1)}, u32[]{:S(2)}, u32[]{:S(2)}) collective-permute-start(f32[128,128]{1,0:T(8,128)S(1)} %get-tuple-element.22), channel_id=1, source_target_pairs={{0,1},{1,2},{2,3},{3,4},{4,5},{5,6},{6,7},{7,8},{8,9},{9,10},{10,1... | collective-permute-start | bytes 196616 | tf_op jit(solution)/shard_map/ppermute | solution.py:443
  73.2 7.6 %collective-permute-start.7 = (f32[128,128]{1,0:T(8,128)S(1)}, f32[128,128]{1,0:T(8,128)S(1)}, u32[]{:S(2)}, u32[]{:S(2)}) collective-permute-start(f32[128,128]{1,0:T(8,128)S(1)} %get-tuple-element.22), channel_id=1, source_target_pairs={{1,0},{2,1},{3,2},{4,3},{5,4},{6,5},{7,6},{8,7},{9,8},{10,9},{11,1... | collective-permute-start | bytes 196616 | tf_op jit(solution)/shard_map/ppermute | solution.py:443
  90.0 0.7 copy-start.1
  102.8 42.8 %all-to-all-start.2 = ((f32[64,16,128]{2,1,0:T(8,128)}), f32[64,16,128]{2,1,0:T(8,128)S(1)}, u32[]{:S(2)}, u32[]{:S(2)}) async-start(f32[64,16,128]{2,1,0:T(8,128)} %bitcast.23), calls=%async_computation.2 | async-start | bytes 1048576 | tf_op jit(solution)/shard_map/all_to_all | solution.py:447
  111.7 7.6 %collective-permute-start.8 = (f32[2,32,128]{2,1,0:T(8,128)S(1)}, f32[2,32,128]{2,1,0:T(8,128)S(1)}, u32[]{:S(2)}, u32[]{:S(2)}) collective-permute-start(f32[2,32,128]{2,1,0:T(8,128)S(1)} %get-tuple-element.28), channel_id=1, source_target_pairs={{0,1},{1,2},{2,3},{3,4},{4,5},{5,6},{6,7},{7,8},{8,9},{9,10},{10,1... | collective-permute-start | bytes 98312 | tf_op jit(solution)/shard_map/ppermute | solution.py:443
  116.8 7.2 %collective-permute-start.9 = (f32[2,32,128]{2,1,0:T(8,128)S(1)}, f32[2,32,128]{2,1,0:T(8,128)S(1)}, u32[]{:S(2)}, u32[]{:S(2)}) collective-permute-start(f32[2,32,128]{2,1,0:T(8,128)S(1)} %get-tuple-element.28), channel_id=1, source_target_pairs={{1,0},{2,1},{3,2},{4,3},{5,4},{6,5},{7,6},{8,7},{9,8},{10,9},{11,1... | collective-permute-start | bytes 98312 | tf_op jit(solution)/shard_map/ppermute | solution.py:443

commit v3 on v2

--- a/solution.py
+++ b/solution.py
@@ -20,6 +20,8 @@
 UP2 = 3
 PAIRS = [(0, 4), (1, 5), (2, 6), (3, 7), (-3, 8), (-2, 9), (-1, 10)]
 WHERE = {row: (q, half) for q, pair in enumerate(PAIRS) for half, row in enumerate(pair)}
+FACE, TILE = ("x", "y_lo"), ("z", "y_hi", "core")
+PLANE = ("x", "y_lo", "y_hi", "core")
 bf16, f32 = jnp.bfloat16, jnp.float32
 
 
@@ -125,7 +127,7 @@
 
 def fine_strip(left, right, place):
     group, slot = place // PER, place % PER
-    lane = lanes(left.shape[1])
+    lane = lanes(left[group].shape[0])
     return jnp.where(
         lane < 64, roll(right[group], -SLOT * slot), roll(left[group], 128 - SLOT - SLOT * slot)
     )
@@ -152,31 +154,57 @@
         out_ref[group] = value
 
 
-def fine_rows(up_ref, own_ref, down_ref):
+def before(far, near, odd):
+    return jnp.where(odd == 1, near, far)
+
+
+def after(far, near, odd):
+    return jnp.where(odd == 1, far, near)
+
+
+def fine_rows(far_ref, near_ref, own_ref, odd):
     rows = {}
     for row in range(-UP0, ROWS + UP0):
         if row < 0:
-            rows[row] = up_ref[ROWS + row]
+            rows[row] = before(far_ref[UP0 + row], near_ref[UP0 + row], odd)
         elif row < ROWS:
             rows[row] = own_ref[row]
         else:
-            rows[row] = down_ref[row - ROWS]
+            rows[row] = after(far_ref[row - ROWS], near_ref[row - ROWS], odd)
     return rows
 
 
-def ends_kernel(up_ref, own_ref, down_ref, out_ref):
+def rows_kernel(flags, maps_ref, own_ref, far_ref, near_ref, t_ref):
+    t_ref[...] = maps_ref[...].astype(f32)
+    rows = [t_ref[pl.ds(row, CI, stride=ROWS), :] for row in range(ROWS)]
+    for row in range(ROWS):
+        own_ref[row] = rows[row]
+    for row in range(UP0):
+        first, last = rows[row], rows[ROWS - UP0 + row]
+        far_ref[row] = before(first, last, flags[6])
+        near_ref[row] = after(first, last, flags[6])
+
+
+def both_strips(far_ref, near_ref, odd):
+    count = far_ref.shape[0]
+    left = [before(far_ref[n], near_ref[n], odd) for n in range(count)]
+    return left, [after(far_ref[n], near_ref[n], odd) for n in range(count)]
+
+
+def ends_kernel(flags, far_ref, near_ref, own_ref, out_ref):
     index = end_index(CI)
-    rows = fine_rows(up_ref, own_ref, down_ref)
+    rows = fine_rows(far_ref, near_ref, own_ref, flags[6])
     put_slots(out_ref, [pick(rows[row], index) for row in sorted(rows)], len(rows))
 
 
 def fine_kernel(
-    flags, up_ref, own_ref, down_ref, left_ref, right_ref, w_ref,
+    flags, far_ref, near_ref, own_ref, far0_ref, near0_ref, w_ref,
     x1_ref, sig_ref, terms_ref, ends_ref, t_ref,
 ):
     turns = fine_turns(flags, CI)
-    block = fine_rows(up_ref, own_ref, down_ref)
-    strip = {row: fine_strip(left_ref, right_ref, row + UP0) for row in block}
+    block = fine_rows(far_ref, near_ref, own_ref, flags[6])
+    left, right = both_strips(far0_ref, near0_ref, flags[7])
+    strip = {row: fine_strip(left, right, row + UP0) for row in block}
     first, first_strip = {}, {}
     for row in range(1 - UP0, ROWS + UP0 - 1):
         first[row], first_strip[row] = fine_lap(block, strip, row, turns, True)
@@ -215,15 +243,16 @@
 
 
 def coarse_kernel(
-    flags, x1_ref, left_ref, right_ref, w_ref, feat_ref, sig_ref, ends_ref, gram_ref, t_ref, s_ref
+    flags, x1_ref, far_ref, near_ref, w_ref, feat_ref, sig_ref, ends_ref, gram_ref, t_ref, s_ref
 ):
     turns = coarse_turns(flags, CA)
     lane = lanes(CA)
+    left, right = both_strips(far_ref, near_ref, flags[7])
     rows = {}
     for row in range(-UP1, CROWS + UP1):
         place = row + UP1
         rows[row] = coarse_row(
-            x1_ref[place], left_ref[place // PER], right_ref[place // PER], place % PER
+            x1_ref[place], left[place // PER], right[place // PER], place % PER
         )
     first = {row: coarse_lap(rows, row, turns) for row in range(1 - UP1, CROWS + UP1 - 1)}
     second = {
@@ -279,7 +308,7 @@
 
 def back_kernel(
     flags, feat_ref, shift_ref, labels_ref, fw_ref, out_ref, w1_ref, w0_ref,
-    sig1_ref, left_ref, right_ref, gram_ref, sig0_ref, terms_ref,
+    sig1_ref, far_ref, near_ref, gram_ref, sig0_ref, terms_ref,
     logits_ref, grads_ref, g_ref, ends_ref, s_ref, d_ref,
     *, pooled,
 ):
@@ -308,7 +337,10 @@
         coarse.append(value + roll(value, 32))
     slabs = len(PAIRS) + 2
     for q in range(slabs):
-        value = sig1_ref[q] if q < len(PAIRS) else (left_ref, right_ref)[q - len(PAIRS)][...]
+        if q < len(PAIRS):
+            value = sig1_ref[q]
+        else:
+            value = (before, after)[q - len(PAIRS)](far_ref[...], near_ref[...], flags[7])
         high, low = halves(value * dfull)
         here = pl.ds(q * 128, 128)
         for m in range(MAPS):
@@ -381,13 +413,14 @@
     put_slots(ends_ref, filled, len(filled))
 
 
-def saliency_kernel(flags, g_ref, left_ref, right_ref, out_ref, *, pixels):
+def saliency_kernel(flags, g_ref, far_ref, near_ref, out_ref, *, pixels):
     turns = fine_turns(flags, CI)
+    left, right = both_strips(far_ref, near_ref, flags[7])
     g0, g1, g2, s1, s2 = {}, {}, {}, {}, {}
     for row in range(-2, ROWS + 2):
         value = g_ref[row + 2]
         g0[row], g1[row], g2[row] = (value[CI * k : CI * (k + 1)] for k in range(3))
-        strip = fine_strip(left_ref, right_ref, row + 2)
+        strip = fine_strip(left, right, row + 2)
         s1[row], s2[row] = strip[:CI], strip[CI:]
     inner, inner_strip = {}, {}
     for row in range(-1, ROWS + 1):
@@ -405,6 +438,10 @@
         value = value + in_ref[CI * n : CI * (n + 1)]
     for n in range(out_ref.shape[0] // CI):
         out_ref[CI * n : CI * (n + 1)] = value
+
+
+def row_again_kernel(in_ref, out_ref):
+    out_ref[...] = jnp.broadcast_to(jnp.sum(in_ref[...], axis=0, keepdims=True), out_ref.shape)
 
 
 def last_kernel(in_ref, fine_ref, coarse_ref, tmp_ref):
@@ -436,11 +473,11 @@
     return jax.ShapeDtypeStruct(dims, dtype)
 
 
-def both_ways(value, axis):
+def exchange(axis, far_value, near_value):
     count = lax.axis_size(axis)
-    forward = [(n, (n + 1) % count) for n in range(count)]
-    backward = [(target, source) for source, target in forward]
-    return lax.ppermute(value, axis, forward), lax.ppermute(value, axis, backward)
+    far = [(n, (n + (1 if n % 2 else count - 1)) % count) for n in range(count)]
+    near = [(n, n + (1 if n % 2 == 0 else -1)) for n in range(count)]
+    return lax.ppermute(far_value, axis, far), lax.ppermute(near_value, axis, near)
 
 
 def share(rows, axes):
@@ -451,11 +488,12 @@
     maps, params, labels, edge_flip,
     fine_weight, coarse_weight, feature_weight, param_weight, out_weight,
 ):
-    faces, tiles = lax.axis_size("face"), lax.axis_size("tile")
-    devices = faces * tiles
-    f, t = lax.axis_index("face"), lax.axis_index("tile")
+    faces, tiles = lax.axis_size(FACE), lax.axis_size(TILE)
+    f, t = lax.axis_index(FACE), lax.axis_index(TILE)
     columns = jnp.stack([(t + tiles - 1) % tiles, t, (t + 1) % tiles])
-    flags = jnp.concatenate([edge_flip[f][columns], edge_flip[(f + 1) % faces][columns]])
+    flags = jnp.concatenate(
+        [edge_flip[f][columns], edge_flip[(f + 1) % faces][columns], jnp.stack([f % 2, t % 2])]
+    )
     eye = jnp.eye(MAPS, dtype=f32)
     fine = jnp.einsum("kio,mn->monki", fine_weight, eye)
     fine = fine.transpose(0, 1, 3, 2, 4).reshape(CA, ORDER * CI)
@@ -469,10 +507,15 @@
     shift = jnp.dot(jnp.pad(params, pad), param_weight, precision=exact)
     labels8 = jnp.broadcast_to(jnp.pad(labels.astype(f32)[:, None], pad), (8, 128))
 
-    own = maps.reshape(CI, ROWS, COLS).transpose(1, 0, 2).astype(f32)
-    up, down = both_ways(own, "face")
-    ends0 = call(ends_kernel, shape(groups(ROWS + 2 * UP0), CI, 128), up, own, down)
-    left0, right0 = both_ways(ends0, "tile")
+    trade = shape(UP0, CI, COLS)
+    own, far, near = call(
+        rows_kernel, (shape(ROWS, CI, COLS), trade, trade), flags, maps.reshape(CI * ROWS, COLS),
+        smem=1,
+        scratch=[pltpu.VMEM((CI * ROWS, COLS), f32)],
+    )
+    far, near = exchange(FACE, far, near)
+    ends0 = call(ends_kernel, shape(groups(ROWS + 2 * UP0), CI, 128), flags, far, near, own, smem=1)
+    far0, near0 = exchange(TILE, ends0, ends0)
     crows = CROWS + 2 * UP1
     x1, sig0, terms0, ends1 = call(
         fine_kernel,
@@ -482,53 +525,55 @@
             shape(5 * CI, ROWS * 128, dtype=bf16),
             shape(groups(crows), CA, 128),
         ),
-        flags, up, own, down, left0, right0, fine_forward,
+        flags, far, near, own, far0, near0, fine_forward,
         smem=1,
         scratch=[pltpu.VMEM((8 * CI, 2 * crows * 128), bf16)],
     )
-    left1, right1 = both_ways(ends1, "tile")
+    far1, near1 = exchange(TILE, ends1, ends1)
     feats, sig1, ends2, grams = call(
         coarse_kernel,
         (
-            shape(devices, CB),
+            shape(lax.axis_size(PLANE), CB),
             shape(len(PAIRS), CB, 128),
             shape(CB, 128),
             shape(ORDER, CH0, 128),
         ),
-        flags, x1, left1, right1, coarse_forward,
+        flags, x1, far1, near1, coarse_forward,
         smem=1,
         scratch=[
             pltpu.VMEM((MAPS, 3 * ORDER * CH0, len(PAIRS) * 128), bf16),
             pltpu.VMEM((2 * CB, 4 * 128), bf16),
         ],
     )
-    left2, right2 = both_ways(ends2, "tile")
-    feats = share(feats, ("face", "tile"))
+    far2, near2 = exchange(TILE, ends2, ends2)
+    feats = share(feats, PLANE)
+    feats = call(row_again_kernel, shape(lax.axis_size("z"), CB), feats)
+    feats = share(feats, "z")
     pooled = CROWS * faces * CCOLS * tiles
     logits, grads, g, ends3 = call(
         lambda *refs: back_kernel(*refs, pooled=pooled),
         (
             shape(8, 128),
-            shape(faces * CI, 128),
+            shape(lax.axis_size(PLANE) * CI, 128),
             shape(ROWS + 4, ORDER * CI, 128),
             shape(groups(ROWS + 4), 2 * CI, 128),
         ),
         flags, feats, shift, labels8, features4, out_weight[None],
-        coarse_backward, fine_backward, sig1, left2, right2, grams, sig0, terms0,
+        coarse_backward, fine_backward, sig1, far2, near2, grams, sig0, terms0,
         smem=1,
         scratch=[
             pltpu.VMEM((MAPS, 3 * CH1, (len(PAIRS) + 2) * 128), bf16),
             pltpu.VMEM((3 * CA, (ROWS + 4) * 128), bf16),
         ],
     )
-    left3, right3 = both_ways(ends3, "tile")
-    grads = share(grads, "face")
-    grads = call(again_kernel, shape(tiles * CI, 128), grads)
-    grads = share(grads, "tile")
+    far3, near3 = exchange(TILE, ends3, ends3)
+    grads = share(grads, PLANE)
+    grads = call(again_kernel, shape(lax.axis_size("z") * CI, 128), grads)
+    grads = share(grads, "z")
     pixels = float(ROWS * faces * COLS * tiles)
     saliency = call(
         lambda *refs: saliency_kernel(*refs, pixels=pixels),
-        shape(CI * ROWS, COLS), flags, g, left3, right3,
+        shape(CI * ROWS, COLS), flags, g, far3, near3,
         smem=1,
     )
     grad_f, grad_c = call(
@@ -539,8 +584,14 @@
 
 
 def solution(mesh):
-    in_specs = (P(None, None, "face", "tile"), P(), P(), P(), P(), P(), P(), P(), P())
-    out_specs = (P(), P(None, None, "face", "tile"), P(), P())
+    faces, tiles = mesh.devices.shape
+    sizes = (faces // 2, 2, tiles // 4, 2, 2)
+    fine_mesh = jax.sharding.Mesh(mesh.devices.reshape(sizes), ("x", "y_lo", "z", "y_hi", "core"))
+    tiled = P(None, None, FACE, TILE)
     return jax.shard_map(
-        on_device, mesh=mesh, in_specs=in_specs, out_specs=out_specs, check_vma=False
-    )
+        on_device,
+        mesh=fine_mesh,
+        in_specs=(tiled, P(), P(), P(), P(), P(), P(), P(), P()),
+        out_specs=(P(), tiled, P(), P()),
+        check_vma=False,
+    )

time: 147 us -> 122 us (0.83)
  starting transfers between devices: 74.7 us -> 56.8 us
  waiting for transfers between devices: 41.2 us -> 26 us
  blocking collectives: 8.18 us -> 15.6 us
  local copies, waits for them, and re-layouts: 7.76 us -> 5.76 us
    all_to_all x2 -> x3, waiting for transfers between devices: 29 us -> 12.1 us  [share(): return lax.all_to_all(rows, axes, 0, 0, tiled=True)]
    all_to_all x2 -> x3, starting transfers between devices: 31.4 us -> 17.8 us  [share(): return lax.all_to_all(rows, axes, 0, 0, tiled=True)]
    all_to_all x1, blocking collectives: 8.18 us -> 15.6 us  [share(): return lax.all_to_all(rows, axes, 0, 0, tiled=True)]
    ppermute x10, starting transfers between devices: 43.3 us -> 39 us  [the longest x5 21.1 us: exchange(): lax.ppermute(near_value, axis, near)]
    ppermute x10, waiting for transfers between devices: 12.2 us -> 13.9 us  [the longest x5 12.3 us: exchange(): lax.ppermute(far_value, axis, far)]
    pallas_call x7 -> x9, Pallas kernels: 12.9 us -> 14.3 us  [call(): pl.pallas_call(kernel, out_shape=outs, in_specs=in_specs, out_specs=jax.t...]
    unnamed x14 -> x16, local copies, waits for them, and re-layouts: 3.9 us -> 2.78 us
  transfers between devices with their start and end apart: 12 -> 13, of which waited for: 6 -> 6; matrix products, arithmetic and copies ran while one was open for 2% -> 1% of each run, Pallas kernels for 1% -> 2%
where the time goes in v3:
time: 122 us; the launch traced here: 120 us
  starting transfers between devices  56.8 us (47%)
  waiting for transfers between devices  26 us (21%)
  blocking collectives  15.6 us (13%)
  Pallas kernels  14.3 us (12%)
  local copies, waits for them, and re-layouts  5.76 us (5%)
    ppermute x5, starting transfers between devices, exchange(): lax.ppermute(near_value, axis, near)  21.1 us
    ppermute x5, starting transfers between devices, exchange(): lax.ppermute(far_value, axis, far)  17.9 us
    all_to_all x3, starting transfers between devices, share(): return lax.all_to_all(rows, axes, 0, 0, tiled=True)  17.8 us
    all_to_all x1, blocking collectives, share(): return lax.all_to_all(rows, axes, 0, 0, tiled=True)  15.6 us
    pallas_call x9, Pallas kernels, call(): pl.pallas_call(kernel, out_shape=outs, in_specs=in_specs, out_specs=jax.t...  14.3 us
    ppermute x5, waiting for transfers between devices, exchange(): lax.ppermute(far_value, axis, far)  12.3 us
    all_to_all x3, waiting for transfers between devices, share(): return lax.all_to_all(rows, axes, 0, 0, tiled=True)  12.1 us
    unnamed x16, local copies, waits for them, and re-layouts  2.78 us
  transfers between devices with their start and end apart: 13, of which 6 were waited for; matrix products, arithmetic and copies ran while one was open for 1% of the time, Pallas kernels for 2%

profile of v3, /device:TPU:1, one launch (start us, length us, event | category | flops | bytes accessed | tf_op | source)
XLA Modules:
  0.0 120.2 jit_solution(12590871183193070233)
XLA Ops:
  0.7 0.1 fusion.3
  0.8 0.8 dynamic-slice_bitcast_fusion.1
  1.5 0.6 gather_fusion.1
  2.2 0.6 gather_fusion
  2.8 0.1 pad_add_fusion.flags.refs_0_
  2.9 0.1 copy-done.1
  3.0 0.6 shard_map.120
  3.6 6.2 %collective-permute-start = (f32[12,16,128]{2,1,0:T(8,128)S(1)}, f32[12,16,128]{2,1,0:T(8,128)S(1)}, u32[]{:S(2)}, u32[]{:S(2)}) collective-permute-start(f32[12,16,128]{2,1,0:T(8,128)S(1)} %get-tuple-element.21), channel_id=1, source_target_pairs={{0,448},{64,128},{128,64},{192,256},{256,192},{320,384},{384,320},... | collective-permute-start | bytes 294920 | tf_op jit(solution)/shard_map/ppermute | solution.py:480
  9.9 1.9 %collective-permute-start.1 = (f32[12,16,128]{2,1,0:T(8,128)S(1)}, f32[12,16,128]{2,1,0:T(8,128)S(1)}, u32[]{:S(2)}, u32[]{:S(2)}) collective-permute-start(f32[12,16,128]{2,1,0:T(8,128)S(1)} %get-tuple-element.22), channel_id=1, source_target_pairs={{0,64},{64,0},{128,192},{192,128},{256,320},{320,256},{384,448},{4... | collective-permute-start | bytes 294920 | tf_op jit(solution)/shard_map/ppermute | solution.py:480
  11.9 0.7 copy-done.5
  12.6 0.1 multiply_bitcast_fusion
  12.6 0.1 reshape.152
  12.8 0.6 copy-done.6
  13.4 0.2 fusion.1.refs_2_
  13.7 1.6 %collective-permute-done.1.near_ref = f32[12,16,128]{2,1,0:T(8,128)S(1)} collective-permute-done((f32[12,16,128]{2,1,0:T(8,128)S(1)}, f32[12,16,128]{2,1,0:T(8,128)S(1)}, u32[]{:S(2)}, u32[]{:S(2)}) %collective-permute-start.1) | collective-permute-done | bytes 98336 | tf_op jit(solution)/shard_map/ppermute | solution.py:480
  15.2 0.7 shard_map.121
  15.9 6.7 %collective-permute-start.3 = (f32[3,16,128]{2,1,0:T(8,128)S(1)}, f32[3,16,128]{2,1,0:T(8,128)S(1)}, u32[]{:S(2)}, u32[]{:S(2)}) collective-permute-start(f32[3,16,128]{2,1,0:T(8,128)S(1)} %shard_map.121), channel_id=1, source_target_pairs={{0,1},{1,0},{2,3},{3,2},{4,5},{5,4},{6,7},{7,6},{8,9},{9,8},{10,11... | collective-permute-start | bytes 73736 | tf_op jit(solution)/shard_map/ppermute | solution.py:480
  22.6 1.9 %collective-permute-start.2 = (f32[3,16,128]{2,1,0:T(8,128)S(1)}, f32[3,16,128]{2,1,0:T(8,128)S(1)}, u32[]{:S(2)}, u32[]{:S(2)}) collective-permute-start(f32[3,16,128]{2,1,0:T(8,128)S(1)} %shard_map.121), channel_id=1, source_target_pairs={{0,63},{1,2},{2,1},{3,4},{4,3},{5,6},{6,5},{7,8},{8,7},{9,10},{10,... | collective-permute-start | bytes 73736 | tf_op jit(solution)/shard_map/ppermute | solution.py:480
  24.6 0.1 pad_maximum_fusion.2.refs_7_
  24.7 0.6 copy-done.3
  25.3 0.1 copy.18
  25.5 3.8 %collective-permute-done.2.far0_ref = f32[3,16,128]{2,1,0:T(8,128)S(1)} collective-permute-done((f32[3,16,128]{2,1,0:T(8,128)S(1)}, f32[3,16,128]{2,1,0:T(8,128)S(1)}, u32[]{:S(2)}, u32[]{:S(2)}) %collective-permute-start.2) | collective-permute-done | bytes 24608 | tf_op jit(solution)/shard_map/ppermute | solution.py:480
  29.3 3.3 %shard_map.122 = (f32[18,64,128]{2,1,0:T(8,128)S(1)}, f32[20,64,128]{2,1,0:T(8,128)S(1)}, bf16[80,2048]{1,0:T(8,128)(2,1)S(1)}, f32[2,64,128]{2,1,0:T(8,128)S(1)}) custom-call(s32[8]{0:T(128)S(1)} %pad_add_fusion.flags.refs_0_, f32[12,16,128]{2,1,0:T(8,128)S(1)} %collective-permute-done.far_ref, f32[12,16,128]{2,1,0:T(8,128)S(1)} %collective-permute-done.1.near_ref, ...), custom_call_target="tpu_custom_call" | custom-call | tf_op jit(solution)/shard_map/pallas_call | solution.py:462
  32.5 8.0 %collective-permute-start.5 = (f32[2,64,128]{2,1,0:T(8,128)S(1)}, f32[2,64,128]{2,1,0:T(8,128)S(1)}, u32[]{:S(2)}, u32[]{:S(2)}) collective-permute-start(f32[2,64,128]{2,1,0:T(8,128)S(1)} %get-tuple-element.25), channel_id=1, source_target_pairs={{0,1},{1,0},{2,3},{3,2},{4,5},{5,4},{6,7},{7,6},{8,9},{9,8},{10,11... | collective-permute-start | bytes 196616 | tf_op jit(solution)/shard_map/ppermute | solution.py:480
  40.5 1.9 %collective-permute-start.4 = (f32[2,64,128]{2,1,0:T(8,128)S(1)}, f32[2,64,128]{2,1,0:T(8,128)S(1)}, u32[]{:S(2)}, u32[]{:S(2)}) collective-permute-start(f32[2,64,128]{2,1,0:T(8,128)S(1)} %get-tuple-element.25), channel_id=1, source_target_pairs={{0,63},{1,2},{2,1},{3,4},{4,3},{5,6},{6,5},{7,8},{8,7},{9,10},{10,... | collective-permute-start | bytes 196616 | tf_op jit(solution)/shard_map/ppermute | solution.py:480
  42.4 0.1 pad_maximum_fusion.3.w_ref
  42.5 5.1 %collective-permute-done.4.far_ref = f32[2,64,128]{2,1,0:T(8,128)S(1)} collective-permute-done((f32[2,64,128]{2,1,0:T(8,128)S(1)}, f32[2,64,128]{2,1,0:T(8,128)S(1)}, u32[]{:S(2)}, u32[]{:S(2)}) %collective-permute-start.4) | collective-permute-done | bytes 65568 | tf_op jit(solution)/shard_map/ppermute | solution.py:480
  47.6 2.9 %shard_map.123 = (f32[32,128]{1,0:T(8,128)}, f32[7,128,128]{2,1,0:T(8,128)S(1)}, f32[128,128]{1,0:T(8,128)S(1)}, f32[3,16,128]{2,1,0:T(8,128)S(1)}) custom-call(s32[8]{0:T(128)S(1)} %pad_add_fusion.flags.refs_0_, f32[18,64,128]{2,1,0:T(8,128)S(1)} %get-tuple-element.24.x1_ref, f32[2,64,128]{2,1,0:T(8,128)S(1)} %collective-permute-done.4.far_ref, ...), custom_call_target="tpu_custom_call" | custom-call | tf_op jit(solution)/shard_map/pallas_call | solution.py:462
  50.5 5.6 %all-to-all-start = ((f32[32,1,128]{2,1,0:T(1,128)}), f32[32,1,128]{2,1,0:T(1,128)S(1)}, u32[]{:S(2)}, u32[]{:S(2)}) async-start(f32[32,1,128]{2,1,0:T(1,128)} %bitcast.14), calls=%async_computation | async-start | bytes 32768 | tf_op jit(solution)/shard_map/all_to_all | solution.py:484
  56.1 0.1 pad_maximum_fusion.4.refs_6_
  56.2 2.3 %collective-permute-start.7 = (f32[128,128]{1,0:T(8,128)S(1)}, f32[128,128]{1,0:T(8,128)S(1)}, u32[]{:S(2)}, u32[]{:S(2)}) collective-permute-start(f32[128,128]{1,0:T(8,128)S(1)} %get-tuple-element.28), channel_id=1, source_target_pairs={{0,1},{1,0},{2,3},{3,2},{4,5},{5,4},{6,7},{7,6},{8,9},{9,8},{10,11... | collective-permute-start | bytes 196616 | tf_op jit(solution)/shard_map/ppermute | solution.py:480
  58.5 4.9 %collective-permute-start.6 = (f32[128,128]{1,0:T(8,128)S(1)}, f32[128,128]{1,0:T(8,128)S(1)}, u32[]{:S(2)}, u32[]{:S(2)}) collective-permute-start(f32[128,128]{1,0:T(8,128)S(1)} %get-tuple-element.28), channel_id=1, source_target_pairs={{0,63},{1,2},{2,1},{3,4},{4,3},{5,6},{6,5},{7,8},{8,7},{9,10},{10,... | collective-permute-start | bytes 196616 | tf_op jit(solution)/shard_map/ppermute | solution.py:480
  63.3 0.6 shard_map.124
  63.9 8.7 %all-to-all-start.1 = ((f32[16,1,128]{2,1,0:T(1,128)}), f32[16,1,128]{2,1,0:T(1,128)S(1)}, u32[]{:S(2)}, u32[]{:S(2)}) async-start(f32[16,1,128]{2,1,0:T(1,128)} %bitcast.17), calls=%async_computation.1 | async-start | bytes 16384 | tf_op jit(solution)/shard_map/all_to_all | solution.py:484
  72.6 11.2 %all-to-all-done.1 = f32[16,1,128]{2,1,0:T(1,128)S(1)} async-done(((f32[16,1,128]{2,1,0:T(1,128)}), f32[16,1,128]{2,1,0:T(1,128)S(1)}, u32[]{:S(2)}, u32[]{:S(2)}) %all-to-all-start.1) | async-done | bytes 8224 | tf_op jit(solution)/shard_map/all_to_all | solution.py:484
  83.9 0.1 broadcast_in_dim.17.refs_3_
  83.9 0.7 copy-done.2
  84.6 3.1 %shard_map.125 = (f32[8,128]{1,0:T(8,128)S(1)}, f32[512,128]{1,0:T(8,128)S(1)}, f32[20,48,128]{2,1,0:T(8,128)S(1)}, f32[2,32,128]{2,1,0:T(8,128)S(1)}) custom-call(s32[8]{0:T(128)S(1)} %pad_add_fusion.flags.refs_0_, f32[16,128]{1,0:T(8,128)S(1)} %bitcast.44, f32[8,128]{1,0:T(8,128)S(1)} %fusion.1.refs_2_, f32[8,128]{1,0:T(8,128)S(1)} %broadcast_in_dim.17.refs_3_, ...), custom_call_target="tpu_custom_call" | custom-call | tf_op jit(solution)/shard_map/pallas_call | solution.py:462
  87.7 15.6 %all_to_all.44 = f32[32,16,128]{2,1,0:T(8,128)S(1)} all-to-all(f32[32,16,128]{2,1,0:T(8,128)S(1)} %bitcast.41), channel_id=1, replica_groups=mesh['x'=4,'y_lo'=2,'z'=16,'y_hi'=2,'core'=2] {'x','y_lo','y_hi','core'}, dimensions={0} | all-to-all | bytes 524288 | tf_op jit(solution)/shard_map/all_to_all | solution.py:484
  103.3 0.7 shard_map.127
  104.0 3.5 %all-to-all-start.3 = ((f32[16,16,128]{2,1,0:T(8,128)}), f32[16,16,128]{2,1,0:T(8,128)S(1)}, u32[]{:S(2)}, u32[]{:S(2)}) async-start(f32[16,16,128]{2,1,0:T(8,128)} %bitcast.26), calls=%async_computation.3 | async-start | bytes 262144 | tf_op jit(solution)/shard_map/all_to_all | solution.py:484
  107.5 2.3 %collective-permute-start.9 = (f32[2,32,128]{2,1,0:T(8,128)S(1)}, f32[2,32,128]{2,1,0:T(8,128)S(1)}, u32[]{:S(2)}, u32[]{:S(2)}) collective-permute-start(f32[2,32,128]{2,1,0:T(8,128)S(1)} %get-tuple-element.34), channel_id=1, source_target_pairs={{0,1},{1,0},{2,3},{3,2},{4,5},{5,4},{6,7},{7,6},{8,9},{9,8},{10,11... | collective-permute-start | bytes 98312 | tf_op jit(solution)/shard_map/ppermute | solution.py:480
  109.9 3.0 %collective-permute-start.8 = (f32[2,32,128]{2,1,0:T(8,128)S(1)}, f32[2,32,128]{2,1,0:T(8,128)S(1)}, u32[]{:S(2)}, u32[]{:S(2)}) collective-permute-start(f32[2,32,128]{2,1,0:T(8,128)S(1)} %get-tuple-element.34), channel_id=1, source_target_pairs={{0,63},{1,2},{2,1},{3,4},{4,3},{5,6},{6,5},{7,8},{8,7},{9,10},{10,... | collective-permute-start | bytes 98312 | tf_op jit(solution)/shard_map/ppermute | solution.py:480
  112.8 0.6 slice_reduce_fusion
  113.4 3.4 %collective-permute-done.8.refs_2_ = f32[2,32,128]{2,1,0:T(8,128)S(1)} collective-permute-done((f32[2,32,128]{2,1,0:T(8,128)S(1)}, f32[2,32,128]{2,1,0:T(8,128)S(1)}, u32[]{:S(2)}, u32[]{:S(2)}) %collective-permute-start.8) | collective-permute-done | bytes 32800 | tf_op jit(solution)/shard_map/ppermute | solution.py:480
  116.9 1.8 %shard_map.126 = f32[256,128]{1,0:T(8,128)} custom-call(s32[8]{0:T(128)S(1)} %pad_add_fusion.flags.refs_0_, f32[20,48,128]{2,1,0:T(8,128)S(1)} %get-tuple-element.33.refs_1_, f32[2,32,128]{2,1,0:T(8,128)S(1)} %collective-permute-done.8.refs_2_, f32[2,32,128]{2,1,0:T(8,128)S(1)} %collective-permute-done.9.refs_3_), custom_call_target="tpu_custom_call" | custom-call | tf_op jit(solution)/shard_map/pallas_call | solution.py:462
  118.7 0.8 all-to-all-done.3
  119.5 0.7 shard_map.128
  (26 shorter events, 0.2 us)
Async XLA Ops:
  0.6 12.1 %copy-start = (f32[2,128]{1,0:T(2,128)S(1)}, f32[2,128]{1,0:T(2,128)}, u32[]{:S(2)}) copy-start(f32[2,128]{1,0:T(2,128)} %param.16) | copy-start | bytes 3076
  2.2 0.8 copy-start.1
  3.0 8.8 %copy-start.4 = (f32[32,128]{1,0:T(8,128)S(1)}, f32[32,128]{1,0:T(8,128)}, u32[]{:S(2)}) copy-start(f32[32,128]{1,0:T(8,128)} %param.15) | copy-start | bytes 49156
  3.6 10.0 %collective-permute-start = (f32[12,16,128]{2,1,0:T(8,128)S(1)}, f32[12,16,128]{2,1,0:T(8,128)S(1)}, u32[]{:S(2)}, u32[]{:S(2)}) collective-permute-start(f32[12,16,128]{2,1,0:T(8,128)S(1)} %get-tuple-element.21), channel_id=1, source_target_pairs={{0,448},{64,128},{128,64},{192,256},{256,192},{320,384},{384,320},... | collective-permute-start | bytes 294920 | tf_op jit(solution)/shard_map/ppermute | solution.py:480
  9.9 2.0 %copy-start.7 = (s32[4]{0:T(128)S(1)}, s32[4]{0:T(128)}, u32[]{:S(2)}) copy-start(s32[4]{0:T(128)} %param.11) | copy-start | bytes 52
  9.9 5.4 %collective-permute-start.1 = (f32[12,16,128]{2,1,0:T(8,128)S(1)}, f32[12,16,128]{2,1,0:T(8,128)S(1)}, u32[]{:S(2)}, u32[]{:S(2)}) collective-permute-start(f32[12,16,128]{2,1,0:T(8,128)S(1)} %get-tuple-element.22), channel_id=1, source_target_pairs={{0,64},{64,0},{128,192},{192,128},{256,320},{320,256},{384,448},{4... | collective-permute-start | bytes 294920 | tf_op jit(solution)/shard_map/ppermute | solution.py:480
  11.9 0.7 copy-start.5
  12.7 0.7 copy-start.6
  15.9 9.5 %collective-permute-start.3 = (f32[3,16,128]{2,1,0:T(8,128)S(1)}, f32[3,16,128]{2,1,0:T(8,128)S(1)}, u32[]{:S(2)}, u32[]{:S(2)}) collective-permute-start(f32[3,16,128]{2,1,0:T(8,128)S(1)} %shard_map.121), channel_id=1, source_target_pairs={{0,1},{1,0},{2,3},{3,2},{4,5},{5,4},{6,7},{7,6},{8,9},{9,8},{10,11... | collective-permute-start | bytes 73736 | tf_op jit(solution)/shard_map/ppermute | solution.py:480
  22.6 6.7 %collective-permute-start.2 = (f32[3,16,128]{2,1,0:T(8,128)S(1)}, f32[3,16,128]{2,1,0:T(8,128)S(1)}, u32[]{:S(2)}, u32[]{:S(2)}) collective-permute-start(f32[3,16,128]{2,1,0:T(8,128)S(1)} %shard_map.121), channel_id=1, source_target_pairs={{0,63},{1,2},{2,1},{3,4},{4,3},{5,6},{6,5},{7,8},{8,7},{9,10},{10,... | collective-permute-start | bytes 73736 | tf_op jit(solution)/shard_map/ppermute | solution.py:480
  24.6 0.7 copy-start.3
  32.5 10.0 %collective-permute-start.5 = (f32[2,64,128]{2,1,0:T(8,128)S(1)}, f32[2,64,128]{2,1,0:T(8,128)S(1)}, u32[]{:S(2)}, u32[]{:S(2)}) collective-permute-start(f32[2,64,128]{2,1,0:T(8,128)S(1)} %get-tuple-element.25), channel_id=1, source_target_pairs={{0,1},{1,0},{2,3},{3,2},{4,5},{5,4},{6,7},{7,6},{8,9},{9,8},{10,11... | collective-permute-start | bytes 196616 | tf_op jit(solution)/shard_map/ppermute | solution.py:480
  40.5 7.1 %collective-permute-start.4 = (f32[2,64,128]{2,1,0:T(8,128)S(1)}, f32[2,64,128]{2,1,0:T(8,128)S(1)}, u32[]{:S(2)}, u32[]{:S(2)}) collective-permute-start(f32[2,64,128]{2,1,0:T(8,128)S(1)} %get-tuple-element.25), channel_id=1, source_target_pairs={{0,63},{1,2},{2,1},{3,4},{4,3},{5,6},{6,5},{7,8},{8,7},{9,10},{10,... | collective-permute-start | bytes 196616 | tf_op jit(solution)/shard_map/ppermute | solution.py:480
  50.5 12.8 %all-to-all-start = ((f32[32,1,128]{2,1,0:T(1,128)}), f32[32,1,128]{2,1,0:T(1,128)S(1)}, u32[]{:S(2)}, u32[]{:S(2)}) async-start(f32[32,1,128]{2,1,0:T(1,128)} %bitcast.14), calls=%async_computation | async-start | bytes 32768 | tf_op jit(solution)/shard_map/all_to_all | solution.py:484
  56.2 27.7 %collective-permute-start.7 = (f32[128,128]{1,0:T(8,128)S(1)}, f32[128,128]{1,0:T(8,128)S(1)}, u32[]{:S(2)}, u32[]{:S(2)}) collective-permute-start(f32[128,128]{1,0:T(8,128)S(1)} %get-tuple-element.28), channel_id=1, source_target_pairs={{0,1},{1,0},{2,3},{3,2},{4,5},{5,4},{6,7},{7,6},{8,9},{9,8},{10,11... | collective-permute-start | bytes 196616 | tf_op jit(solution)/shard_map/ppermute | solution.py:480
  58.5 25.4 %collective-permute-start.6 = (f32[128,128]{1,0:T(8,128)S(1)}, f32[128,128]{1,0:T(8,128)S(1)}, u32[]{:S(2)}, u32[]{:S(2)}) collective-permute-start(f32[128,128]{1,0:T(8,128)S(1)} %get-tuple-element.28), channel_id=1, source_target_pairs={{0,63},{1,2},{2,1},{3,4},{4,3},{5,6},{6,5},{7,8},{8,7},{9,10},{10,... | collective-permute-start | bytes 196616 | tf_op jit(solution)/shard_map/ppermute | solution.py:480
  63.9 19.9 %all-to-all-start.1 = ((f32[16,1,128]{2,1,0:T(1,128)}), f32[16,1,128]{2,1,0:T(1,128)S(1)}, u32[]{:S(2)}, u32[]{:S(2)}) async-start(f32[16,1,128]{2,1,0:T(1,128)} %bitcast.17), calls=%async_computation.1 | async-start | bytes 16384 | tf_op jit(solution)/shard_map/all_to_all | solution.py:484
  83.9 0.7 copy-start.2
  104.0 15.5 %all-to-all-start.3 = ((f32[16,16,128]{2,1,0:T(8,128)}), f32[16,16,128]{2,1,0:T(8,128)S(1)}, u32[]{:S(2)}, u32[]{:S(2)}) async-start(f32[16,16,128]{2,1,0:T(8,128)} %bitcast.26), calls=%async_computation.3 | async-start | bytes 262144 | tf_op jit(solution)/shard_map/all_to_all | solution.py:484
  107.5 5.9 %collective-permute-start.9 = (f32[2,32,128]{2,1,0:T(8,128)S(1)}, f32[2,32,128]{2,1,0:T(8,128)S(1)}, u32[]{:S(2)}, u32[]{:S(2)}) collective-permute-start(f32[2,32,128]{2,1,0:T(8,128)S(1)} %get-tuple-element.34), channel_id=1, source_target_pairs={{0,1},{1,0},{2,3},{3,2},{4,5},{5,4},{6,7},{7,6},{8,9},{9,8},{10,11... | collective-permute-start | bytes 98312 | tf_op jit(solution)/shard_map/ppermute | solution.py:480
  109.9 7.0 %collective-permute-start.8 = (f32[2,32,128]{2,1,0:T(8,128)S(1)}, f32[2,32,128]{2,1,0:T(8,128)S(1)}, u32[]{:S(2)}, u32[]{:S(2)}) collective-permute-start(f32[2,32,128]{2,1,0:T(8,128)S(1)} %get-tuple-element.34), channel_id=1, source_target_pairs={{0,63},{1,2},{2,1},{3,4},{4,3},{5,6},{6,5},{7,8},{8,7},{9,10},{10,... | collective-permute-start | bytes 98312 | tf_op jit(solution)/shard_map/ppermute | solution.py:480

commit v4 on v3

--- a/solution.py
+++ b/solution.py
@@ -19,9 +19,12 @@
 UP1 = 5
 UP2 = 3
 PAIRS = [(0, 4), (1, 5), (2, 6), (3, 7), (-3, 8), (-2, 9), (-1, 10)]
+SLABS = len(PAIRS) + 2
+OWN = 4
 WHERE = {row: (q, half) for q, pair in enumerate(PAIRS) for half, row in enumerate(pair)}
 FACE, TILE = ("x", "y_lo"), ("z", "y_hi", "core")
 PLANE = ("x", "y_lo", "y_hi", "core")
+FIRST, SECOND = ("z", "core"), ("x", "y_lo", "y_hi")
 bf16, f32 = jnp.bfloat16, jnp.float32
 
 
@@ -57,11 +60,23 @@
     return lax.dot_general(a, b, (((1,), (1,)), ((), ())), preferred_element_type=f32)
 
 
-def fine_turns(flags, count):
+class Place:
+    def __init__(self, flips=None):
+        self.face, self.tile = lax.axis_index(FACE), lax.axis_index(TILE)
+        self.odd_face, self.odd_tile = self.face % 2, self.tile % 2
+        self.flips = flips
+
+    def flags(self, side):
+        faces, tiles = self.flips.shape
+        face = (self.face + side) % faces
+        return [self.flips[face, (self.tile + step) % tiles] for step in (tiles - 1, 0, 1)]
+
+
+def fine_turns(place, count):
     lane = lanes(count)
     turns = []
     for side in range(2):
-        left, own, right = (flags[3 * side + n] for n in range(3))
+        left, own, right = place.flags(side)
         block = jnp.where(own == 1, 127 - lane, lane)
         strip = jnp.where(
             lane < 64,
@@ -72,11 +87,11 @@
     return turns
 
 
-def coarse_turns(flags, count):
+def coarse_turns(place, count):
     lane = lanes(count)
     turns = []
     for side in range(2):
-        left, own, right = (flags[3 * side + n] for n in range(3))
+        left, own, right = place.flags(side)
         index = jnp.where((lane < 64) & (own == 1), 63 - lane, lane)
         index = jnp.where((lane >= 64) & (lane < 64 + SLOT) & (right == 1), 127 + SLOT - lane, index)
         index = jnp.where((lane >= 128 - SLOT) & (left == 1), 255 - SLOT - lane, index)
@@ -145,13 +160,14 @@
     return -(-count // PER)
 
 
-def put_slots(out_ref, filled, count):
+def put_slots(out_refs, filled, count):
     lane = lanes(filled[0].shape[0])
     for group in range(groups(count)):
         value = filled[group * PER]
         for n in range(group * PER + 1, min(count, group * PER + PER)):
             value = jnp.where(lane // SLOT == n % PER, filled[n], value)
-        out_ref[group] = value
+        for out_ref in out_refs:
+            out_ref[group] = value
 
 
 def before(far, near, odd):
@@ -174,15 +190,16 @@
     return rows
 
 
-def rows_kernel(flags, maps_ref, own_ref, far_ref, near_ref, t_ref):
+def rows_kernel(maps_ref, own_ref, far_ref, near_ref, t_ref):
+    here = Place()
     t_ref[...] = maps_ref[...].astype(f32)
     rows = [t_ref[pl.ds(row, CI, stride=ROWS), :] for row in range(ROWS)]
     for row in range(ROWS):
         own_ref[row] = rows[row]
     for row in range(UP0):
         first, last = rows[row], rows[ROWS - UP0 + row]
-        far_ref[row] = before(first, last, flags[6])
-        near_ref[row] = after(first, last, flags[6])
+        far_ref[row] = before(first, last, here.odd_face)
+        near_ref[row] = after(first, last, here.odd_face)
 
 
 def both_strips(far_ref, near_ref, odd):
@@ -191,19 +208,20 @@
     return left, [after(far_ref[n], near_ref[n], odd) for n in range(count)]
 
 
-def ends_kernel(flags, far_ref, near_ref, own_ref, out_ref):
+def ends_kernel(far_ref, near_ref, own_ref, *out_refs):
     index = end_index(CI)
-    rows = fine_rows(far_ref, near_ref, own_ref, flags[6])
-    put_slots(out_ref, [pick(rows[row], index) for row in sorted(rows)], len(rows))
+    rows = fine_rows(far_ref, near_ref, own_ref, Place().odd_face)
+    put_slots(out_refs, [pick(rows[row], index) for row in sorted(rows)], len(rows))
 
 
 def fine_kernel(
-    flags, far_ref, near_ref, own_ref, far0_ref, near0_ref, w_ref,
-    x1_ref, sig_ref, terms_ref, ends_ref, t_ref,
+    flips, far_ref, near_ref, own_ref, far0_ref, near0_ref, w_ref,
+    x1_ref, sig_ref, terms_ref, ends_ref, ends_copy_ref, t_ref,
 ):
-    turns = fine_turns(flags, CI)
-    block = fine_rows(far_ref, near_ref, own_ref, flags[6])
-    left, right = both_strips(far0_ref, near0_ref, flags[7])
+    here = Place(flips)
+    turns = fine_turns(here, CI)
+    block = fine_rows(far_ref, near_ref, own_ref, here.odd_face)
+    left, right = both_strips(far0_ref, near0_ref, here.odd_tile)
     strip = {row: fine_strip(left, right, row + UP0) for row in block}
     first, first_strip = {}, {}
     for row in range(1 - UP0, ROWS + UP0 - 1):
@@ -211,13 +229,13 @@
     low, high = -2 * UP1, ROWS + 2 * UP1
     for row in range(low, high):
         second = 2.0 * fine_lap(first, first_strip, row, turns, False) - block[row]
-        here = pl.ds((row - low) * 128, 128)
+        at = pl.ds((row - low) * 128, 128)
         one, one_low = halves(first[row])
         two, two_low = halves(second)
         for n, part in enumerate((block[row].astype(bf16), one, two, one_low, two_low)):
-            t_ref[CI * n : CI * (n + 1), here] = part
+            t_ref[CI * n : CI * (n + 1), at] = part
         for n, part in enumerate((block[row].astype(bf16), one, two)):
-            t_ref[CI * (5 + n) : CI * (6 + n), here] = part
+            t_ref[CI * (5 + n) : CI * (6 + n), at] = part
     own = pl.ds(-low * 128, ROWS * 128)
     terms_ref[...] = t_ref[0 : 5 * CI, own]
     weights = weight_halves(w_ref, 5 * CI)
@@ -239,15 +257,16 @@
         both = 0.25 * (both + roll(both, -1))
         x1_ref[place] = pick(both, even)
         filled.append(pick(both, ends))
-    put_slots(ends_ref, filled, len(filled))
+    put_slots((ends_ref, ends_copy_ref), filled, len(filled))
 
 
 def coarse_kernel(
-    flags, x1_ref, far_ref, near_ref, w_ref, feat_ref, sig_ref, ends_ref, gram_ref, t_ref, s_ref
+    flips, x1_ref, far_ref, near_ref, w_ref, feat_ref, sig_ref, t_ref
 ):
-    turns = coarse_turns(flags, CA)
+    here = Place(flips)
+    turns = coarse_turns(here, CA)
     lane = lanes(CA)
-    left, right = both_strips(far_ref, near_ref, flags[7])
+    left, right = both_strips(far_ref, near_ref, here.odd_tile)
     rows = {}
     for row in range(-UP1, CROWS + UP1):
         place = row + UP1
@@ -260,20 +279,17 @@
         for row in range(-UP2, CROWS + UP2)
     }
     for q, (a, b) in enumerate(PAIRS):
-        here = pl.ds(q * 128, 128)
+        at = pl.ds(q * 128, 128)
         for k, term in enumerate((rows, first, second)):
             packed = jnp.where(lane < 64, term[a], roll(term[b], 64))
             high, low = halves(packed)
             for m in range(MAPS):
                 chans = slice(CH0 * m, CH0 * (m + 1))
-                t_ref[m, CH0 * k : CH0 * (k + 1), here] = high[chans]
-                t_ref[m, CH0 * (3 + k) : CH0 * (4 + k), here] = low[chans]
-                t_ref[m, CH0 * (6 + k) : CH0 * (7 + k), here] = high[chans]
+                t_ref[m, CH0 * k : CH0 * (k + 1), at] = high[chans]
+                t_ref[m, CH0 * (3 + k) : CH0 * (4 + k), at] = low[chans]
+                t_ref[m, CH0 * (6 + k) : CH0 * (7 + k), at] = high[chans]
     weights = weight_halves(w_ref, 2 * ORDER * CH0)
-    own = 4 * 128
-    j = lanes(CH1) % SLOT
-    column = jnp.where(j < STRIP, j, CCOLS - SLOT + j)
-    index = jnp.where(lanes(CH1) // SLOT % 2 == 0, column, 64 + column)
+    own = OWN * 128
     sums = []
     for m in range(MAPS):
         pre = dot(weights, t_ref[m])
@@ -281,22 +297,28 @@
         inverse = 1.0 / (1.0 + decay)
         sig = jnp.where(pre >= 0, inverse, decay * inverse)
         act = jnp.maximum(pre[:, :own], 0.0) + jnp.log(1.0 + decay[:, :own])
-        sums.append(sum(act[:, 128 * q : 128 * (q + 1)] for q in range(4)))
-        high, low = halves(sig[:, :own])
-        s_ref[CH1 * m : CH1 * (m + 1)] = high
-        s_ref[CB + CH1 * m : CB + CH1 * (m + 1)] = low
-        chans = slice(CH1 * m, CH1 * (m + 1))
-        ends = jnp.zeros((CH1, 128), f32)
+        sums.append(sum(act[:, 128 * q : 128 * (q + 1)] for q in range(OWN)))
         for q in range(len(PAIRS)):
-            value = sig[:, 128 * q : 128 * (q + 1)]
-            sig_ref[q, chans] = value
-            ends = jnp.where(lanes(CH1) // (2 * SLOT) == q, pick(value, index), ends)
-        ends_ref[chans] = ends
+            sig_ref[q, CH1 * m : CH1 * (m + 1)] = sig[:, 128 * q : 128 * (q + 1)]
     total = jnp.sum(jnp.concatenate(sums, axis=0).T, axis=0, keepdims=True)
     feat_ref[...] = jnp.broadcast_to(total, feat_ref.shape)
+
+
+def gram_kernel(sig_ref, t_ref, ends_ref, ends_copy_ref, gram_ref, s_ref):
+    j = lanes(CB) % SLOT
+    column = jnp.where(j < STRIP, j, CCOLS - SLOT + j)
+    index = jnp.where(lanes(CB) // SLOT % 2 == 0, column, 64 + column)
+    ends = jnp.zeros((CB, 128), f32)
+    for q in range(len(PAIRS)):
+        value = sig_ref[q]
+        ends = jnp.where(lanes(CB) // (2 * SLOT) == q, pick(value, index), ends)
+        if q < OWN:
+            s_ref[:CB, 128 * q : 128 * (q + 1)], s_ref[CB:, 128 * q : 128 * (q + 1)] = halves(value)
+    ends_ref[...] = ends
+    ends_copy_ref[...] = ends
     grams = [jnp.zeros((CH0, 128), f32) for _ in range(ORDER)]
     for m in range(MAPS):
-        both = dot_nt(t_ref[m, : 2 * ORDER * CH0, :own], s_ref[...])
+        both = dot_nt(t_ref[m, : 2 * ORDER * CH0, : OWN * 128], s_ref[...])
         for k in range(ORDER):
             high = both[CH0 * k : CH0 * (k + 1)]
             low = both[CH0 * (3 + k) : CH0 * (4 + k)]
@@ -306,24 +328,46 @@
         gram_ref[k] = grams[k]
 
 
+def split_kernel(
+    sig1_ref, far_ref, near_ref, shift_ref, labels_ref, out_ref, s_ref, head_ref
+):
+    here = Place()
+    for q in range(SLABS):
+        if q < len(PAIRS):
+            value = sig1_ref[q]
+        else:
+            value = (before, after)[q - len(PAIRS)](far_ref[...], near_ref[...], here.odd_tile)
+        high, low = halves(value)
+        at = pl.ds(q * 128, 128)
+        for m in range(MAPS):
+            chans = slice(CH1 * m, CH1 * (m + 1))
+            s_ref[m, :CH1, at] = high[chans]
+            s_ref[m, CH1 : 2 * CH1, at] = low[chans]
+            s_ref[m, 2 * CH1 :, at] = high[chans]
+    head_ref[0] = shift_ref[...]
+    head_ref[1] = labels_ref[...]
+    head_ref[2] = jnp.broadcast_to(out_ref[...], (8, 128))
+
+
 def back_kernel(
-    flags, feat_ref, shift_ref, labels_ref, fw_ref, out_ref, w1_ref, w0_ref,
-    sig1_ref, far_ref, near_ref, gram_ref, sig0_ref, terms_ref,
-    logits_ref, grads_ref, g_ref, ends_ref, s_ref, d_ref,
+    flips, feat_ref, head_ref, fw_ref, w1_ref, s_ref, gram_ref, sig0_ref, terms_ref,
+    logits_ref, grads_ref, d_ref,
     *, pooled,
 ):
+    here = Place(flips)
     features = jnp.sum(feat_ref[...], axis=0, keepdims=True) * (1.0 / pooled)
     row8 = lax.broadcasted_iota(jnp.int32, (8, 128), 0)
     spread = jnp.where(lanes(8) // CH1 == row8, jnp.broadcast_to(features, (8, 128)), 0.0)
     fw = fw_ref[...]
+    shift, labels, out = head_ref[0], head_ref[1], head_ref[2]
     hidden = jnp.tanh(
-        jnp.dot(spread, fw, precision=exact, preferred_element_type=f32) + shift_ref[...]
-    )
-    logits = jnp.sum(hidden * out_ref[...], axis=1, keepdims=True)
+        jnp.dot(spread, fw, precision=exact, preferred_element_type=f32) + shift
+    )
+    logits = jnp.sum(hidden * out, axis=1, keepdims=True)
     logits_ref[...] = jnp.broadcast_to(logits, (8, 128))
     decay = jnp.exp(-jnp.abs(logits))
-    dlogit = jnp.where(logits >= 0, 1.0, decay) / (1.0 + decay) - labels_ref[...]
-    dhidden = dlogit * out_ref[...] * (1.0 - hidden * hidden)
+    dlogit = jnp.where(logits >= 0, 1.0, decay) / (1.0 + decay) - labels
+    dhidden = dlogit * out * (1.0 - hidden * hidden)
     dhidden = jnp.concatenate(
         [jnp.broadcast_to(dhidden[m : m + 1], (CH1, 128)) for m in range(MAPS)], axis=0
     )
@@ -335,21 +379,15 @@
         value = gram_ref[k] * drow
         value = value + roll(value, 64)
         coarse.append(value + roll(value, 32))
-    slabs = len(PAIRS) + 2
-    for q in range(slabs):
-        if q < len(PAIRS):
-            value = sig1_ref[q]
-        else:
-            value = (before, after)[q - len(PAIRS)](far_ref[...], near_ref[...], flags[7])
-        high, low = halves(value * dfull)
-        here = pl.ds(q * 128, 128)
-        for m in range(MAPS):
-            chans = slice(CH1 * m, CH1 * (m + 1))
-            s_ref[m, :CH1, here] = high[chans]
-            s_ref[m, CH1 : 2 * CH1, here] = low[chans]
-            s_ref[m, 2 * CH1 :, here] = high[chans]
-    weights = weight_halves(w1_ref, 2 * CH1)
-    parts = [dot(weights, s_ref[m]) for m in range(MAPS)]
+    weighted = w1_ref[...] * jnp.broadcast_to(drow[:1], w1_ref.shape)
+    lane = lanes(w1_ref.shape[0])
+    parts = []
+    for m in range(MAPS):
+        weights = jnp.where(lane // CH1 == m, weighted, 0.0)
+        weights = weights + roll(weights, 64)
+        high, low = halves(weights + roll(weights, 32))
+        weights = jnp.where(lane < 2 * CH1, high.astype(f32), low.astype(f32)).astype(bf16)
+        parts.append(dot(weights[:, : 3 * CH1], s_ref[m]))
 
     def slab(k, q):
         return jnp.concatenate(
@@ -357,7 +395,7 @@
         )
 
     def spread_rows(k, low, high, strips):
-        left, right = (slab(k, slabs - 2), slab(k, slabs - 1)) if strips else (None, None)
+        left, right = (slab(k, SLABS - 2), slab(k, SLABS - 1)) if strips else (None, None)
         packed = [slab(k, q) for q in range(len(PAIRS))]
         rows = {}
         for row in range(low, high):
@@ -366,7 +404,7 @@
             rows[row] = coarse_row(value, left, right, 2 * q + half) if strips else value
         return rows
 
-    turns = coarse_turns(flags, CA)
+    turns = coarse_turns(here, CA)
     g0 = spread_rows(0, -1, CROWS + 1, False)
     g1 = spread_rows(1, 1 - UP2, CROWS + UP2 - 1, True)
     g2 = spread_rows(2, -UP2, CROWS + UP2, True)
@@ -377,10 +415,10 @@
         dx1 = 0.25 * pick(dx1, doubled)
         for n in (2 * (crow + 1), 2 * (crow + 1) + 1):
             high, low = halves(dx1 * sig0_ref[n])
-            here = pl.ds(n * 128, 128)
-            d_ref[:CA, here] = high
-            d_ref[CA : 2 * CA, here] = low
-            d_ref[2 * CA :, here] = high
+            at = pl.ds(n * 128, 128)
+            d_ref[:CA, at] = high
+            d_ref[CA : 2 * CA, at] = low
+            d_ref[2 * CA :, at] = high
     both = dot_nt(terms_ref[...], d_ref[: 2 * CA, 2 * 128 : (2 + ROWS) * 128])
     lane = lanes(CI)
     row16 = lax.broadcasted_iota(jnp.int32, (CI, 128), 0)
@@ -401,6 +439,9 @@
         value = jnp.where(lane // CH1 == k, coarse[k], value)
     for n in range(grads_ref.shape[0] // CI):
         grads_ref[CI * n : CI * (n + 1)] = value
+
+
+def terms_kernel(d_ref, w0_ref, g_ref, ends_ref, ends_copy_ref):
     weights = weight_halves(w0_ref, 2 * CA)
     index = end_index(2 * CI)
     filled = []
@@ -410,12 +451,13 @@
             part = value[:, 128 * step : 128 * (step + 1)]
             g_ref[n + step] = part
             filled.append(pick(part[CI:], index))
-    put_slots(ends_ref, filled, len(filled))
-
-
-def saliency_kernel(flags, g_ref, far_ref, near_ref, out_ref, *, pixels):
-    turns = fine_turns(flags, CI)
-    left, right = both_strips(far_ref, near_ref, flags[7])
+    put_slots((ends_ref, ends_copy_ref), filled, len(filled))
+
+
+def saliency_kernel(flips, g_ref, far_ref, near_ref, out_ref, *, pixels):
+    here = Place(flips)
+    turns = fine_turns(here, CI)
+    left, right = both_strips(far_ref, near_ref, here.odd_tile)
     g0, g1, g2, s1, s2 = {}, {}, {}, {}, {}
     for row in range(-2, ROWS + 2):
         value = g_ref[row + 2]
@@ -489,11 +531,6 @@
     fine_weight, coarse_weight, feature_weight, param_weight, out_weight,
 ):
     faces, tiles = lax.axis_size(FACE), lax.axis_size(TILE)
-    f, t = lax.axis_index(FACE), lax.axis_index(TILE)
-    columns = jnp.stack([(t + tiles - 1) % tiles, t, (t + 1) % tiles])
-    flags = jnp.concatenate(
-        [edge_flip[f][columns], edge_flip[(f + 1) % faces][columns], jnp.stack([f % 2, t % 2])]
-    )
     eye = jnp.eye(MAPS, dtype=f32)
     fine = jnp.einsum("kio,mn->monki", fine_weight, eye)
     fine = fine.transpose(0, 1, 3, 2, 4).reshape(CA, ORDER * CI)
@@ -501,7 +538,7 @@
     fine_backward = jnp.concatenate([fine.T] * 3, axis=1)
     coarse = coarse_weight.reshape(ORDER * CH0, CH1)
     coarse_forward = jnp.concatenate([coarse.T] * 3, axis=1)
-    coarse_backward = jnp.concatenate([coarse] * 3, axis=1)
+    coarse_backward = jnp.concatenate([coarse] * MAPS, axis=1)
     features4 = jnp.concatenate([feature_weight] * MAPS, axis=0)
     pad = [(0, 8 - MAPS), (0, 0)]
     shift = jnp.dot(jnp.pad(params, pad), param_weight, precision=exact)
@@ -509,71 +546,76 @@
 
     trade = shape(UP0, CI, COLS)
     own, far, near = call(
-        rows_kernel, (shape(ROWS, CI, COLS), trade, trade), flags, maps.reshape(CI * ROWS, COLS),
-        smem=1,
+        rows_kernel, (shape(ROWS, CI, COLS), trade, trade), maps.reshape(CI * ROWS, COLS),
         scratch=[pltpu.VMEM((CI * ROWS, COLS), f32)],
     )
     far, near = exchange(FACE, far, near)
-    ends0 = call(ends_kernel, shape(groups(ROWS + 2 * UP0), CI, 128), flags, far, near, own, smem=1)
-    far0, near0 = exchange(TILE, ends0, ends0)
+    trade = shape(groups(ROWS + 2 * UP0), CI, 128)
+    far0, near0 = call(ends_kernel, (trade, trade), far, near, own)
+    far0, near0 = exchange(TILE, far0, near0)
     crows = CROWS + 2 * UP1
-    x1, sig0, terms0, ends1 = call(
+    trade = shape(groups(crows), CA, 128)
+    x1, sig0, terms0, far1, near1 = call(
         fine_kernel,
         (
             shape(crows, CA, 128),
             shape(ROWS + 4, CA, 128),
             shape(5 * CI, ROWS * 128, dtype=bf16),
-            shape(groups(crows), CA, 128),
+            trade,
+            trade,
         ),
-        flags, far, near, own, far0, near0, fine_forward,
+        edge_flip, far, near, own, far0, near0, fine_forward,
         smem=1,
         scratch=[pltpu.VMEM((8 * CI, 2 * crows * 128), bf16)],
     )
-    far1, near1 = exchange(TILE, ends1, ends1)
-    feats, sig1, ends2, grams = call(
+    far1, near1 = exchange(TILE, far1, near1)
+    feats, sig1, terms1 = call(
         coarse_kernel,
         (
-            shape(lax.axis_size(PLANE), CB),
+            shape(lax.axis_size(FIRST), CB),
             shape(len(PAIRS), CB, 128),
-            shape(CB, 128),
-            shape(ORDER, CH0, 128),
+            shape(MAPS, 3 * ORDER * CH0, len(PAIRS) * 128, dtype=bf16),
         ),
-        flags, x1, far1, near1, coarse_forward,
+        edge_flip, x1, far1, near1, coarse_forward,
         smem=1,
-        scratch=[
-            pltpu.VMEM((MAPS, 3 * ORDER * CH0, len(PAIRS) * 128), bf16),
-            pltpu.VMEM((2 * CB, 4 * 128), bf16),
-        ],
-    )
-    far2, near2 = exchange(TILE, ends2, ends2)
-    feats = share(feats, PLANE)
-    feats = call(row_again_kernel, shape(lax.axis_size("z"), CB), feats)
-    feats = share(feats, "z")
+    )
+    feats = share(feats, FIRST)
+    feats = call(row_again_kernel, shape(lax.axis_size(SECOND), CB), feats)
+    trade = shape(CB, 128)
+    far2, near2, grams = call(
+        gram_kernel, (trade, trade, shape(ORDER, CH0, 128)), sig1, terms1,
+        scratch=[pltpu.VMEM((2 * CB, OWN * 128), bf16)],
+    )
+    feats = share(feats, SECOND)
+    far2, near2 = exchange(TILE, far2, near2)
     pooled = CROWS * faces * CCOLS * tiles
-    logits, grads, g, ends3 = call(
+    split1, head = call(
+        split_kernel,
+        (shape(MAPS, 3 * CH1, SLABS * 128, dtype=bf16), shape(3, 8, 128)),
+        sig1, far2, near2, shift, labels8, out_weight[None],
+    )
+    logits, grads, dpre0 = call(
         lambda *refs: back_kernel(*refs, pooled=pooled),
         (
             shape(8, 128),
             shape(lax.axis_size(PLANE) * CI, 128),
-            shape(ROWS + 4, ORDER * CI, 128),
-            shape(groups(ROWS + 4), 2 * CI, 128),
+            shape(3 * CA, (ROWS + 4) * 128, dtype=bf16),
         ),
-        flags, feats, shift, labels8, features4, out_weight[None],
-        coarse_backward, fine_backward, sig1, far2, near2, grams, sig0, terms0,
+        edge_flip, feats, head, features4, coarse_backward, split1, grams, sig0, terms0,
         smem=1,
-        scratch=[
-            pltpu.VMEM((MAPS, 3 * CH1, (len(PAIRS) + 2) * 128), bf16),
-            pltpu.VMEM((3 * CA, (ROWS + 4) * 128), bf16),
-        ],
-    )
-    far3, near3 = exchange(TILE, ends3, ends3)
+    )
     grads = share(grads, PLANE)
+    trade = shape(groups(ROWS + 4), 2 * CI, 128)
+    g, far3, near3 = call(
+        terms_kernel, (shape(ROWS + 4, ORDER * CI, 128), trade, trade), dpre0, fine_backward
+    )
+    far3, near3 = exchange(TILE, far3, near3)
     grads = call(again_kernel, shape(lax.axis_size("z") * CI, 128), grads)
     grads = share(grads, "z")
     pixels = float(ROWS * faces * COLS * tiles)
     saliency = call(
         lambda *refs: saliency_kernel(*refs, pixels=pixels),
-        shape(CI * ROWS, COLS), flags, g, far3, near3,
+        shape(CI * ROWS, COLS), edge_flip, g, far3, near3,
         smem=1,
     )
     grad_f, grad_c = call(

time: 122 us -> 116 us (0.951)
  waiting for transfers between devices: 26 us -> 14.4 us
  starting transfers between devices: 56.8 us -> 64.7 us
  blocking collectives: 15.6 us -> 14 us
    ppermute x5, waiting for transfers between devices: 12.3 us -> 0.01 us  [exchange(): lax.ppermute(far_value, axis, far)]
    ppermute x5, starting transfers between devices: 21.1 us -> 24.8 us  [exchange(): lax.ppermute(near_value, axis, near)]
    ppermute x5, starting transfers between devices: 17.9 us -> 20.1 us  [exchange(): lax.ppermute(far_value, axis, far)]
    all_to_all x3, starting transfers between devices: 17.8 us -> 19.8 us  [share(): return lax.all_to_all(rows, axes, 0, 0, tiled=True)]
    all_to_all x1, blocking collectives: 15.6 us -> 14 us  [share(): return lax.all_to_all(rows, axes, 0, 0, tiled=True)]
    unnamed x16 -> x18, local copies, waits for them, and re-layouts: 2.78 us -> 4.1 us
    gather x2 -> x0, local copies, waits for them, and re-layouts: 1.28 us -> none  [the longest x1 0.64 us: on_device(): edge_flip[f][columns]]
    pallas_call x9 -> x12, Pallas kernels: 14.3 us -> 14.2 us  [call(): pl.pallas_call(kernel, out_shape=outs, in_specs=in_specs, out_specs=jax.t...]
  transfers between devices with their start and end apart: 13 -> 13, of which waited for: 6 -> 6; matrix products, arithmetic and copies ran while one was open for 1% -> 1% of each run, Pallas kernels for 2% -> 3%
where the time goes in v4:
time: 116 us; the launch traced here: 114 us
  starting transfers between devices  64.7 us (56%)
  waiting for transfers between devices  14.4 us (12%)
  Pallas kernels  14.2 us (12%)
  blocking collectives  14 us (12%)
  local copies, waits for them, and re-layouts  5.04 us (4%)
    ppermute x5, starting transfers between devices, exchange(): lax.ppermute(near_value, axis, near)  24.8 us
    ppermute x5, starting transfers between devices, exchange(): lax.ppermute(far_value, axis, far)  20.1 us
    all_to_all x3, starting transfers between devices, share(): return lax.all_to_all(rows, axes, 0, 0, tiled=True)  19.8 us
    pallas_call x12, Pallas kernels, call(): pl.pallas_call(kernel, out_shape=outs, in_specs=in_specs, out_specs=jax.t...  14.2 us
    all_to_all x1, blocking collectives, share(): return lax.all_to_all(rows, axes, 0, 0, tiled=True)  14 us
    all_to_all x3, waiting for transfers between devices, share(): return lax.all_to_all(rows, axes, 0, 0, tiled=True)  11.7 us
    unnamed x18, local copies, waits for them, and re-layouts  4.1 us
    ppermute x5, waiting for transfers between devices, exchange(): lax.ppermute(near_value, axis, near)  2.64 us
  transfers between devices with their start and end apart: 13, of which 6 were waited for; matrix products, arithmetic and copies ran while one was open for 1% of the time, Pallas kernels for 3%

profile of v4, /device:TPU:1, one launch (start us, length us, event | category | flops | bytes accessed | tf_op | source)
XLA Modules:
  0.0 113.8 jit_solution(10989087608740650099)
XLA Ops:
  0.7 0.8 copy-done.2
  1.5 0.1 shard_map.120
  1.6 6.2 %collective-permute-start = (f32[12,16,128]{2,1,0:T(8,128)S(1)}, f32[12,16,128]{2,1,0:T(8,128)S(1)}, u32[]{:S(2)}, u32[]{:S(2)}) collective-permute-start(f32[12,16,128]{2,1,0:T(8,128)S(1)} %get-tuple-element.30), channel_id=1, source_target_pairs={{0,448},{64,128},{128,64},{192,256},{256,192},{320,384},{384,320},... | collective-permute-start | bytes 294920 | tf_op jit(solution)/shard_map/ppermute | solution.py:522
  7.8 1.9 %collective-permute-start.1 = (f32[12,16,128]{2,1,0:T(8,128)S(1)}, f32[12,16,128]{2,1,0:T(8,128)S(1)}, u32[]{:S(2)}, u32[]{:S(2)}) collective-permute-start(f32[12,16,128]{2,1,0:T(8,128)S(1)} %get-tuple-element.31), channel_id=1, source_target_pairs={{0,64},{64,0},{128,192},{192,128},{256,320},{320,256},{384,448},{4... | collective-permute-start | bytes 294920 | tf_op jit(solution)/shard_map/ppermute | solution.py:522
  9.7 0.1 multiply_bitcast_fusion
  9.8 0.1 reshape.29
  10.0 0.6 copy-done.8
  10.6 0.7 copy-done.7
  11.3 0.2 fusion.1.shift_ref
  11.5 1.7 %collective-permute-done.1.near_ref = f32[12,16,128]{2,1,0:T(8,128)S(1)} collective-permute-done((f32[12,16,128]{2,1,0:T(8,128)S(1)}, f32[12,16,128]{2,1,0:T(8,128)S(1)}, u32[]{:S(2)}, u32[]{:S(2)}) %collective-permute-start.1) | collective-permute-done | bytes 98336 | tf_op jit(solution)/shard_map/ppermute | solution.py:522
  13.2 0.2 shard_map.121
  13.3 6.5 %collective-permute-start.2 = (f32[3,16,128]{2,1,0:T(8,128)S(1)}, f32[3,16,128]{2,1,0:T(8,128)S(1)}, u32[]{:S(2)}, u32[]{:S(2)}) collective-permute-start(f32[3,16,128]{2,1,0:T(8,128)S(1)} %get-tuple-element.33), channel_id=1, source_target_pairs={{0,63},{1,2},{2,1},{3,4},{4,3},{5,6},{6,5},{7,8},{8,7},{9,10},{10,... | collective-permute-start | bytes 73736 | tf_op jit(solution)/shard_map/ppermute | solution.py:522
  19.9 9.2 %collective-permute-start.3 = (f32[3,16,128]{2,1,0:T(8,128)S(1)}, f32[3,16,128]{2,1,0:T(8,128)S(1)}, u32[]{:S(2)}, u32[]{:S(2)}) collective-permute-start(f32[3,16,128]{2,1,0:T(8,128)S(1)} %get-tuple-element.34), channel_id=1, source_target_pairs={{0,1},{1,0},{2,3},{3,2},{4,5},{5,4},{6,7},{7,6},{8,9},{9,8},{10,11... | collective-permute-start | bytes 73736 | tf_op jit(solution)/shard_map/ppermute | solution.py:522
  29.1 0.1 copy.17.w_ref
  29.2 0.7 copy-done.4
  29.9 0.1 copy.18
  30.0 0.6 copy-done.1
  30.6 3.3 %shard_map.122 = (f32[18,64,128]{2,1,0:T(8,128)S(1)}, f32[20,64,128]{2,1,0:T(8,128)S(1)}, bf16[80,2048]{1,0:T(8,128)(2,1)S(1)}, f32[2,64,128]{2,1,0:T(8,128)S(1)}, f32[2,64,128]{2,1,0:T(8,128)S(1)}) custom-call(s32[8,64]{1,0:T(8,128)S(1)} %copy-done.1, f32[12,16,128]{2,1,0:T(8,128)S(1)} %collective-permute-done.far_ref, ...), custom_call_target="tpu_custom_call" | custom-call | tf_op jit(solution)/shard_map/pallas_call | solution.py:504
  33.9 1.9 %collective-permute-start.4 = (f32[2,64,128]{2,1,0:T(8,128)S(1)}, f32[2,64,128]{2,1,0:T(8,128)S(1)}, u32[]{:S(2)}, u32[]{:S(2)}) collective-permute-start(f32[2,64,128]{2,1,0:T(8,128)S(1)} %get-tuple-element.36), channel_id=1, source_target_pairs={{0,63},{1,2},{2,1},{3,4},{4,3},{5,6},{6,5},{7,8},{8,7},{9,10},{10,... | collective-permute-start | bytes 196616 | tf_op jit(solution)/shard_map/ppermute | solution.py:522
  35.8 5.4 %collective-permute-start.5 = (f32[2,64,128]{2,1,0:T(8,128)S(1)}, f32[2,64,128]{2,1,0:T(8,128)S(1)}, u32[]{:S(2)}, u32[]{:S(2)}) collective-permute-start(f32[2,64,128]{2,1,0:T(8,128)S(1)} %get-tuple-element.37), channel_id=1, source_target_pairs={{0,1},{1,0},{2,3},{3,2},{4,5},{5,4},{6,7},{7,6},{8,9},{9,8},{10,11... | collective-permute-start | bytes 196616 | tf_op jit(solution)/shard_map/ppermute | solution.py:522
  41.2 0.1 pad_maximum_fusion.3.w_ref
  41.3 0.8 collective-permute-done.5.near_ref
  42.1 2.7 %shard_map.123 = (f32[32,128]{1,0:T(8,128)}, f32[7,128,128]{2,1,0:T(8,128)S(1)}, bf16[4,144,896]{2,1,0:T(8,128)(2,1)S(1)}) custom-call(s32[8,64]{1,0:T(8,128)S(1)} %copy-done.1, f32[18,64,128]{2,1,0:T(8,128)S(1)} %get-tuple-element.35.x1_ref, f32[2,64,128]{2,1,0:T(8,128)S(1)} %collective-permute-done.4.far_ref, ...), custom_call_target="tpu_custom_call" | custom-call | tf_op jit(solution)/shard_map/pallas_call | solution.py:504
  44.8 9.9 %all-to-all-start = ((f32[32,1,128]{2,1,0:T(1,128)}), f32[32,1,128]{2,1,0:T(1,128)S(1)}, u32[]{:S(2)}, u32[]{:S(2)}) async-start(f32[32,1,128]{2,1,0:T(1,128)} %bitcast.6), calls=%async_computation | async-start | bytes 32768 | tf_op jit(solution)/shard_map/all_to_all | solution.py:526
  54.7 0.1 pad_maximum_fusion.4.refs_4_
  54.8 0.5 shard_map.125
  55.3 1.9 %collective-permute-start.6 = (f32[128,128]{1,0:T(8,128)S(1)}, f32[128,128]{1,0:T(8,128)S(1)}, u32[]{:S(2)}, u32[]{:S(2)}) collective-permute-start(f32[128,128]{1,0:T(8,128)S(1)} %get-tuple-element.41), channel_id=1, source_target_pairs={{0,63},{1,2},{2,1},{3,4},{4,3},{5,6},{6,5},{7,8},{8,7},{9,10},{10,... | collective-permute-start | bytes 196616 | tf_op jit(solution)/shard_map/ppermute | solution.py:522
  57.2 4.2 %collective-permute-start.7 = (f32[128,128]{1,0:T(8,128)S(1)}, f32[128,128]{1,0:T(8,128)S(1)}, u32[]{:S(2)}, u32[]{:S(2)}) collective-permute-start(f32[128,128]{1,0:T(8,128)S(1)} %get-tuple-element.42), channel_id=1, source_target_pairs={{0,1},{1,0},{2,3},{3,2},{4,5},{5,4},{6,7},{7,6},{8,9},{9,8},{10,11... | collective-permute-start | bytes 196616 | tf_op jit(solution)/shard_map/ppermute | solution.py:522
  61.4 5.0 %all-to-all-done = f32[32,1,128]{2,1,0:T(1,128)S(1)} async-done(((f32[32,1,128]{2,1,0:T(1,128)}), f32[32,1,128]{2,1,0:T(1,128)S(1)}, u32[]{:S(2)}, u32[]{:S(2)}) %all-to-all-start) | async-done | bytes 16416 | tf_op jit(solution)/shard_map/all_to_all | solution.py:526
  66.5 0.6 shard_map.124
  67.1 3.5 %all-to-all-start.1 = ((f32[16,1,128]{2,1,0:T(1,128)}), f32[16,1,128]{2,1,0:T(1,128)S(1)}, u32[]{:S(2)}, u32[]{:S(2)}) async-start(f32[16,1,128]{2,1,0:T(1,128)} %bitcast.9), calls=%async_computation.1 | async-start | bytes 16384 | tf_op jit(solution)/shard_map/all_to_all | solution.py:526
  70.6 0.1 broadcast_in_dim.15.labels_ref
  70.6 0.7 copy-done.3
  71.3 0.1 shard_map.126
  71.4 5.4 %all-to-all-done.1 = f32[16,1,128]{2,1,0:T(1,128)S(1)} async-done(((f32[16,1,128]{2,1,0:T(1,128)}), f32[16,1,128]{2,1,0:T(1,128)S(1)}, u32[]{:S(2)}, u32[]{:S(2)}) %all-to-all-start.1) | async-done | bytes 8224 | tf_op jit(solution)/shard_map/all_to_all | solution.py:526
  76.8 3.1 %shard_map.127 = (f32[8,128]{1,0:T(8,128)S(1)}, f32[512,128]{1,0:T(8,128)S(1)}, bf16[192,2560]{1,0:T(8,128)(2,1)S(1)}) custom-call(s32[8,64]{1,0:T(8,128)S(1)} %copy-done.1, f32[16,128]{1,0:T(8,128)S(1)} %bitcast.33, f32[3,8,128]{2,1,0:T(8,128)S(1)} %get-tuple-element.43.refs_2_, f32[128,128]{1,0:T(8,128)S(1)} %pad_maximum_fusion.1.refs_3_, ...), custom_call_target="tpu_custom_call" | custom-call | tf_op jit(solution)/shard_map/pallas_call | solution.py:504
  79.9 14.0 %all_to_all.44 = f32[32,16,128]{2,1,0:T(8,128)S(1)} all-to-all(f32[32,16,128]{2,1,0:T(8,128)S(1)} %bitcast.30), channel_id=1, replica_groups=mesh['x'=4,'y_lo'=2,'z'=16,'y_hi'=2,'core'=2] {'x','y_lo','y_hi','core'}, dimensions={0} | all-to-all | bytes 524288 | tf_op jit(solution)/shard_map/all_to_all | solution.py:526
  93.9 0.7 shard_map.130
  94.6 6.4 %all-to-all-start.3 = ((f32[16,16,128]{2,1,0:T(8,128)}), f32[16,16,128]{2,1,0:T(8,128)S(1)}, u32[]{:S(2)}, u32[]{:S(2)}) async-start(f32[16,16,128]{2,1,0:T(8,128)} %bitcast.18), calls=%async_computation.3 | async-start | bytes 262144 | tf_op jit(solution)/shard_map/all_to_all | solution.py:526
  101.0 0.1 pad_maximum_fusion.2.w0_ref
  101.1 0.4 shard_map.128
  101.5 3.5 %collective-permute-start.8 = (f32[2,32,128]{2,1,0:T(8,128)S(1)}, f32[2,32,128]{2,1,0:T(8,128)S(1)}, u32[]{:S(2)}, u32[]{:S(2)}) collective-permute-start(f32[2,32,128]{2,1,0:T(8,128)S(1)} %get-tuple-element.51), channel_id=1, source_target_pairs={{0,63},{1,2},{2,1},{3,4},{4,3},{5,6},{6,5},{7,8},{8,7},{9,10},{10,... | collective-permute-start | bytes 98312 | tf_op jit(solution)/shard_map/ppermute | solution.py:522
  105.0 4.1 %collective-permute-start.9 = (f32[2,32,128]{2,1,0:T(8,128)S(1)}, f32[2,32,128]{2,1,0:T(8,128)S(1)}, u32[]{:S(2)}, u32[]{:S(2)}) collective-permute-start(f32[2,32,128]{2,1,0:T(8,128)S(1)} %get-tuple-element.52), channel_id=1, source_target_pairs={{0,1},{1,0},{2,3},{3,2},{4,5},{5,4},{6,7},{7,6},{8,9},{9,8},{10,11... | collective-permute-start | bytes 98312 | tf_op jit(solution)/shard_map/ppermute | solution.py:522
  109.1 0.6 slice_reduce_fusion
  109.7 0.2 collective-permute-done.9.refs_3_
  109.9 1.9 %shard_map.129 = f32[256,128]{1,0:T(8,128)} custom-call(s32[8,64]{1,0:T(8,128)S(1)} %copy-done.1, f32[20,48,128]{2,1,0:T(8,128)S(1)} %get-tuple-element.50.refs_1_, f32[2,32,128]{2,1,0:T(8,128)S(1)} %collective-permute-done.8.refs_2_, f32[2,32,128]{2,1,0:T(8,128)S(1)} %collective-permute-done.9.refs_3_), custom_call_target="tpu_custom_call" | custom-call | tf_op jit(solution)/shard_map/pallas_call | solution.py:504
  111.8 1.3 %all-to-all-done.3 = f32[16,16,128]{2,1,0:T(8,128)S(1)} async-done(((f32[16,16,128]{2,1,0:T(8,128)}), f32[16,16,128]{2,1,0:T(8,128)S(1)}, u32[]{:S(2)}, u32[]{:S(2)}) %all-to-all-start.3) | async-done | bytes 131104 | tf_op jit(solution)/shard_map/all_to_all | solution.py:526
  113.1 0.7 shard_map.131
  (25 shorter events, 0.1 us)
Async XLA Ops:
  0.6 10.0 %copy-start = (f32[2,128]{1,0:T(2,128)S(1)}, f32[2,128]{1,0:T(2,128)}, u32[]{:S(2)}) copy-start(f32[2,128]{1,0:T(2,128)} %param.16) | copy-start | bytes 3076
  0.6 0.8 copy-start.2
  1.5 8.2 %copy-start.6 = (f32[3,4,16]{2,1,0:T(4,128)S(1)}, f32[3,4,16]{2,1,0:T(4,128)}, u32[]{:S(2)}) copy-start(f32[3,4,16]{2,1,0:T(4,128)} %param.13) | copy-start | bytes 2308
  1.6 9.9 %collective-permute-start = (f32[12,16,128]{2,1,0:T(8,128)S(1)}, f32[12,16,128]{2,1,0:T(8,128)S(1)}, u32[]{:S(2)}, u32[]{:S(2)}) collective-permute-start(f32[12,16,128]{2,1,0:T(8,128)S(1)} %get-tuple-element.30), channel_id=1, source_target_pairs={{0,448},{64,128},{128,64},{192,256},{256,192},{320,384},{384,320},... | collective-permute-start | bytes 294920 | tf_op jit(solution)/shard_map/ppermute | solution.py:522
  7.8 5.4 %collective-permute-start.1 = (f32[12,16,128]{2,1,0:T(8,128)S(1)}, f32[12,16,128]{2,1,0:T(8,128)S(1)}, u32[]{:S(2)}, u32[]{:S(2)}) collective-permute-start(f32[12,16,128]{2,1,0:T(8,128)S(1)} %get-tuple-element.31), channel_id=1, source_target_pairs={{0,64},{64,0},{128,192},{192,128},{256,320},{320,256},{384,448},{4... | collective-permute-start | bytes 294920 | tf_op jit(solution)/shard_map/ppermute | solution.py:522
  9.9 0.7 copy-start.8
  10.6 0.7 copy-start.7
  13.2 15.9 %copy-start.5 = (f32[32,128]{1,0:T(8,128)S(1)}, f32[32,128]{1,0:T(8,128)}, u32[]{:S(2)}) copy-start(f32[32,128]{1,0:T(8,128)} %param.15) | copy-start | bytes 49156
  13.3 16.6 %collective-permute-start.2 = (f32[3,16,128]{2,1,0:T(8,128)S(1)}, f32[3,16,128]{2,1,0:T(8,128)S(1)}, u32[]{:S(2)}, u32[]{:S(2)}) collective-permute-start(f32[3,16,128]{2,1,0:T(8,128)S(1)} %get-tuple-element.33), channel_id=1, source_target_pairs={{0,63},{1,2},{2,1},{3,4},{4,3},{5,6},{6,5},{7,8},{8,7},{9,10},{10,... | collective-permute-start | bytes 73736 | tf_op jit(solution)/shard_map/ppermute | solution.py:522
  19.9 10.1 %collective-permute-start.3 = (f32[3,16,128]{2,1,0:T(8,128)S(1)}, f32[3,16,128]{2,1,0:T(8,128)S(1)}, u32[]{:S(2)}, u32[]{:S(2)}) collective-permute-start(f32[3,16,128]{2,1,0:T(8,128)S(1)} %get-tuple-element.34), channel_id=1, source_target_pairs={{0,1},{1,0},{2,3},{3,2},{4,5},{5,4},{6,7},{7,6},{8,9},{9,8},{10,11... | collective-permute-start | bytes 73736 | tf_op jit(solution)/shard_map/ppermute | solution.py:522
  29.1 0.7 copy-start.4
  29.9 0.7 copy-start.1
  33.9 7.4 %collective-permute-start.4 = (f32[2,64,128]{2,1,0:T(8,128)S(1)}, f32[2,64,128]{2,1,0:T(8,128)S(1)}, u32[]{:S(2)}, u32[]{:S(2)}) collective-permute-start(f32[2,64,128]{2,1,0:T(8,128)S(1)} %get-tuple-element.36), channel_id=1, source_target_pairs={{0,63},{1,2},{2,1},{3,4},{4,3},{5,6},{6,5},{7,8},{8,7},{9,10},{10,... | collective-permute-start | bytes 196616 | tf_op jit(solution)/shard_map/ppermute | solution.py:522
  35.8 6.3 %collective-permute-start.5 = (f32[2,64,128]{2,1,0:T(8,128)S(1)}, f32[2,64,128]{2,1,0:T(8,128)S(1)}, u32[]{:S(2)}, u32[]{:S(2)}) collective-permute-start(f32[2,64,128]{2,1,0:T(8,128)S(1)} %get-tuple-element.37), channel_id=1, source_target_pairs={{0,1},{1,0},{2,3},{3,2},{4,5},{5,4},{6,7},{7,6},{8,9},{9,8},{10,11... | collective-permute-start | bytes 196616 | tf_op jit(solution)/shard_map/ppermute | solution.py:522
  44.8 21.6 %all-to-all-start = ((f32[32,1,128]{2,1,0:T(1,128)}), f32[32,1,128]{2,1,0:T(1,128)S(1)}, u32[]{:S(2)}, u32[]{:S(2)}) async-start(f32[32,1,128]{2,1,0:T(1,128)} %bitcast.6), calls=%async_computation | async-start | bytes 32768 | tf_op jit(solution)/shard_map/all_to_all | solution.py:526
  55.3 15.3 %collective-permute-start.6 = (f32[128,128]{1,0:T(8,128)S(1)}, f32[128,128]{1,0:T(8,128)S(1)}, u32[]{:S(2)}, u32[]{:S(2)}) collective-permute-start(f32[128,128]{1,0:T(8,128)S(1)} %get-tuple-element.41), channel_id=1, source_target_pairs={{0,63},{1,2},{2,1},{3,4},{4,3},{5,6},{6,5},{7,8},{8,7},{9,10},{10,... | collective-permute-start | bytes 196616 | tf_op jit(solution)/shard_map/ppermute | solution.py:522
  57.2 13.3 %collective-permute-start.7 = (f32[128,128]{1,0:T(8,128)S(1)}, f32[128,128]{1,0:T(8,128)S(1)}, u32[]{:S(2)}, u32[]{:S(2)}) collective-permute-start(f32[128,128]{1,0:T(8,128)S(1)} %get-tuple-element.42), channel_id=1, source_target_pairs={{0,1},{1,0},{2,3},{3,2},{4,5},{5,4},{6,7},{7,6},{8,9},{9,8},{10,11... | collective-permute-start | bytes 196616 | tf_op jit(solution)/shard_map/ppermute | solution.py:522
  67.1 9.8 %all-to-all-start.1 = ((f32[16,1,128]{2,1,0:T(1,128)}), f32[16,1,128]{2,1,0:T(1,128)S(1)}, u32[]{:S(2)}, u32[]{:S(2)}) async-start(f32[16,1,128]{2,1,0:T(1,128)} %bitcast.9), calls=%async_computation.1 | async-start | bytes 16384 | tf_op jit(solution)/shard_map/all_to_all | solution.py:526
  70.6 0.7 copy-start.3
  94.6 18.5 %all-to-all-start.3 = ((f32[16,16,128]{2,1,0:T(8,128)}), f32[16,16,128]{2,1,0:T(8,128)S(1)}, u32[]{:S(2)}, u32[]{:S(2)}) async-start(f32[16,16,128]{2,1,0:T(8,128)} %bitcast.18), calls=%async_computation.3 | async-start | bytes 262144 | tf_op jit(solution)/shard_map/all_to_all | solution.py:526
  101.5 8.2 %collective-permute-start.8 = (f32[2,32,128]{2,1,0:T(8,128)S(1)}, f32[2,32,128]{2,1,0:T(8,128)S(1)}, u32[]{:S(2)}, u32[]{:S(2)}) collective-permute-start(f32[2,32,128]{2,1,0:T(8,128)S(1)} %get-tuple-element.51), channel_id=1, source_target_pairs={{0,63},{1,2},{2,1},{3,4},{4,3},{5,6},{6,5},{7,8},{8,7},{9,10},{10,... | collective-permute-start | bytes 98312 | tf_op jit(solution)/shard_map/ppermute | solution.py:522
  105.0 5.0 %collective-permute-start.9 = (f32[2,32,128]{2,1,0:T(8,128)S(1)}, f32[2,32,128]{2,1,0:T(8,128)S(1)}, u32[]{:S(2)}, u32[]{:S(2)}) collective-permute-start(f32[2,32,128]{2,1,0:T(8,128)S(1)} %get-tuple-element.52), channel_id=1, source_target_pairs={{0,1},{1,0},{2,3},{3,2},{4,5},{5,4},{6,7},{7,6},{8,9},{9,8},{10,11... | collective-permute-start | bytes 98312 | tf_op jit(solution)/shard_map/ppermute | solution.py:522

commit v5 on v4

--- a/solution.py
+++ b/solution.py
@@ -12,14 +12,13 @@
 CI = MAPS * BINS
 CA = MAPS * CH0
 CB = MAPS * CH1
-STRIP = 4
+STRIP = 2
 SLOT = 2 * STRIP
 PER = 128 // SLOT
 UP0 = 12
 UP1 = 5
 UP2 = 3
 PAIRS = [(0, 4), (1, 5), (2, 6), (3, 7), (-3, 8), (-2, 9), (-1, 10)]
-SLABS = len(PAIRS) + 2
 OWN = 4
 WHERE = {row: (q, half) for q, pair in enumerate(PAIRS) for half, row in enumerate(pair)}
 FACE, TILE = ("x", "y_lo"), ("z", "y_hi", "core")
@@ -129,10 +128,31 @@
     return out, -0.25 * (vertical(strip, row, ROWS, top_strip, bottom_strip) + side)
 
 
-def coarse_lap(rows, row, turns):
-    value = rows[row]
-    side = roll(value, 1) + roll(value, -1)
-    return -0.25 * (vertical(rows, row, CROWS, turns[0], turns[1]) + side)
+def coarse_laps(rows, low, high, turns, around, ref):
+    count = rows[low].shape[0]
+    for n, row in enumerate(range(low, high)):
+        side_by_side(ref, slice(count * n, count * (n + 1)), rows[row])
+    sides = dot(ref[0 : count * (high - low)], around)
+    return {
+        row: sides[count * n : count * (n + 1)] - 0.25 * vertical(rows, row, CROWS, *turns)
+        for n, row in enumerate(range(low, high))
+    }
+
+
+def grid(rows, columns):
+    return (lax.broadcasted_iota(jnp.int32, (rows, columns), axis) for axis in range(2))
+
+
+def ring(length, copies=1):
+    i, j = grid(length * copies, length)
+    step = (i - j + length) % length
+    return jnp.where((step == 1) | (step == length - 1), -0.25, 0.0).astype(bf16)
+
+
+def side_by_side(ref, at, value):
+    high, low = halves(value)
+    width = value.shape[1]
+    ref[at, :width], ref[at, width:] = high, low
 
 
 def end_index(count, stride=1, width=COLS):
@@ -216,33 +236,42 @@
 
 def fine_kernel(
     flips, far_ref, near_ref, own_ref, far0_ref, near0_ref, w_ref,
-    x1_ref, sig_ref, terms_ref, ends_ref, ends_copy_ref, t_ref,
+    x1_ref, sig_ref, terms_ref, ends_ref, ends_copy_ref, t_ref, x_ref, y_ref, a_ref,
 ):
     here = Place(flips)
     turns = fine_turns(here, CI)
     block = fine_rows(far_ref, near_ref, own_ref, here.odd_face)
     left, right = both_strips(far0_ref, near0_ref, here.odd_tile)
     strip = {row: fine_strip(left, right, row + UP0) for row in block}
-    first, first_strip = {}, {}
-    for row in range(1 - UP0, ROWS + UP0 - 1):
-        first[row], first_strip[row] = fine_lap(block, strip, row, turns, True)
+    around = ring(256)
+    for n, row in enumerate(sorted(block)):
+        x_ref[CI * n : CI * (n + 1), :128] = block[row].astype(bf16)
+        x_ref[CI * n : CI * (n + 1), 128:] = strip[row].astype(bf16)
+    sides = dot(x_ref[...], around)
+    (top, top_strip), (bottom, bottom_strip) = turns
+    first, split = {}, {}
+    for n, row in enumerate(range(1 - UP0, ROWS + UP0 - 1)):
+        side = sides[CI * (n + 1) : CI * (n + 2)]
+        first[row] = side[:, :128] - 0.25 * vertical(block, row, ROWS, top, bottom)
+        other = side[:, 128:] - 0.25 * vertical(strip, row, ROWS, top_strip, bottom_strip)
+        split[row] = halves(first[row])
+        at = slice(CI * n, CI * (n + 1))
+        y_ref[at, :128], y_ref[at, 256:384] = split[row]
+        y_ref[at, 128:256], y_ref[at, 384:] = halves(other)
+    around = around[:, :128]
+    sides = dot(y_ref[:, :256], around) + dot(y_ref[:, 256:], around)
     low, high = -2 * UP1, ROWS + 2 * UP1
-    for row in range(low, high):
-        second = 2.0 * fine_lap(first, first_strip, row, turns, False) - block[row]
-        at = pl.ds((row - low) * 128, 128)
-        one, one_low = halves(first[row])
-        two, two_low = halves(second)
-        for n, part in enumerate((block[row].astype(bf16), one, two, one_low, two_low)):
-            t_ref[CI * n : CI * (n + 1), at] = part
-        for n, part in enumerate((block[row].astype(bf16), one, two)):
-            t_ref[CI * (5 + n) : CI * (6 + n), at] = part
+    for n, row in enumerate(range(low, high)):
+        lap = sides[CI * (n + 1) : CI * (n + 2)] - 0.25 * vertical(first, row, ROWS, top, bottom)
+        at = pl.ds(n * 128, 128)
+        zero = block[row].astype(bf16)
+        one, one_low = split[row]
+        two, two_low = halves(2.0 * lap - block[row])
+        for k, part in enumerate((zero, one, two, one_low, two_low, zero, one, two)):
+            t_ref[CI * k : CI * (k + 1), at] = part
     own = pl.ds(-low * 128, ROWS * 128)
     terms_ref[...] = t_ref[0 : 5 * CI, own]
     weights = weight_halves(w_ref, 5 * CI)
-    lane = lanes(CA)
-    even = 2 * (lane % 64)
-    ends = end_index(CA, 2, CCOLS)
-    filled = []
     for crow in range(-UP1, CROWS + UP1):
         place = crow + UP1
         pre = dot(weights, t_ref[:, place * 256 : place * 256 + 256])
@@ -253,15 +282,22 @@
             sig = jnp.where(pre >= 0, inverse, decay * inverse)
             sig_ref[2 * (crow + 1)] = sig[:, :128]
             sig_ref[2 * (crow + 1) + 1] = sig[:, 128:]
-        both = act[:, :128] + act[:, 128:]
-        both = 0.25 * (both + roll(both, -1))
-        x1_ref[place] = pick(both, even)
-        filled.append(pick(both, ends))
+        side_by_side(a_ref, slice(CA * place, CA * (place + 1)), act[:, :128] + act[:, 128:])
+    i, j = grid(256, 256)
+    slot = j % SLOT
+    end = jnp.where(slot < STRIP, slot, CCOLS - SLOT + slot)
+    column = jnp.where(j < 128, j, end)
+    means = dot(a_ref[...], jnp.where(i % 128 // 2 == column, 0.25, 0.0).astype(bf16))
+    filled = []
+    for place in range(CROWS + 2 * UP1):
+        value = means[CA * place : CA * (place + 1)]
+        x1_ref[place] = value[:, :128]
+        filled.append(value[:, 128:])
     put_slots((ends_ref, ends_copy_ref), filled, len(filled))
 
 
 def coarse_kernel(
-    flips, x1_ref, far_ref, near_ref, w_ref, feat_ref, sig_ref, t_ref
+    flips, x1_ref, far_ref, near_ref, w_ref, feat_ref, sig_ref, t_ref, z_ref
 ):
     here = Place(flips)
     turns = coarse_turns(here, CA)
@@ -273,11 +309,10 @@
         rows[row] = coarse_row(
             x1_ref[place], left[place // PER], right[place // PER], place % PER
         )
-    first = {row: coarse_lap(rows, row, turns) for row in range(1 - UP1, CROWS + UP1 - 1)}
-    second = {
-        row: 2.0 * coarse_lap(first, row, turns) - rows[row]
-        for row in range(-UP2, CROWS + UP2)
-    }
+    around = ring(128, 2)
+    first = coarse_laps(rows, 1 - UP1, CROWS + UP1 - 1, turns, around, z_ref)
+    second = coarse_laps(first, -UP2, CROWS + UP2, turns, around, z_ref)
+    second = {row: 2.0 * second[row] - rows[row] for row in second}
     for q, (a, b) in enumerate(PAIRS):
         at = pl.ds(q * 128, 128)
         for k, term in enumerate((rows, first, second)):
@@ -332,13 +367,13 @@
     sig1_ref, far_ref, near_ref, shift_ref, labels_ref, out_ref, s_ref, head_ref
 ):
     here = Place()
-    for q in range(SLABS):
-        if q < len(PAIRS):
-            value = sig1_ref[q]
-        else:
-            value = (before, after)[q - len(PAIRS)](far_ref[...], near_ref[...], here.odd_tile)
+    left = before(far_ref[...], near_ref[...], here.odd_tile)
+    right = after(far_ref[...], near_ref[...], here.odd_tile)
+    for n, row in enumerate(range(-UP2, CROWS + UP2)):
+        q, half = WHERE[row]
+        value = coarse_row(roll(sig1_ref[q], 64 * half), left, right, 2 * q + half)
         high, low = halves(value)
-        at = pl.ds(q * 128, 128)
+        at = pl.ds(n * 128, 128)
         for m in range(MAPS):
             chans = slice(CH1 * m, CH1 * (m + 1))
             s_ref[m, :CH1, at] = high[chans]
@@ -351,17 +386,17 @@
 
 def back_kernel(
     flips, feat_ref, head_ref, fw_ref, w1_ref, s_ref, gram_ref, sig0_ref, terms_ref,
-    logits_ref, grads_ref, d_ref,
+    logits_ref, grads_ref, d_ref, z_ref,
     *, pooled,
 ):
     here = Place(flips)
     features = jnp.sum(feat_ref[...], axis=0, keepdims=True) * (1.0 / pooled)
     row8 = lax.broadcasted_iota(jnp.int32, (8, 128), 0)
-    spread = jnp.where(lanes(8) // CH1 == row8, jnp.broadcast_to(features, (8, 128)), 0.0)
+    apart = jnp.where(lanes(8) // CH1 == row8, jnp.broadcast_to(features, (8, 128)), 0.0)
     fw = fw_ref[...]
     shift, labels, out = head_ref[0], head_ref[1], head_ref[2]
     hidden = jnp.tanh(
-        jnp.dot(spread, fw, precision=exact, preferred_element_type=f32) + shift
+        jnp.dot(apart, fw, precision=exact, preferred_element_type=f32) + shift
     )
     logits = jnp.sum(hidden * out, axis=1, keepdims=True)
     logits_ref[...] = jnp.broadcast_to(logits, (8, 128))
@@ -389,36 +424,34 @@
         weights = jnp.where(lane < 2 * CH1, high.astype(f32), low.astype(f32)).astype(bf16)
         parts.append(dot(weights[:, : 3 * CH1], s_ref[m]))
 
-    def slab(k, q):
-        return jnp.concatenate(
-            [part[CH0 * k : CH0 * (k + 1), 128 * q : 128 * (q + 1)] for part in parts], axis=0
-        )
-
-    def spread_rows(k, low, high, strips):
-        left, right = (slab(k, SLABS - 2), slab(k, SLABS - 1)) if strips else (None, None)
-        packed = [slab(k, q) for q in range(len(PAIRS))]
+    def term(k, low, high):
         rows = {}
         for row in range(low, high):
-            q, half = WHERE[row]
-            value = roll(packed[q], 64 * half)
-            rows[row] = coarse_row(value, left, right, 2 * q + half) if strips else value
+            at = slice(128 * (row + UP2), 128 * (row + UP2 + 1))
+            rows[row] = jnp.concatenate([part[CH0 * k : CH0 * (k + 1), at] for part in parts], axis=0)
         return rows
 
     turns = coarse_turns(here, CA)
-    g0 = spread_rows(0, -1, CROWS + 1, False)
-    g1 = spread_rows(1, 1 - UP2, CROWS + UP2 - 1, True)
-    g2 = spread_rows(2, -UP2, CROWS + UP2, True)
-    inner = {row: g1[row] + 2.0 * coarse_lap(g2, row, turns) for row in g1}
-    doubled = lanes(CA) // 2
-    for crow in range(-1, CROWS + 1):
-        dx1 = g0[crow] - g2[crow] + coarse_lap(inner, crow, turns)
-        dx1 = 0.25 * pick(dx1, doubled)
-        for n in (2 * (crow + 1), 2 * (crow + 1) + 1):
-            high, low = halves(dx1 * sig0_ref[n])
-            at = pl.ds(n * 128, 128)
-            d_ref[:CA, at] = high
-            d_ref[CA : 2 * CA, at] = low
-            d_ref[2 * CA :, at] = high
+    around = ring(128, 2)
+    g0 = term(0, -1, CROWS + 1)
+    g1 = term(1, 1 - UP2, CROWS + UP2 - 1)
+    g2 = term(2, -UP2, CROWS + UP2)
+    inner = coarse_laps(g2, 1 - UP2, CROWS + UP2 - 1, turns, around, z_ref)
+    inner = {row: g1[row] + 2.0 * inner[row] for row in g1}
+    outer = coarse_laps(inner, -1, CROWS + 1, turns, around, z_ref)
+    for n, crow in enumerate(range(-1, CROWS + 1)):
+        at = slice(CA * n, CA * (n + 1))
+        side_by_side(z_ref, at, g0[crow] - g2[crow] + outer[crow])
+    i, j = grid(256, 128)
+    doubled = jnp.where(i % 128 == j // 2, 0.25, 0.0).astype(bf16)
+    spread = dot(z_ref[0 : CA * (CROWS + 2)], doubled)
+    for n in range(ROWS + 4):
+        value = spread[CA * (n // 2) : CA * (n // 2 + 1)]
+        high, low = halves(value * sig0_ref[n])
+        at = pl.ds(n * 128, 128)
+        d_ref[:CA, at] = high
+        d_ref[CA : 2 * CA, at] = low
+        d_ref[2 * CA :, at] = high
     both = dot_nt(terms_ref[...], d_ref[: 2 * CA, 2 * 128 : (2 + ROWS) * 128])
     lane = lanes(CI)
     row16 = lax.broadcasted_iota(jnp.int32, (CI, 128), 0)
@@ -566,7 +599,12 @@
         ),
         edge_flip, far, near, own, far0, near0, fine_forward,
         smem=1,
-        scratch=[pltpu.VMEM((8 * CI, 2 * crows * 128), bf16)],
+        scratch=[
+            pltpu.VMEM((8 * CI, 2 * crows * 128), bf16),
+            pltpu.VMEM(((ROWS + 2 * UP0) * CI, 256), bf16),
+            pltpu.VMEM(((ROWS + 2 * UP0 - 2) * CI, 512), bf16),
+            pltpu.VMEM((crows * CA, 256), bf16),
+        ],
     )
     far1, near1 = exchange(TILE, far1, near1)
     feats, sig1, terms1 = call(
@@ -578,6 +616,7 @@
         ),
         edge_flip, x1, far1, near1, coarse_forward,
         smem=1,
+        scratch=[pltpu.VMEM((crows * CA, 256), bf16)],
     )
     feats = share(feats, FIRST)
     feats = call(row_again_kernel, shape(lax.axis_size(SECOND), CB), feats)
@@ -591,7 +630,7 @@
     pooled = CROWS * faces * CCOLS * tiles
     split1, head = call(
         split_kernel,
-        (shape(MAPS, 3 * CH1, SLABS * 128, dtype=bf16), shape(3, 8, 128)),
+        (shape(MAPS, 3 * CH1, (CROWS + 2 * UP2) * 128, dtype=bf16), shape(3, 8, 128)),
         sig1, far2, near2, shift, labels8, out_weight[None],
     )
     logits, grads, dpre0 = call(
@@ -603,6 +642,7 @@
         ),
         edge_flip, feats, head, features4, coarse_backward, split1, grams, sig0, terms0,
         smem=1,
+        scratch=[pltpu.VMEM(((CROWS + 2 * UP2) * CA, 256), bf16)],
     )
     grads = share(grads, PLANE)
     trade = shape(groups(ROWS + 4), 2 * CI, 128)

time: 116 us -> 119 us (1.026)
  other arithmetic: 0.35 us -> 3.18 us
  local copies, waits for them, and re-layouts: 5.04 us -> 7.72 us
  waiting for transfers between devices: 14.4 us -> 12.1 us
  Pallas kernels: 14.2 us -> 12.9 us
    unnamed x18 -> x30, local copies, waits for them, and re-layouts: 4.1 us -> 6.02 us
    all_to_all x3, waiting for transfers between devices: 11.7 us -> 10.2 us  [share(): return lax.all_to_all(rows, axes, 0, 0, tiled=True)]
    pallas_call x12, Pallas kernels: 14.2 us -> 12.9 us  [call(): pl.pallas_call(kernel, out_shape=outs, in_specs=in_specs, out_specs=jax.t...]
  transfers between devices with their start and end apart: 13 -> 13, of which waited for: 6 -> 6; matrix products, arithmetic and copies ran while one was open for 1% -> 5% of each run, Pallas kernels for 3% -> 3%
where the time goes in v5:
time: 119 us; the launch traced here: 117 us
  starting transfers between devices  64.9 us (55%)
  blocking collectives  14.1 us (12%)
  Pallas kernels  12.9 us (11%)
  waiting for transfers between devices  12.1 us (10%)
  local copies, waits for them, and re-layouts  7.72 us (6%)
  other arithmetic  3.18 us (3%)
    ppermute x5, starting transfers between devices, exchange(): lax.ppermute(near_value, axis, near)  24.8 us
    ppermute x5, starting transfers between devices, exchange(): lax.ppermute(far_value, axis, far)  20.1 us
    all_to_all x3, starting transfers between devices, share(): return lax.all_to_all(rows, axes, 0, 0, tiled=True)  20 us
    all_to_all x1, blocking collectives, share(): return lax.all_to_all(rows, axes, 0, 0, tiled=True)  14.1 us
    pallas_call x12, Pallas kernels, call(): pl.pallas_call(kernel, out_shape=outs, in_specs=in_specs, out_specs=jax.t...  12.9 us
    all_to_all x3, waiting for transfers between devices, share(): return lax.all_to_all(rows, axes, 0, 0, tiled=True)  10.2 us
    unnamed x30, local copies, waits for them, and re-layouts  6.02 us
  transfers between devices with their start and end apart: 13, of which 6 were waited for; matrix products, arithmetic and copies ran while one was open for 5% of the time, Pallas kernels for 3%

profile of v5, /device:TPU:1, one launch (start us, length us, event | category | flops | bytes accessed | tf_op | source)
XLA Modules:
  0.0 116.7 jit_solution(8595612591329556754)
XLA Ops:
  0.7 0.8 copy-done.6
  1.6 6.2 %collective-permute-start = (f32[12,16,128]{2,1,0:T(8,128)S(1)}, f32[12,16,128]{2,1,0:T(8,128)S(1)}, u32[]{:S(2)}, u32[]{:S(2)}) collective-permute-start(f32[12,16,128]{2,1,0:T(8,128)S(1)} %get-tuple-element.30), channel_id=1, source_target_pairs={{0,448},{64,128},{128,64},{192,256},{256,192},{320,384},{384,320},... | collective-permute-start | bytes 294920 | tf_op jit(solution)/shard_map/ppermute | solution.py:555
  7.8 1.9 %collective-permute-start.1 = (f32[12,16,128]{2,1,0:T(8,128)S(1)}, f32[12,16,128]{2,1,0:T(8,128)S(1)}, u32[]{:S(2)}, u32[]{:S(2)}) collective-permute-start(f32[12,16,128]{2,1,0:T(8,128)S(1)} %get-tuple-element.31), channel_id=1, source_target_pairs={{0,64},{64,0},{128,192},{192,128},{256,320},{320,256},{384,448},{4... | collective-permute-start | bytes 294920 | tf_op jit(solution)/shard_map/ppermute | solution.py:555
  9.7 0.8 multiply_bitcast_fusion
  10.5 0.1 reshape.29
  10.6 0.7 convert_bitcast_fusion
  11.3 0.9 fusion.1.shift_ref
  12.2 0.9 collective-permute-done.1.near_ref
  13.2 0.2 shard_map.121
  13.3 6.5 %collective-permute-start.2 = (f32[2,16,128]{2,1,0:T(8,128)S(1)}, f32[2,16,128]{2,1,0:T(8,128)S(1)}, u32[]{:S(2)}, u32[]{:S(2)}) collective-permute-start(f32[2,16,128]{2,1,0:T(8,128)S(1)} %get-tuple-element.33), channel_id=1, source_target_pairs={{0,63},{1,2},{2,1},{3,4},{4,3},{5,6},{6,5},{7,8},{8,7},{9,10},{10,... | collective-permute-start | bytes 49160 | tf_op jit(solution)/shard_map/ppermute | solution.py:555
  19.9 9.2 %collective-permute-start.3 = (f32[2,16,128]{2,1,0:T(8,128)S(1)}, f32[2,16,128]{2,1,0:T(8,128)S(1)}, u32[]{:S(2)}, u32[]{:S(2)}) collective-permute-start(f32[2,16,128]{2,1,0:T(8,128)S(1)} %get-tuple-element.34), channel_id=1, source_target_pairs={{0,1},{1,0},{2,3},{3,2},{4,5},{5,4},{6,7},{7,6},{8,9},{9,8},{10,11... | collective-permute-start | bytes 49160 | tf_op jit(solution)/shard_map/ppermute | solution.py:555
  29.1 0.9 pad_maximum_fusion.1.refs_3_
  30.1 0.8 copy.18
  30.9 0.7 copy-done.4
  31.6 2.1 %shard_map.122 = (f32[18,64,128]{2,1,0:T(8,128)S(1)}, f32[20,64,128]{2,1,0:T(8,128)S(1)}, bf16[80,2048]{1,0:T(8,128)(2,1)S(1)}, f32[1,64,128]{2,1,0:T(8,128)S(1)}, f32[1,64,128]{2,1,0:T(8,128)S(1)}) custom-call(s32[8,64]{1,0:T(8,128)S(1)} %copy-done.4, f32[12,16,128]{2,1,0:T(8,128)S(1)} %collective-permute-done.far_ref, ...), custom_call_target="tpu_custom_call" | custom-call | tf_op jit(solution)/shard_map/pallas_call | solution.py:537
  33.7 0.7 copy-done.1
  34.4 1.9 %collective-permute-start.4 = (f32[1,64,128]{2,1,0:T(8,128)S(1)}, f32[1,64,128]{2,1,0:T(8,128)S(1)}, u32[]{:S(2)}, u32[]{:S(2)}) collective-permute-start(f32[1,64,128]{2,1,0:T(8,128)S(1)} %get-tuple-element.36), channel_id=1, source_target_pairs={{0,63},{1,2},{2,1},{3,4},{4,3},{5,6},{6,5},{7,8},{8,7},{9,10},{10,... | collective-permute-start | bytes 98312 | tf_op jit(solution)/shard_map/ppermute | solution.py:555
  36.3 4.9 %collective-permute-start.5 = (f32[1,64,128]{2,1,0:T(8,128)S(1)}, f32[1,64,128]{2,1,0:T(8,128)S(1)}, u32[]{:S(2)}, u32[]{:S(2)}) collective-permute-start(f32[1,64,128]{2,1,0:T(8,128)S(1)} %get-tuple-element.37), channel_id=1, source_target_pairs={{0,1},{1,0},{2,3},{3,2},{4,5},{5,4},{6,7},{7,6},{8,9},{9,8},{10,11... | collective-permute-start | bytes 98312 | tf_op jit(solution)/shard_map/ppermute | solution.py:555
  41.2 0.1 pad_maximum_fusion.3.w_ref
  41.3 0.7 collective-permute-done.5.near_ref
  42.1 2.4 %shard_map.123 = (f32[32,128]{1,0:T(8,128)}, f32[7,128,128]{2,1,0:T(8,128)S(1)}, bf16[4,144,896]{2,1,0:T(8,128)(2,1)S(1)}) custom-call(s32[8,64]{1,0:T(8,128)S(1)} %copy-done.4, f32[18,64,128]{2,1,0:T(8,128)S(1)} %get-tuple-element.35.x1_ref, f32[1,64,128]{2,1,0:T(8,128)S(1)} %collective-permute-done.4.far_ref, ...), custom_call_target="tpu_custom_call" | custom-call | tf_op jit(solution)/shard_map/pallas_call | solution.py:537
  44.5 9.6 %all-to-all-start = ((f32[32,1,128]{2,1,0:T(1,128)}), f32[32,1,128]{2,1,0:T(1,128)S(1)}, u32[]{:S(2)}, u32[]{:S(2)}) async-start(f32[32,1,128]{2,1,0:T(1,128)} %bitcast.6), calls=%async_computation | async-start | bytes 32768 | tf_op jit(solution)/shard_map/all_to_all | solution.py:559
  54.1 0.7 pad_maximum_fusion.4.refs_4_
  54.8 0.5 shard_map.125
  55.3 2.0 %collective-permute-start.6 = (f32[128,128]{1,0:T(8,128)S(1)}, f32[128,128]{1,0:T(8,128)S(1)}, u32[]{:S(2)}, u32[]{:S(2)}) collective-permute-start(f32[128,128]{1,0:T(8,128)S(1)} %get-tuple-element.41), channel_id=1, source_target_pairs={{0,63},{1,2},{2,1},{3,4},{4,3},{5,6},{6,5},{7,8},{8,7},{9,10},{10,... | collective-permute-start | bytes 196616 | tf_op jit(solution)/shard_map/ppermute | solution.py:555
  57.3 4.6 %collective-permute-start.7 = (f32[128,128]{1,0:T(8,128)S(1)}, f32[128,128]{1,0:T(8,128)S(1)}, u32[]{:S(2)}, u32[]{:S(2)}) collective-permute-start(f32[128,128]{1,0:T(8,128)S(1)} %get-tuple-element.42), channel_id=1, source_target_pairs={{0,1},{1,0},{2,3},{3,2},{4,5},{5,4},{6,7},{7,6},{8,9},{9,8},{10,11... | collective-permute-start | bytes 196616 | tf_op jit(solution)/shard_map/ppermute | solution.py:555
  61.9 4.0 %all-to-all-done = f32[32,1,128]{2,1,0:T(1,128)S(1)} async-done(((f32[32,1,128]{2,1,0:T(1,128)}), f32[32,1,128]{2,1,0:T(1,128)S(1)}, u32[]{:S(2)}, u32[]{:S(2)}) %all-to-all-start) | async-done | bytes 16416 | tf_op jit(solution)/shard_map/all_to_all | solution.py:559
  65.8 0.6 shard_map.124
  66.5 3.4 %all-to-all-start.1 = ((f32[16,1,128]{2,1,0:T(1,128)}), f32[16,1,128]{2,1,0:T(1,128)S(1)}, u32[]{:S(2)}, u32[]{:S(2)}) async-start(f32[16,1,128]{2,1,0:T(1,128)} %bitcast.9), calls=%async_computation.1 | async-start | bytes 16384 | tf_op jit(solution)/shard_map/all_to_all | solution.py:559
  70.0 0.7 shard_map.126
  70.7 0.6 copy-done.9
  71.2 5.0 %all-to-all-done.1 = f32[16,1,128]{2,1,0:T(1,128)S(1)} async-done(((f32[16,1,128]{2,1,0:T(1,128)}), f32[16,1,128]{2,1,0:T(1,128)S(1)}, u32[]{:S(2)}, u32[]{:S(2)}) %all-to-all-start.1) | async-done | bytes 8224 | tf_op jit(solution)/shard_map/all_to_all | solution.py:559
  76.2 1.0 copy-done.2
  77.2 0.7 copy-done.3
  77.9 0.7 copy-done.8
  78.7 0.7 copy-done.10
  79.4 2.8 %shard_map.127 = (f32[8,128]{1,0:T(8,128)S(1)}, f32[512,128]{1,0:T(8,128)S(1)}, bf16[192,2560]{1,0:T(8,128)(2,1)S(1)}) custom-call(s32[8,64]{1,0:T(8,128)S(1)} %copy-done.5, f32[16,128]{1,0:T(8,128)S(1)} %bitcast.33, f32[3,8,128]{2,1,0:T(8,128)S(1)} %copy-done.10, f32[128,128]{1,0:T(8,128)S(1)} %pad_maximum_fusion.1.refs_3_, f32[48,128]{1,0:T(8,128)S(1)} %copy-done.3, ...), custom_call_target="tpu_custom_call" | custom-call | tf_op jit(solution)/shard_map/pallas_call | solution.py:537
  82.2 14.1 %all_to_all.44 = f32[32,16,128]{2,1,0:T(8,128)S(1)} all-to-all(f32[32,16,128]{2,1,0:T(8,128)S(1)} %bitcast.30), channel_id=1, replica_groups=mesh['x'=4,'y_lo'=2,'z'=16,'y_hi'=2,'core'=2] {'x','y_lo','y_hi','core'}, dimensions={0} | all-to-all | bytes 524288 | tf_op jit(solution)/shard_map/all_to_all | solution.py:559
  96.3 0.7 shard_map.130
  97.0 7.0 %all-to-all-start.3 = ((f32[16,16,128]{2,1,0:T(8,128)}), f32[16,16,128]{2,1,0:T(8,128)S(1)}, u32[]{:S(2)}, u32[]{:S(2)}) async-start(f32[16,16,128]{2,1,0:T(8,128)} %bitcast.18), calls=%async_computation.3 | async-start | bytes 262144 | tf_op jit(solution)/shard_map/all_to_all | solution.py:559
  104.1 0.4 shard_map.128
  104.4 3.5 %collective-permute-start.8 = (f32[1,32,128]{2,1,0:T(8,128)S(1)}, f32[1,32,128]{2,1,0:T(8,128)S(1)}, u32[]{:S(2)}, u32[]{:S(2)}) collective-permute-start(f32[1,32,128]{2,1,0:T(8,128)S(1)} %get-tuple-element.51), channel_id=1, source_target_pairs={{0,63},{1,2},{2,1},{3,4},{4,3},{5,6},{6,5},{7,8},{8,7},{9,10},{10,... | collective-permute-start | bytes 49160 | tf_op jit(solution)/shard_map/ppermute | solution.py:555
  107.9 4.1 %collective-permute-start.9 = (f32[1,32,128]{2,1,0:T(8,128)S(1)}, f32[1,32,128]{2,1,0:T(8,128)S(1)}, u32[]{:S(2)}, u32[]{:S(2)}) collective-permute-start(f32[1,32,128]{2,1,0:T(8,128)S(1)} %get-tuple-element.52), channel_id=1, source_target_pairs={{0,1},{1,0},{2,3},{3,2},{4,5},{5,4},{6,7},{7,6},{8,9},{9,8},{10,11... | collective-permute-start | bytes 49160 | tf_op jit(solution)/shard_map/ppermute | solution.py:555
  112.0 0.6 slice_reduce_fusion
  112.7 0.2 collective-permute-done.9.refs_3_
  112.9 1.9 %shard_map.129 = f32[256,128]{1,0:T(8,128)} custom-call(s32[8,64]{1,0:T(8,128)S(1)} %copy-done.5, f32[20,48,128]{2,1,0:T(8,128)S(1)} %get-tuple-element.50.refs_1_, f32[1,32,128]{2,1,0:T(8,128)S(1)} %collective-permute-done.8.refs_2_, f32[1,32,128]{2,1,0:T(8,128)S(1)} %collective-permute-done.9.refs_3_), custom_call_target="tpu_custom_call" | custom-call | tf_op jit(solution)/shard_map/pallas_call | solution.py:537
  114.7 1.3 %all-to-all-done.3 = f32[16,16,128]{2,1,0:T(8,128)S(1)} async-done(((f32[16,16,128]{2,1,0:T(8,128)}), f32[16,16,128]{2,1,0:T(8,128)S(1)}, u32[]{:S(2)}, u32[]{:S(2)}) %all-to-all-start.3) | async-done | bytes 131104 | tf_op jit(solution)/shard_map/all_to_all | solution.py:559
  116.0 0.7 shard_map.131
  (37 shorter events, 0.4 us)
Async XLA Ops:
  0.6 10.7 %copy-start = (f32[2,128]{1,0:T(2,128)S(1)}, f32[2,128]{1,0:T(2,128)}, u32[]{:S(2)}) copy-start(f32[2,128]{1,0:T(2,128)} %param.16) | copy-start | bytes 3076
  0.6 0.8 copy-start.6
  1.5 52.6 %copy-start.14 = (f32[3,16,32]{2,1,0:T(8,128)S(1)}, f32[3,16,32]{2,1,0:T(8,128)}, u32[]{:S(2)}) copy-start(f32[3,16,32]{2,1,0:T(8,128)} %param.14) | copy-start | bytes 18436
  1.6 10.6 %collective-permute-start = (f32[12,16,128]{2,1,0:T(8,128)S(1)}, f32[12,16,128]{2,1,0:T(8,128)S(1)}, u32[]{:S(2)}, u32[]{:S(2)}) collective-permute-start(f32[12,16,128]{2,1,0:T(8,128)S(1)} %get-tuple-element.30), channel_id=1, source_target_pairs={{0,448},{64,128},{128,64},{192,256},{256,192},{320,384},{384,320},... | collective-permute-start | bytes 294920 | tf_op jit(solution)/shard_map/ppermute | solution.py:555
  7.8 5.4 %collective-permute-start.1 = (f32[12,16,128]{2,1,0:T(8,128)S(1)}, f32[12,16,128]{2,1,0:T(8,128)S(1)}, u32[]{:S(2)}, u32[]{:S(2)}) collective-permute-start(f32[12,16,128]{2,1,0:T(8,128)S(1)} %get-tuple-element.31), channel_id=1, source_target_pairs={{0,64},{64,0},{128,192},{192,128},{256,320},{320,256},{384,448},{4... | collective-permute-start | bytes 294920 | tf_op jit(solution)/shard_map/ppermute | solution.py:555
  10.6 31.5 %copy-start.12 = (f32[64,48]{0,1:T(8,128)}, f32[64,48]{0,1:T(8,128)S(1)}, u32[]{:S(2)}) copy-start(f32[64,48]{0,1:T(8,128)S(1)} %reshape.29) | copy-start | bytes 36868
  13.3 17.6 %collective-permute-start.2 = (f32[2,16,128]{2,1,0:T(8,128)S(1)}, f32[2,16,128]{2,1,0:T(8,128)S(1)}, u32[]{:S(2)}, u32[]{:S(2)}) collective-permute-start(f32[2,16,128]{2,1,0:T(8,128)S(1)} %get-tuple-element.33), channel_id=1, source_target_pairs={{0,63},{1,2},{2,1},{3,4},{4,3},{5,6},{6,5},{7,8},{8,7},{9,10},{10,... | collective-permute-start | bytes 49160 | tf_op jit(solution)/shard_map/ppermute | solution.py:555
  19.9 11.0 %collective-permute-start.3 = (f32[2,16,128]{2,1,0:T(8,128)S(1)}, f32[2,16,128]{2,1,0:T(8,128)S(1)}, u32[]{:S(2)}, u32[]{:S(2)}) collective-permute-start(f32[2,16,128]{2,1,0:T(8,128)S(1)} %get-tuple-element.34), channel_id=1, source_target_pairs={{0,1},{1,0},{2,3},{3,2},{4,5},{5,4},{6,7},{7,6},{8,9},{9,8},{10,11... | collective-permute-start | bytes 49160 | tf_op jit(solution)/shard_map/ppermute | solution.py:555
  30.0 39.9 %copy-start.11 = (f32[128]{0:T(128)S(1)}, f32[128]{0:T(128)}, u32[]{:S(2)}) copy-start(f32[128]{0:T(128)} %param.17) | copy-start | bytes 1540
  30.9 0.7 copy-start.4
  33.6 0.7 copy-start.1
  34.4 7.0 %collective-permute-start.4 = (f32[1,64,128]{2,1,0:T(8,128)S(1)}, f32[1,64,128]{2,1,0:T(8,128)S(1)}, u32[]{:S(2)}, u32[]{:S(2)}) collective-permute-start(f32[1,64,128]{2,1,0:T(8,128)S(1)} %get-tuple-element.36), channel_id=1, source_target_pairs={{0,63},{1,2},{2,1},{3,4},{4,3},{5,6},{6,5},{7,8},{8,7},{9,10},{10,... | collective-permute-start | bytes 98312 | tf_op jit(solution)/shard_map/ppermute | solution.py:555
  36.3 5.8 %collective-permute-start.5 = (f32[1,64,128]{2,1,0:T(8,128)S(1)}, f32[1,64,128]{2,1,0:T(8,128)S(1)}, u32[]{:S(2)}, u32[]{:S(2)}) collective-permute-start(f32[1,64,128]{2,1,0:T(8,128)S(1)} %get-tuple-element.37), channel_id=1, source_target_pairs={{0,1},{1,0},{2,3},{3,2},{4,5},{5,4},{6,7},{7,6},{8,9},{9,8},{10,11... | collective-permute-start | bytes 98312 | tf_op jit(solution)/shard_map/ppermute | solution.py:555
  42.1 34.1 %copy-start.5 = (s32[8,64]{1,0:T(8,128)S(1)}, s32[8,64]{1,0:T(8,128)}, u32[]{:S(2)}) copy-start(s32[8,64]{1,0:T(8,128)} %refs_0_.3) | copy-start | bytes 6148
  44.5 21.3 %all-to-all-start = ((f32[32,1,128]{2,1,0:T(1,128)}), f32[32,1,128]{2,1,0:T(1,128)S(1)}, u32[]{:S(2)}, u32[]{:S(2)}) async-start(f32[32,1,128]{2,1,0:T(1,128)} %bitcast.6), calls=%async_computation | async-start | bytes 32768 | tf_op jit(solution)/shard_map/all_to_all | solution.py:559
  55.3 14.7 %copy-start.7 = (f32[3,16,128]{2,1,0:T(8,128)}, f32[3,16,128]{2,1,0:T(8,128)S(1)}, u32[]{:S(2)}) copy-start(f32[3,16,128]{2,1,0:T(8,128)S(1)} %get-tuple-element.45.refs_6_) | copy-start | bytes 73732
  55.3 14.6 %collective-permute-start.6 = (f32[128,128]{1,0:T(8,128)S(1)}, f32[128,128]{1,0:T(8,128)S(1)}, u32[]{:S(2)}, u32[]{:S(2)}) collective-permute-start(f32[128,128]{1,0:T(8,128)S(1)} %get-tuple-element.41), channel_id=1, source_target_pairs={{0,63},{1,2},{2,1},{3,4},{4,3},{5,6},{6,5},{7,8},{8,7},{9,10},{10,... | collective-permute-start | bytes 196616 | tf_op jit(solution)/shard_map/ppermute | solution.py:555
  57.3 12.6 %collective-permute-start.7 = (f32[128,128]{1,0:T(8,128)S(1)}, f32[128,128]{1,0:T(8,128)S(1)}, u32[]{:S(2)}, u32[]{:S(2)}) collective-permute-start(f32[128,128]{1,0:T(8,128)S(1)} %get-tuple-element.42), channel_id=1, source_target_pairs={{0,1},{1,0},{2,3},{3,2},{4,5},{5,4},{6,7},{7,6},{8,9},{9,8},{10,11... | collective-permute-start | bytes 196616 | tf_op jit(solution)/shard_map/ppermute | solution.py:555
  66.5 9.8 %all-to-all-start.1 = ((f32[16,1,128]{2,1,0:T(1,128)}), f32[16,1,128]{2,1,0:T(1,128)S(1)}, u32[]{:S(2)}, u32[]{:S(2)}) async-start(f32[16,1,128]{2,1,0:T(1,128)} %bitcast.9), calls=%async_computation.1 | async-start | bytes 16384 | tf_op jit(solution)/shard_map/all_to_all | solution.py:559
  70.6 0.6 copy-start.9
  76.2 1.0 copy-start.2
  77.2 0.7 copy-start.3
  77.9 0.7 copy-start.8
  78.7 0.7 copy-start.10
  79.4 24.6 %copy-start.13 = (f32[64,48]{0,1:T(8,128)S(1)}, f32[64,48]{0,1:T(8,128)}, u32[]{:S(2)}) copy-start(f32[64,48]{0,1:T(8,128)} %copy-done.12) | copy-start | bytes 36868
  97.0 19.0 %all-to-all-start.3 = ((f32[16,16,128]{2,1,0:T(8,128)}), f32[16,16,128]{2,1,0:T(8,128)S(1)}, u32[]{:S(2)}, u32[]{:S(2)}) async-start(f32[16,16,128]{2,1,0:T(8,128)} %bitcast.18), calls=%async_computation.3 | async-start | bytes 262144 | tf_op jit(solution)/shard_map/all_to_all | solution.py:559
  104.4 8.2 %collective-permute-start.8 = (f32[1,32,128]{2,1,0:T(8,128)S(1)}, f32[1,32,128]{2,1,0:T(8,128)S(1)}, u32[]{:S(2)}, u32[]{:S(2)}) collective-permute-start(f32[1,32,128]{2,1,0:T(8,128)S(1)} %get-tuple-element.51), channel_id=1, source_target_pairs={{0,63},{1,2},{2,1},{3,4},{4,3},{5,6},{6,5},{7,8},{8,7},{9,10},{10,... | collective-permute-start | bytes 49160 | tf_op jit(solution)/shard_map/ppermute | solution.py:555
  107.9 4.9 %collective-permute-start.9 = (f32[1,32,128]{2,1,0:T(8,128)S(1)}, f32[1,32,128]{2,1,0:T(8,128)S(1)}, u32[]{:S(2)}, u32[]{:S(2)}) collective-permute-start(f32[1,32,128]{2,1,0:T(8,128)S(1)} %get-tuple-element.52), channel_id=1, source_target_pairs={{0,1},{1,0},{2,3},{3,2},{4,5},{5,4},{6,7},{7,6},{8,9},{9,8},{10,11... | collective-permute-start | bytes 49160 | tf_op jit(solution)/shard_map/ppermute | solution.py:555

commit v6 on v5

--- a/solution.py
+++ b/solution.py
@@ -377,8 +377,7 @@
         for m in range(MAPS):
             chans = slice(CH1 * m, CH1 * (m + 1))
             s_ref[m, :CH1, at] = high[chans]
-            s_ref[m, CH1 : 2 * CH1, at] = low[chans]
-            s_ref[m, 2 * CH1 :, at] = high[chans]
+            s_ref[m, CH1:, at] = low[chans]
     head_ref[0] = shift_ref[...]
     head_ref[1] = labels_ref[...]
     head_ref[2] = jnp.broadcast_to(out_ref[...], (8, 128))
@@ -421,8 +420,7 @@
         weights = jnp.where(lane // CH1 == m, weighted, 0.0)
         weights = weights + roll(weights, 64)
         high, low = halves(weights + roll(weights, 32))
-        weights = jnp.where(lane < 2 * CH1, high.astype(f32), low.astype(f32)).astype(bf16)
-        parts.append(dot(weights[:, : 3 * CH1], s_ref[m]))
+        parts.append(dot(high[:, : 2 * CH1], s_ref[m]) + dot(low[:, :CH1], s_ref[m, :CH1]))
 
     def term(k, low, high):
         rows = {}
@@ -630,7 +628,7 @@
     pooled = CROWS * faces * CCOLS * tiles
     split1, head = call(
         split_kernel,
-        (shape(MAPS, 3 * CH1, (CROWS + 2 * UP2) * 128, dtype=bf16), shape(3, 8, 128)),
+        (shape(MAPS, 2 * CH1, (CROWS + 2 * UP2) * 128, dtype=bf16), shape(3, 8, 128)),
         sig1, far2, near2, shift, labels8, out_weight[None],
     )
     logits, grads, dpre0 = call(

time: 119 us -> 113 us (0.950)
  other arithmetic: 3.18 us -> 0.35 us
  local copies, waits for them, and re-layouts: 7.72 us -> 5.04 us
  waiting for transfers between devices: 12.1 us -> 13.7 us
    unnamed x30 -> x18, local copies, waits for them, and re-layouts: 6.02 us -> 4.1 us
  transfers between devices with their start and end apart: 13 -> 13, of which waited for: 6 -> 6; matrix products, arithmetic and copies ran while one was open for 5% -> 1% of each run, Pallas kernels for 3% -> 4%
where the time goes in v6:
time: 113 us; the launch traced here: 111 us
  starting transfers between devices  64.4 us (57%)
  blocking collectives  14 us (12%)
  waiting for transfers between devices  13.7 us (12%)
  Pallas kernels  12.9 us (11%)
  local copies, waits for them, and re-layouts  5.04 us (4%)
    ppermute x5, starting transfers between devices, exchange(): lax.ppermute(near_value, axis, near)  24.8 us
    ppermute x5, starting transfers between devices, exchange(): lax.ppermute(far_value, axis, far)  20.1 us
    all_to_all x3, starting transfers between devices, share(): return lax.all_to_all(rows, axes, 0, 0, tiled=True)  19.5 us
    all_to_all x1, blocking collectives, share(): return lax.all_to_all(rows, axes, 0, 0, tiled=True)  14 us
    pallas_call x12, Pallas kernels, call(): pl.pallas_call(kernel, out_shape=outs, in_specs=in_specs, out_specs=jax.t...  12.9 us
    all_to_all x3, waiting for transfers between devices, share(): return lax.all_to_all(rows, axes, 0, 0, tiled=True)  11.1 us
    unnamed x18, local copies, waits for them, and re-layouts  4.1 us
    ppermute x5, waiting for transfers between devices, exchange(): lax.ppermute(near_value, axis, near)  2.58 us
  transfers between devices with their start and end apart: 13, of which 6 were waited for; matrix products, arithmetic and copies ran while one was open for 1% of the time, Pallas kernels for 4%

profile of v6, /device:TPU:1, one launch (start us, length us, event | category | flops | bytes accessed | tf_op | source)
XLA Modules:
  0.0 111.5 jit_solution(3914485392704221665)
XLA Ops:
  0.7 0.8 copy-done.2
  1.5 0.1 shard_map.120
  1.6 6.2 %collective-permute-start = (f32[12,16,128]{2,1,0:T(8,128)S(1)}, f32[12,16,128]{2,1,0:T(8,128)S(1)}, u32[]{:S(2)}, u32[]{:S(2)}) collective-permute-start(f32[12,16,128]{2,1,0:T(8,128)S(1)} %get-tuple-element.30), channel_id=1, source_target_pairs={{0,448},{64,128},{128,64},{192,256},{256,192},{320,384},{384,320},... | collective-permute-start | bytes 294920 | tf_op jit(solution)/shard_map/ppermute | solution.py:553
  7.8 1.9 %collective-permute-start.1 = (f32[12,16,128]{2,1,0:T(8,128)S(1)}, f32[12,16,128]{2,1,0:T(8,128)S(1)}, u32[]{:S(2)}, u32[]{:S(2)}) collective-permute-start(f32[12,16,128]{2,1,0:T(8,128)S(1)} %get-tuple-element.31), channel_id=1, source_target_pairs={{0,64},{64,0},{128,192},{192,128},{256,320},{320,256},{384,448},{4... | collective-permute-start | bytes 294920 | tf_op jit(solution)/shard_map/ppermute | solution.py:553
  9.7 0.1 multiply_bitcast_fusion
  9.8 0.1 reshape.29
  10.0 0.6 copy-done.8
  10.6 0.7 copy-done.7
  11.3 0.2 fusion.1.shift_ref
  11.5 1.7 %collective-permute-done.1.near_ref = f32[12,16,128]{2,1,0:T(8,128)S(1)} collective-permute-done((f32[12,16,128]{2,1,0:T(8,128)S(1)}, f32[12,16,128]{2,1,0:T(8,128)S(1)}, u32[]{:S(2)}, u32[]{:S(2)}) %collective-permute-start.1) | collective-permute-done | bytes 98336 | tf_op jit(solution)/shard_map/ppermute | solution.py:553
  13.2 0.2 shard_map.121
  13.3 6.5 %collective-permute-start.2 = (f32[2,16,128]{2,1,0:T(8,128)S(1)}, f32[2,16,128]{2,1,0:T(8,128)S(1)}, u32[]{:S(2)}, u32[]{:S(2)}) collective-permute-start(f32[2,16,128]{2,1,0:T(8,128)S(1)} %get-tuple-element.33), channel_id=1, source_target_pairs={{0,63},{1,2},{2,1},{3,4},{4,3},{5,6},{6,5},{7,8},{8,7},{9,10},{10,... | collective-permute-start | bytes 49160 | tf_op jit(solution)/shard_map/ppermute | solution.py:553
  19.9 9.2 %collective-permute-start.3 = (f32[2,16,128]{2,1,0:T(8,128)S(1)}, f32[2,16,128]{2,1,0:T(8,128)S(1)}, u32[]{:S(2)}, u32[]{:S(2)}) collective-permute-start(f32[2,16,128]{2,1,0:T(8,128)S(1)} %get-tuple-element.34), channel_id=1, source_target_pairs={{0,1},{1,0},{2,3},{3,2},{4,5},{5,4},{6,7},{7,6},{8,9},{9,8},{10,11... | collective-permute-start | bytes 49160 | tf_op jit(solution)/shard_map/ppermute | solution.py:553
  29.1 0.1 copy.17.w_ref
  29.2 0.7 copy-done.4
  29.9 0.1 copy.18
  30.0 0.6 copy-done.1
  30.6 2.1 %shard_map.122 = (f32[18,64,128]{2,1,0:T(8,128)S(1)}, f32[20,64,128]{2,1,0:T(8,128)S(1)}, bf16[80,2048]{1,0:T(8,128)(2,1)S(1)}, f32[1,64,128]{2,1,0:T(8,128)S(1)}, f32[1,64,128]{2,1,0:T(8,128)S(1)}) custom-call(s32[8,64]{1,0:T(8,128)S(1)} %copy-done.1, f32[12,16,128]{2,1,0:T(8,128)S(1)} %collective-permute-done.far_ref, ...), custom_call_target="tpu_custom_call" | custom-call | tf_op jit(solution)/shard_map/pallas_call | solution.py:535
  32.6 1.9 %collective-permute-start.4 = (f32[1,64,128]{2,1,0:T(8,128)S(1)}, f32[1,64,128]{2,1,0:T(8,128)S(1)}, u32[]{:S(2)}, u32[]{:S(2)}) collective-permute-start(f32[1,64,128]{2,1,0:T(8,128)S(1)} %get-tuple-element.36), channel_id=1, source_target_pairs={{0,63},{1,2},{2,1},{3,4},{4,3},{5,6},{6,5},{7,8},{8,7},{9,10},{10,... | collective-permute-start | bytes 98312 | tf_op jit(solution)/shard_map/ppermute | solution.py:553
  34.6 5.3 %collective-permute-start.5 = (f32[1,64,128]{2,1,0:T(8,128)S(1)}, f32[1,64,128]{2,1,0:T(8,128)S(1)}, u32[]{:S(2)}, u32[]{:S(2)}) collective-permute-start(f32[1,64,128]{2,1,0:T(8,128)S(1)} %get-tuple-element.37), channel_id=1, source_target_pairs={{0,1},{1,0},{2,3},{3,2},{4,5},{5,4},{6,7},{7,6},{8,9},{9,8},{10,11... | collective-permute-start | bytes 98312 | tf_op jit(solution)/shard_map/ppermute | solution.py:553
  39.9 0.1 pad_maximum_fusion.3.w_ref
  40.0 0.7 collective-permute-done.5.near_ref
  40.7 2.4 %shard_map.123 = (f32[32,128]{1,0:T(8,128)}, f32[7,128,128]{2,1,0:T(8,128)S(1)}, bf16[4,144,896]{2,1,0:T(8,128)(2,1)S(1)}) custom-call(s32[8,64]{1,0:T(8,128)S(1)} %copy-done.1, f32[18,64,128]{2,1,0:T(8,128)S(1)} %get-tuple-element.35.x1_ref, f32[1,64,128]{2,1,0:T(8,128)S(1)} %collective-permute-done.4.far_ref, ...), custom_call_target="tpu_custom_call" | custom-call | tf_op jit(solution)/shard_map/pallas_call | solution.py:535
  43.1 9.6 %all-to-all-start = ((f32[32,1,128]{2,1,0:T(1,128)}), f32[32,1,128]{2,1,0:T(1,128)S(1)}, u32[]{:S(2)}, u32[]{:S(2)}) async-start(f32[32,1,128]{2,1,0:T(1,128)} %bitcast.6), calls=%async_computation | async-start | bytes 32768 | tf_op jit(solution)/shard_map/all_to_all | solution.py:557
  52.7 0.1 pad_maximum_fusion.4.refs_4_
  52.8 0.5 shard_map.125
  53.3 1.9 %collective-permute-start.6 = (f32[128,128]{1,0:T(8,128)S(1)}, f32[128,128]{1,0:T(8,128)S(1)}, u32[]{:S(2)}, u32[]{:S(2)}) collective-permute-start(f32[128,128]{1,0:T(8,128)S(1)} %get-tuple-element.41), channel_id=1, source_target_pairs={{0,63},{1,2},{2,1},{3,4},{4,3},{5,6},{6,5},{7,8},{8,7},{9,10},{10,... | collective-permute-start | bytes 196616 | tf_op jit(solution)/shard_map/ppermute | solution.py:553
  55.2 4.3 %collective-permute-start.7 = (f32[128,128]{1,0:T(8,128)S(1)}, f32[128,128]{1,0:T(8,128)S(1)}, u32[]{:S(2)}, u32[]{:S(2)}) collective-permute-start(f32[128,128]{1,0:T(8,128)S(1)} %get-tuple-element.42), channel_id=1, source_target_pairs={{0,1},{1,0},{2,3},{3,2},{4,5},{5,4},{6,7},{7,6},{8,9},{9,8},{10,11... | collective-permute-start | bytes 196616 | tf_op jit(solution)/shard_map/ppermute | solution.py:553
  59.5 4.9 %all-to-all-done = f32[32,1,128]{2,1,0:T(1,128)S(1)} async-done(((f32[32,1,128]{2,1,0:T(1,128)}), f32[32,1,128]{2,1,0:T(1,128)S(1)}, u32[]{:S(2)}, u32[]{:S(2)}) %all-to-all-start) | async-done | bytes 16416 | tf_op jit(solution)/shard_map/all_to_all | solution.py:557
  64.4 0.6 shard_map.124
  65.0 3.5 %all-to-all-start.1 = ((f32[16,1,128]{2,1,0:T(1,128)}), f32[16,1,128]{2,1,0:T(1,128)S(1)}, u32[]{:S(2)}, u32[]{:S(2)}) async-start(f32[16,1,128]{2,1,0:T(1,128)} %bitcast.9), calls=%async_computation.1 | async-start | bytes 16384 | tf_op jit(solution)/shard_map/all_to_all | solution.py:557
  68.6 0.1 broadcast_in_dim.15.labels_ref
  68.6 0.7 copy-done.3
  69.3 0.7 shard_map.126
  70.0 4.9 %all-to-all-done.1 = f32[16,1,128]{2,1,0:T(1,128)S(1)} async-done(((f32[16,1,128]{2,1,0:T(1,128)}), f32[16,1,128]{2,1,0:T(1,128)S(1)}, u32[]{:S(2)}, u32[]{:S(2)}) %all-to-all-start.1) | async-done | bytes 8224 | tf_op jit(solution)/shard_map/all_to_all | solution.py:557
  74.8 2.8 %shard_map.127 = (f32[8,128]{1,0:T(8,128)S(1)}, f32[512,128]{1,0:T(8,128)S(1)}, bf16[192,2560]{1,0:T(8,128)(2,1)S(1)}) custom-call(s32[8,64]{1,0:T(8,128)S(1)} %copy-done.1, f32[16,128]{1,0:T(8,128)S(1)} %bitcast.33, f32[3,8,128]{2,1,0:T(8,128)S(1)} %get-tuple-element.43.refs_2_, f32[128,128]{1,0:T(8,128)S(1)} %pad_maximum_fusion.1.refs_3_, ...), custom_call_target="tpu_custom_call" | custom-call | tf_op jit(solution)/shard_map/pallas_call | solution.py:535
  77.6 14.0 %all_to_all.44 = f32[32,16,128]{2,1,0:T(8,128)S(1)} all-to-all(f32[32,16,128]{2,1,0:T(8,128)S(1)} %bitcast.30), channel_id=1, replica_groups=mesh['x'=4,'y_lo'=2,'z'=16,'y_hi'=2,'core'=2] {'x','y_lo','y_hi','core'}, dimensions={0} | all-to-all | bytes 524288 | tf_op jit(solution)/shard_map/all_to_all | solution.py:557
  91.6 0.7 shard_map.130
  92.3 6.4 %all-to-all-start.3 = ((f32[16,16,128]{2,1,0:T(8,128)}), f32[16,16,128]{2,1,0:T(8,128)S(1)}, u32[]{:S(2)}, u32[]{:S(2)}) async-start(f32[16,16,128]{2,1,0:T(8,128)} %bitcast.18), calls=%async_computation.3 | async-start | bytes 262144 | tf_op jit(solution)/shard_map/all_to_all | solution.py:557
  98.8 0.1 pad_maximum_fusion.2.w0_ref
  98.8 0.4 shard_map.128
  99.2 3.5 %collective-permute-start.8 = (f32[1,32,128]{2,1,0:T(8,128)S(1)}, f32[1,32,128]{2,1,0:T(8,128)S(1)}, u32[]{:S(2)}, u32[]{:S(2)}) collective-permute-start(f32[1,32,128]{2,1,0:T(8,128)S(1)} %get-tuple-element.51), channel_id=1, source_target_pairs={{0,63},{1,2},{2,1},{3,4},{4,3},{5,6},{6,5},{7,8},{8,7},{9,10},{10,... | collective-permute-start | bytes 49160 | tf_op jit(solution)/shard_map/ppermute | solution.py:553
  102.7 4.1 %collective-permute-start.9 = (f32[1,32,128]{2,1,0:T(8,128)S(1)}, f32[1,32,128]{2,1,0:T(8,128)S(1)}, u32[]{:S(2)}, u32[]{:S(2)}) collective-permute-start(f32[1,32,128]{2,1,0:T(8,128)S(1)} %get-tuple-element.52), channel_id=1, source_target_pairs={{0,1},{1,0},{2,3},{3,2},{4,5},{5,4},{6,7},{7,6},{8,9},{9,8},{10,11... | collective-permute-start | bytes 49160 | tf_op jit(solution)/shard_map/ppermute | solution.py:553
  106.8 0.6 slice_reduce_fusion
  107.4 0.2 collective-permute-done.9.refs_3_
  107.6 1.9 %shard_map.129 = f32[256,128]{1,0:T(8,128)} custom-call(s32[8,64]{1,0:T(8,128)S(1)} %copy-done.1, f32[20,48,128]{2,1,0:T(8,128)S(1)} %get-tuple-element.50.refs_1_, f32[1,32,128]{2,1,0:T(8,128)S(1)} %collective-permute-done.8.refs_2_, f32[1,32,128]{2,1,0:T(8,128)S(1)} %collective-permute-done.9.refs_3_), custom_call_target="tpu_custom_call" | custom-call | tf_op jit(solution)/shard_map/pallas_call | solution.py:535
  109.5 1.3 %all-to-all-done.3 = f32[16,16,128]{2,1,0:T(8,128)S(1)} async-done(((f32[16,16,128]{2,1,0:T(8,128)}), f32[16,16,128]{2,1,0:T(8,128)S(1)}, u32[]{:S(2)}, u32[]{:S(2)}) %all-to-all-start.3) | async-done | bytes 131104 | tf_op jit(solution)/shard_map/all_to_all | solution.py:557
  110.8 0.7 shard_map.131
  (25 shorter events, 0.1 us)
Async XLA Ops:
  0.6 10.0 %copy-start = (f32[2,128]{1,0:T(2,128)S(1)}, f32[2,128]{1,0:T(2,128)}, u32[]{:S(2)}) copy-start(f32[2,128]{1,0:T(2,128)} %param.16) | copy-start | bytes 3076
  0.6 0.8 copy-start.2
  1.5 8.2 %copy-start.6 = (f32[3,4,16]{2,1,0:T(4,128)S(1)}, f32[3,4,16]{2,1,0:T(4,128)}, u32[]{:S(2)}) copy-start(f32[3,4,16]{2,1,0:T(4,128)} %param.13) | copy-start | bytes 2308
  1.6 9.9 %collective-permute-start = (f32[12,16,128]{2,1,0:T(8,128)S(1)}, f32[12,16,128]{2,1,0:T(8,128)S(1)}, u32[]{:S(2)}, u32[]{:S(2)}) collective-permute-start(f32[12,16,128]{2,1,0:T(8,128)S(1)} %get-tuple-element.30), channel_id=1, source_target_pairs={{0,448},{64,128},{128,64},{192,256},{256,192},{320,384},{384,320},... | collective-permute-start | bytes 294920 | tf_op jit(solution)/shard_map/ppermute | solution.py:553
  7.8 5.4 %collective-permute-start.1 = (f32[12,16,128]{2,1,0:T(8,128)S(1)}, f32[12,16,128]{2,1,0:T(8,128)S(1)}, u32[]{:S(2)}, u32[]{:S(2)}) collective-permute-start(f32[12,16,128]{2,1,0:T(8,128)S(1)} %get-tuple-element.31), channel_id=1, source_target_pairs={{0,64},{64,0},{128,192},{192,128},{256,320},{320,256},{384,448},{4... | collective-permute-start | bytes 294920 | tf_op jit(solution)/shard_map/ppermute | solution.py:553
  9.9 0.7 copy-start.8
  10.6 0.7 copy-start.7
  13.2 15.9 %copy-start.5 = (f32[32,128]{1,0:T(8,128)S(1)}, f32[32,128]{1,0:T(8,128)}, u32[]{:S(2)}) copy-start(f32[32,128]{1,0:T(8,128)} %param.15) | copy-start | bytes 49156
  13.3 16.6 %collective-permute-start.2 = (f32[2,16,128]{2,1,0:T(8,128)S(1)}, f32[2,16,128]{2,1,0:T(8,128)S(1)}, u32[]{:S(2)}, u32[]{:S(2)}) collective-permute-start(f32[2,16,128]{2,1,0:T(8,128)S(1)} %get-tuple-element.33), channel_id=1, source_target_pairs={{0,63},{1,2},{2,1},{3,4},{4,3},{5,6},{6,5},{7,8},{8,7},{9,10},{10,... | collective-permute-start | bytes 49160 | tf_op jit(solution)/shard_map/ppermute | solution.py:553
  19.9 10.1 %collective-permute-start.3 = (f32[2,16,128]{2,1,0:T(8,128)S(1)}, f32[2,16,128]{2,1,0:T(8,128)S(1)}, u32[]{:S(2)}, u32[]{:S(2)}) collective-permute-start(f32[2,16,128]{2,1,0:T(8,128)S(1)} %get-tuple-element.34), channel_id=1, source_target_pairs={{0,1},{1,0},{2,3},{3,2},{4,5},{5,4},{6,7},{7,6},{8,9},{9,8},{10,11... | collective-permute-start | bytes 49160 | tf_op jit(solution)/shard_map/ppermute | solution.py:553
  29.1 0.7 copy-start.4
  29.9 0.7 copy-start.1
  32.6 7.3 %collective-permute-start.4 = (f32[1,64,128]{2,1,0:T(8,128)S(1)}, f32[1,64,128]{2,1,0:T(8,128)S(1)}, u32[]{:S(2)}, u32[]{:S(2)}) collective-permute-start(f32[1,64,128]{2,1,0:T(8,128)S(1)} %get-tuple-element.36), channel_id=1, source_target_pairs={{0,63},{1,2},{2,1},{3,4},{4,3},{5,6},{6,5},{7,8},{8,7},{9,10},{10,... | collective-permute-start | bytes 98312 | tf_op jit(solution)/shard_map/ppermute | solution.py:553
  34.6 6.1 %collective-permute-start.5 = (f32[1,64,128]{2,1,0:T(8,128)S(1)}, f32[1,64,128]{2,1,0:T(8,128)S(1)}, u32[]{:S(2)}, u32[]{:S(2)}) collective-permute-start(f32[1,64,128]{2,1,0:T(8,128)S(1)} %get-tuple-element.37), channel_id=1, source_target_pairs={{0,1},{1,0},{2,3},{3,2},{4,5},{5,4},{6,7},{7,6},{8,9},{9,8},{10,11... | collective-permute-start | bytes 98312 | tf_op jit(solution)/shard_map/ppermute | solution.py:553
  43.1 21.3 %all-to-all-start = ((f32[32,1,128]{2,1,0:T(1,128)}), f32[32,1,128]{2,1,0:T(1,128)S(1)}, u32[]{:S(2)}, u32[]{:S(2)}) async-start(f32[32,1,128]{2,1,0:T(1,128)} %bitcast.6), calls=%async_computation | async-start | bytes 32768 | tf_op jit(solution)/shard_map/all_to_all | solution.py:557
  53.3 15.3 %collective-permute-start.6 = (f32[128,128]{1,0:T(8,128)S(1)}, f32[128,128]{1,0:T(8,128)S(1)}, u32[]{:S(2)}, u32[]{:S(2)}) collective-permute-start(f32[128,128]{1,0:T(8,128)S(1)} %get-tuple-element.41), channel_id=1, source_target_pairs={{0,63},{1,2},{2,1},{3,4},{4,3},{5,6},{6,5},{7,8},{8,7},{9,10},{10,... | collective-permute-start | bytes 196616 | tf_op jit(solution)/shard_map/ppermute | solution.py:553
  55.2 13.3 %collective-permute-start.7 = (f32[128,128]{1,0:T(8,128)S(1)}, f32[128,128]{1,0:T(8,128)S(1)}, u32[]{:S(2)}, u32[]{:S(2)}) collective-permute-start(f32[128,128]{1,0:T(8,128)S(1)} %get-tuple-element.42), channel_id=1, source_target_pairs={{0,1},{1,0},{2,3},{3,2},{4,5},{5,4},{6,7},{7,6},{8,9},{9,8},{10,11... | collective-permute-start | bytes 196616 | tf_op jit(solution)/shard_map/ppermute | solution.py:553
  65.0 9.8 %all-to-all-start.1 = ((f32[16,1,128]{2,1,0:T(1,128)}), f32[16,1,128]{2,1,0:T(1,128)S(1)}, u32[]{:S(2)}, u32[]{:S(2)}) async-start(f32[16,1,128]{2,1,0:T(1,128)} %bitcast.9), calls=%async_computation.1 | async-start | bytes 16384 | tf_op jit(solution)/shard_map/all_to_all | solution.py:557
  68.6 0.7 copy-start.3
  92.3 18.5 %all-to-all-start.3 = ((f32[16,16,128]{2,1,0:T(8,128)}), f32[16,16,128]{2,1,0:T(8,128)S(1)}, u32[]{:S(2)}, u32[]{:S(2)}) async-start(f32[16,16,128]{2,1,0:T(8,128)} %bitcast.18), calls=%async_computation.3 | async-start | bytes 262144 | tf_op jit(solution)/shard_map/all_to_all | solution.py:557
  99.2 8.2 %collective-permute-start.8 = (f32[1,32,128]{2,1,0:T(8,128)S(1)}, f32[1,32,128]{2,1,0:T(8,128)S(1)}, u32[]{:S(2)}, u32[]{:S(2)}) collective-permute-start(f32[1,32,128]{2,1,0:T(8,128)S(1)} %get-tuple-element.51), channel_id=1, source_target_pairs={{0,63},{1,2},{2,1},{3,4},{4,3},{5,6},{6,5},{7,8},{8,7},{9,10},{10,... | collective-permute-start | bytes 49160 | tf_op jit(solution)/shard_map/ppermute | solution.py:553
  102.7 4.9 %collective-permute-start.9 = (f32[1,32,128]{2,1,0:T(8,128)S(1)}, f32[1,32,128]{2,1,0:T(8,128)S(1)}, u32[]{:S(2)}, u32[]{:S(2)}) collective-permute-start(f32[1,32,128]{2,1,0:T(8,128)S(1)} %get-tuple-element.52), channel_id=1, source_target_pairs={{0,1},{1,0},{2,3},{3,2},{4,5},{5,4},{6,7},{7,6},{8,9},{9,8},{10,11... | collective-permute-start | bytes 49160 | tf_op jit(solution)/shard_map/ppermute | solution.py:553

commit v7 on v6

--- a/solution.py
+++ b/solution.py
@@ -45,14 +45,14 @@
     return high, (value - high.astype(f32)).astype(bf16)
 
 
-def weight_halves(ref, start):
-    high, low = halves(ref[...])
-    column = lax.broadcasted_iota(jnp.int32, ref.shape, 1)
-    return jnp.where(column < start, high.astype(f32), low.astype(f32)).astype(bf16)
-
-
 def dot(a, b):
     return jnp.dot(a, b, preferred_element_type=f32)
+
+
+def dot_halves(weights, high, low):
+    both = dot(jnp.concatenate(halves(weights), axis=0), high)
+    count = weights.shape[0]
+    return both[:count] + both[count:] + dot(weights.astype(bf16), low)
 
 
 def dot_nt(a, b):
@@ -267,14 +267,16 @@
         zero = block[row].astype(bf16)
         one, one_low = split[row]
         two, two_low = halves(2.0 * lap - block[row])
-        for k, part in enumerate((zero, one, two, one_low, two_low, zero, one, two)):
+        for k, part in enumerate((zero, one, two, jnp.zeros_like(zero), one_low, two_low)):
             t_ref[CI * k : CI * (k + 1), at] = part
     own = pl.ds(-low * 128, ROWS * 128)
-    terms_ref[...] = t_ref[0 : 5 * CI, own]
-    weights = weight_halves(w_ref, 5 * CI)
+    terms_ref[: 3 * CI] = t_ref[: 3 * CI, own]
+    terms_ref[3 * CI :] = t_ref[4 * CI :, own]
+    weights = w_ref[...]
     for crow in range(-UP1, CROWS + UP1):
         place = crow + UP1
-        pre = dot(weights, t_ref[:, place * 256 : place * 256 + 256])
+        at = slice(256 * place, 256 * (place + 1))
+        pre = dot_halves(weights, t_ref[: 3 * CI, at], t_ref[3 * CI :, at])
         decay = jnp.exp(-jnp.abs(pre))
         act = jnp.maximum(pre, 0.0) + jnp.log(1.0 + decay)
         if -1 <= crow <= CROWS:
@@ -322,12 +324,11 @@
                 chans = slice(CH0 * m, CH0 * (m + 1))
                 t_ref[m, CH0 * k : CH0 * (k + 1), at] = high[chans]
                 t_ref[m, CH0 * (3 + k) : CH0 * (4 + k), at] = low[chans]
-                t_ref[m, CH0 * (6 + k) : CH0 * (7 + k), at] = high[chans]
-    weights = weight_halves(w_ref, 2 * ORDER * CH0)
+    weights = w_ref[...].T
     own = OWN * 128
     sums = []
     for m in range(MAPS):
-        pre = dot(weights, t_ref[m])
+        pre = dot_halves(weights, t_ref[m, : ORDER * CH0], t_ref[m, ORDER * CH0 :])
         decay = jnp.exp(-jnp.abs(pre))
         inverse = 1.0 / (1.0 + decay)
         sig = jnp.where(pre >= 0, inverse, decay * inverse)
@@ -353,7 +354,7 @@
     ends_copy_ref[...] = ends
     grams = [jnp.zeros((CH0, 128), f32) for _ in range(ORDER)]
     for m in range(MAPS):
-        both = dot_nt(t_ref[m, : 2 * ORDER * CH0, : OWN * 128], s_ref[...])
+        both = dot_nt(t_ref[m, :, : OWN * 128], s_ref[...])
         for k in range(ORDER):
             high = both[CH0 * k : CH0 * (k + 1)]
             low = both[CH0 * (3 + k) : CH0 * (4 + k)]
@@ -392,7 +393,7 @@
     features = jnp.sum(feat_ref[...], axis=0, keepdims=True) * (1.0 / pooled)
     row8 = lax.broadcasted_iota(jnp.int32, (8, 128), 0)
     apart = jnp.where(lanes(8) // CH1 == row8, jnp.broadcast_to(features, (8, 128)), 0.0)
-    fw = fw_ref[...]
+    fw = jnp.concatenate([fw_ref[...]] * MAPS, axis=0)
     shift, labels, out = head_ref[0], head_ref[1], head_ref[2]
     hidden = jnp.tanh(
         jnp.dot(apart, fw, precision=exact, preferred_element_type=f32) + shift
@@ -448,9 +449,8 @@
         high, low = halves(value * sig0_ref[n])
         at = pl.ds(n * 128, 128)
         d_ref[:CA, at] = high
-        d_ref[CA : 2 * CA, at] = low
-        d_ref[2 * CA :, at] = high
-    both = dot_nt(terms_ref[...], d_ref[: 2 * CA, 2 * 128 : (2 + ROWS) * 128])
+        d_ref[CA:, at] = low
+    both = dot_nt(terms_ref[...], d_ref[:, 2 * 128 : (2 + ROWS) * 128])
     lane = lanes(CI)
     row16 = lax.broadcasted_iota(jnp.int32, (CI, 128), 0)
     same = lane % CA // CH0 == row16 // BINS
@@ -473,11 +473,12 @@
 
 
 def terms_kernel(d_ref, w0_ref, g_ref, ends_ref, ends_copy_ref):
-    weights = weight_halves(w0_ref, 2 * CA)
+    weights = w0_ref[...]
     index = end_index(2 * CI)
     filled = []
     for n in range(0, ROWS + 4, 2):
-        value = dot(weights, d_ref[:, n * 128 : (n + 2) * 128])
+        at = slice(128 * n, 128 * (n + 2))
+        value = dot_halves(weights, d_ref[:CA, at], d_ref[CA:, at])
         for step in range(2):
             part = value[:, 128 * step : 128 * (step + 1)]
             g_ref[n + step] = part
@@ -565,12 +566,8 @@
     eye = jnp.eye(MAPS, dtype=f32)
     fine = jnp.einsum("kio,mn->monki", fine_weight, eye)
     fine = fine.transpose(0, 1, 3, 2, 4).reshape(CA, ORDER * CI)
-    fine_forward = jnp.concatenate([fine, fine[:, CI:], fine], axis=1)
-    fine_backward = jnp.concatenate([fine.T] * 3, axis=1)
     coarse = coarse_weight.reshape(ORDER * CH0, CH1)
-    coarse_forward = jnp.concatenate([coarse.T] * 3, axis=1)
     coarse_backward = jnp.concatenate([coarse] * MAPS, axis=1)
-    features4 = jnp.concatenate([feature_weight] * MAPS, axis=0)
     pad = [(0, 8 - MAPS), (0, 0)]
     shift = jnp.dot(jnp.pad(params, pad), param_weight, precision=exact)
     labels8 = jnp.broadcast_to(jnp.pad(labels.astype(f32)[:, None], pad), (8, 128))
@@ -595,10 +592,10 @@
             trade,
             trade,
         ),
-        edge_flip, far, near, own, far0, near0, fine_forward,
+        edge_flip, far, near, own, far0, near0, fine,
         smem=1,
         scratch=[
-            pltpu.VMEM((8 * CI, 2 * crows * 128), bf16),
+            pltpu.VMEM((6 * CI, 2 * crows * 128), bf16),
             pltpu.VMEM(((ROWS + 2 * UP0) * CI, 256), bf16),
             pltpu.VMEM(((ROWS + 2 * UP0 - 2) * CI, 512), bf16),
             pltpu.VMEM((crows * CA, 256), bf16),
@@ -610,9 +607,9 @@
         (
             shape(lax.axis_size(FIRST), CB),
             shape(len(PAIRS), CB, 128),
-            shape(MAPS, 3 * ORDER * CH0, len(PAIRS) * 128, dtype=bf16),
+            shape(MAPS, 2 * ORDER * CH0, len(PAIRS) * 128, dtype=bf16),
         ),
-        edge_flip, x1, far1, near1, coarse_forward,
+        edge_flip, x1, far1, near1, coarse,
         smem=1,
         scratch=[pltpu.VMEM((crows * CA, 256), bf16)],
     )
@@ -636,16 +633,16 @@
         (
             shape(8, 128),
             shape(lax.axis_size(PLANE) * CI, 128),
-            shape(3 * CA, (ROWS + 4) * 128, dtype=bf16),
+            shape(2 * CA, (ROWS + 4) * 128, dtype=bf16),
         ),
-        edge_flip, feats, head, features4, coarse_backward, split1, grams, sig0, terms0,
+        edge_flip, feats, head, feature_weight, coarse_backward, split1, grams, sig0, terms0,
         smem=1,
         scratch=[pltpu.VMEM(((CROWS + 2 * UP2) * CA, 256), bf16)],
     )
     grads = share(grads, PLANE)
     trade = shape(groups(ROWS + 4), 2 * CI, 128)
     g, far3, near3 = call(
-        terms_kernel, (shape(ROWS + 4, ORDER * CI, 128), trade, trade), dpre0, fine_backward
+        terms_kernel, (shape(ROWS + 4, ORDER * CI, 128), trade, trade), dpre0, fine.T
     )
     far3, near3 = exchange(TILE, far3, near3)
     grads = call(again_kernel, shape(lax.axis_size("z") * CI, 128), grads)

time: 113 us -> 113 us (level)
  waiting for transfers between devices: 13.7 us -> 16.2 us
  local copies, waits for them, and re-layouts: 5.04 us -> 2.56 us
    unnamed x18, local copies, waits for them, and re-layouts: 4.1 us -> 1.66 us
    ppermute x5, waiting for transfers between devices: 2.58 us -> 4.69 us  [exchange(): lax.ppermute(near_value, axis, near)]
  transfers between devices with their start and end apart: 13 -> 13, of which waited for: 6 -> 7; matrix products, arithmetic and copies ran while one was open for 1% -> 1% of each run, Pallas kernels for 4% -> 4%
where the time goes in v7:
time: 113 us; the launch traced here: 112 us
  starting transfers between devices  64.5 us (57%)
  waiting for transfers between devices  16.2 us (14%)
  blocking collectives  14 us (12%)
  Pallas kernels  13 us (12%)
  local copies, waits for them, and re-layouts  2.56 us (2%)
    ppermute x5, starting transfers between devices, exchange(): lax.ppermute(near_value, axis, near)  25 us
    ppermute x5, starting transfers between devices, exchange(): lax.ppermute(far_value, axis, far)  20.1 us
    all_to_all x3, starting transfers between devices, share(): return lax.all_to_all(rows, axes, 0, 0, tiled=True)  19.5 us
    all_to_all x1, blocking collectives, share(): return lax.all_to_all(rows, axes, 0, 0, tiled=True)  14 us
    pallas_call x12, Pallas kernels, call(): pl.pallas_call(kernel, out_shape=outs, in_specs=in_specs, out_specs=jax.t...  13 us
    all_to_all x3, waiting for transfers between devices, share(): return lax.all_to_all(rows, axes, 0, 0, tiled=True)  11.5 us
    ppermute x5, waiting for transfers between devices, exchange(): lax.ppermute(near_value, axis, near)  4.69 us
  transfers between devices with their start and end apart: 13, of which 7 were waited for; matrix products, arithmetic and copies ran while one was open for 1% of the time, Pallas kernels for 4%

profile of v7, /device:TPU:1, one launch (start us, length us, event | category | flops | bytes accessed | tf_op | source)
XLA Modules:
  0.0 111.6 jit_solution(9961186810154107678)
XLA Ops:
  0.6 0.0 copy-start
  0.7 0.8 copy-done.3
  1.5 0.1 shard_map.120
  1.6 6.2 %collective-permute-start = (f32[12,16,128]{2,1,0:T(8,128)S(1)}, f32[12,16,128]{2,1,0:T(8,128)S(1)}, u32[]{:S(2)}, u32[]{:S(2)}) collective-permute-start(f32[12,16,128]{2,1,0:T(8,128)S(1)} %get-tuple-element.30), channel_id=1, source_target_pairs={{0,448},{64,128},{128,64},{192,256},{256,192},{320,384},{384,320},... | collective-permute-start | bytes 294920 | tf_op jit(solution)/shard_map/ppermute | solution.py:554
  7.8 1.9 %collective-permute-start.1 = (f32[12,16,128]{2,1,0:T(8,128)S(1)}, f32[12,16,128]{2,1,0:T(8,128)S(1)}, u32[]{:S(2)}, u32[]{:S(2)}) collective-permute-start(f32[12,16,128]{2,1,0:T(8,128)S(1)} %get-tuple-element.31), channel_id=1, source_target_pairs={{0,64},{64,0},{128,192},{192,128},{256,320},{320,256},{384,448},{4... | collective-permute-start | bytes 294920 | tf_op jit(solution)/shard_map/ppermute | solution.py:554
  9.7 0.1 multiply_bitcast_fusion
  9.8 3.3 %collective-permute-done.1.near_ref = f32[12,16,128]{2,1,0:T(8,128)S(1)} collective-permute-done((f32[12,16,128]{2,1,0:T(8,128)S(1)}, f32[12,16,128]{2,1,0:T(8,128)S(1)}, u32[]{:S(2)}, u32[]{:S(2)}) %collective-permute-start.1) | collective-permute-done | bytes 98336 | tf_op jit(solution)/shard_map/ppermute | solution.py:554
  13.2 0.2 shard_map.121
  13.3 0.0 copy-start.7
  13.3 6.5 %collective-permute-start.2 = (f32[2,16,128]{2,1,0:T(8,128)S(1)}, f32[2,16,128]{2,1,0:T(8,128)S(1)}, u32[]{:S(2)}, u32[]{:S(2)}) collective-permute-start(f32[2,16,128]{2,1,0:T(8,128)S(1)} %get-tuple-element.33), channel_id=1, source_target_pairs={{0,63},{1,2},{2,1},{3,4},{4,3},{5,6},{6,5},{7,8},{8,7},{9,10},{10,... | collective-permute-start | bytes 49160 | tf_op jit(solution)/shard_map/ppermute | solution.py:554
  19.9 9.2 %collective-permute-start.3 = (f32[2,16,128]{2,1,0:T(8,128)S(1)}, f32[2,16,128]{2,1,0:T(8,128)S(1)}, u32[]{:S(2)}, u32[]{:S(2)}) collective-permute-start(f32[2,16,128]{2,1,0:T(8,128)S(1)} %get-tuple-element.34), channel_id=1, source_target_pairs={{0,1},{1,0},{2,3},{3,2},{4,5},{5,4},{6,7},{7,6},{8,9},{9,8},{10,11... | collective-permute-start | bytes 49160 | tf_op jit(solution)/shard_map/ppermute | solution.py:554
  29.1 0.2 fusion.1.shift_ref
  29.3 0.1 reshape.29
  29.4 0.0 copy-start.2
  29.5 0.1 copy.15.w_ref
  29.5 0.4 collective-permute-done.3.near0_ref
  29.9 0.2 copy-done.2
  30.1 2.0 %shard_map.122 = (f32[18,64,128]{2,1,0:T(8,128)S(1)}, f32[20,64,128]{2,1,0:T(8,128)S(1)}, bf16[80,2048]{1,0:T(8,128)(2,1)S(1)}, f32[1,64,128]{2,1,0:T(8,128)S(1)}, f32[1,64,128]{2,1,0:T(8,128)S(1)}) custom-call(s32[8,64]{1,0:T(8,128)S(1)} %copy-done.2, f32[12,16,128]{2,1,0:T(8,128)S(1)} %collective-permute-done.far_ref, ...), custom_call_target="tpu_custom_call" | custom-call | tf_op jit(solution)/shard_map/pallas_call | solution.py:536
  32.2 0.0 copy-start.8
  32.2 1.9 %collective-permute-start.4 = (f32[1,64,128]{2,1,0:T(8,128)S(1)}, f32[1,64,128]{2,1,0:T(8,128)S(1)}, u32[]{:S(2)}, u32[]{:S(2)}) collective-permute-start(f32[1,64,128]{2,1,0:T(8,128)S(1)} %get-tuple-element.36), channel_id=1, source_target_pairs={{0,63},{1,2},{2,1},{3,4},{4,3},{5,6},{6,5},{7,8},{8,7},{9,10},{10,... | collective-permute-start | bytes 98312 | tf_op jit(solution)/shard_map/ppermute | solution.py:554
  34.1 5.7 %collective-permute-start.5 = (f32[1,64,128]{2,1,0:T(8,128)S(1)}, f32[1,64,128]{2,1,0:T(8,128)S(1)}, u32[]{:S(2)}, u32[]{:S(2)}) collective-permute-start(f32[1,64,128]{2,1,0:T(8,128)S(1)} %get-tuple-element.37), channel_id=1, source_target_pairs={{0,1},{1,0},{2,3},{3,2},{4,5},{5,4},{6,7},{7,6},{8,9},{9,8},{10,11... | collective-permute-start | bytes 98312 | tf_op jit(solution)/shard_map/ppermute | solution.py:554
  39.9 0.8 collective-permute-done.5.near_ref
  40.7 2.6 %shard_map.123 = (f32[32,128]{1,0:T(8,128)}, f32[7,128,128]{2,1,0:T(8,128)S(1)}, bf16[4,96,896]{2,1,0:T(8,128)(2,1)S(1)}) custom-call(s32[8,64]{1,0:T(8,128)S(1)} %copy-done.2, f32[18,64,128]{2,1,0:T(8,128)S(1)} %get-tuple-element.35.x1_ref, f32[1,64,128]{2,1,0:T(8,128)S(1)} %collective-permute-done.4.far_ref, ...), custom_call_target="tpu_custom_call" | custom-call | tf_op jit(solution)/shard_map/pallas_call | solution.py:536
  43.3 9.6 %all-to-all-start = ((f32[32,1,128]{2,1,0:T(1,128)}), f32[32,1,128]{2,1,0:T(1,128)S(1)}, u32[]{:S(2)}, u32[]{:S(2)}) async-start(f32[32,1,128]{2,1,0:T(1,128)} %bitcast.4), calls=%async_computation | async-start | bytes 32768 | tf_op jit(solution)/shard_map/all_to_all | solution.py:558
  52.8 0.1 pad_maximum_fusion.refs_4_
  52.9 0.5 shard_map.125
  53.4 1.9 %collective-permute-start.6 = (f32[128,128]{1,0:T(8,128)S(1)}, f32[128,128]{1,0:T(8,128)S(1)}, u32[]{:S(2)}, u32[]{:S(2)}) collective-permute-start(f32[128,128]{1,0:T(8,128)S(1)} %get-tuple-element.41), channel_id=1, source_target_pairs={{0,63},{1,2},{2,1},{3,4},{4,3},{5,6},{6,5},{7,8},{8,7},{9,10},{10,... | collective-permute-start | bytes 196616 | tf_op jit(solution)/shard_map/ppermute | solution.py:554
  55.3 4.0 %collective-permute-start.7 = (f32[128,128]{1,0:T(8,128)S(1)}, f32[128,128]{1,0:T(8,128)S(1)}, u32[]{:S(2)}, u32[]{:S(2)}) collective-permute-start(f32[128,128]{1,0:T(8,128)S(1)} %get-tuple-element.42), channel_id=1, source_target_pairs={{0,1},{1,0},{2,3},{3,2},{4,5},{5,4},{6,7},{7,6},{8,9},{9,8},{10,11... | collective-permute-start | bytes 196616 | tf_op jit(solution)/shard_map/ppermute | solution.py:554
  59.3 5.2 %all-to-all-done = f32[32,1,128]{2,1,0:T(1,128)S(1)} async-done(((f32[32,1,128]{2,1,0:T(1,128)}), f32[32,1,128]{2,1,0:T(1,128)S(1)}, u32[]{:S(2)}, u32[]{:S(2)}) %all-to-all-start) | async-done | bytes 16416 | tf_op jit(solution)/shard_map/all_to_all | solution.py:558
  64.6 0.6 shard_map.124
  65.2 3.5 %all-to-all-start.1 = ((f32[16,1,128]{2,1,0:T(1,128)}), f32[16,1,128]{2,1,0:T(1,128)S(1)}, u32[]{:S(2)}, u32[]{:S(2)}) async-start(f32[16,1,128]{2,1,0:T(1,128)} %bitcast.7), calls=%async_computation.1 | async-start | bytes 16384 | tf_op jit(solution)/shard_map/all_to_all | solution.py:558
  68.7 0.0 copy-start.5
  68.7 0.1 broadcast_in_dim.15.labels_ref
  68.8 0.6 copy-done.5
  69.3 0.7 shard_map.126
  70.0 4.9 %all-to-all-done.1 = f32[16,1,128]{2,1,0:T(1,128)S(1)} async-done(((f32[16,1,128]{2,1,0:T(1,128)}), f32[16,1,128]{2,1,0:T(1,128)S(1)}, u32[]{:S(2)}, u32[]{:S(2)}) %all-to-all-start.1) | async-done | bytes 8224 | tf_op jit(solution)/shard_map/all_to_all | solution.py:558
  74.9 2.8 %shard_map.127 = (f32[8,128]{1,0:T(8,128)S(1)}, f32[512,128]{1,0:T(8,128)S(1)}, bf16[128,2560]{1,0:T(8,128)(2,1)S(1)}) custom-call(s32[8,64]{1,0:T(8,128)S(1)} %copy-done.2, f32[16,128]{1,0:T(8,128)S(1)} %bitcast.34, f32[3,8,128]{2,1,0:T(8,128)S(1)} %get-tuple-element.43.refs_2_, f32[32,128]{1,0:T(8,128)S(1)} %copy-done.4, ...), custom_call_target="tpu_custom_call" | custom-call | tf_op jit(solution)/shard_map/pallas_call | solution.py:536
  77.7 14.0 %all_to_all.44 = f32[32,16,128]{2,1,0:T(8,128)S(1)} all-to-all(f32[32,16,128]{2,1,0:T(8,128)S(1)} %bitcast.28), channel_id=1, replica_groups=mesh['x'=4,'y_lo'=2,'z'=16,'y_hi'=2,'core'=2] {'x','y_lo','y_hi','core'}, dimensions={0} | all-to-all | bytes 524288 | tf_op jit(solution)/shard_map/all_to_all | solution.py:558
  91.7 0.7 shard_map.130
  92.4 6.4 %all-to-all-start.3 = ((f32[16,16,128]{2,1,0:T(8,128)}), f32[16,16,128]{2,1,0:T(8,128)S(1)}, u32[]{:S(2)}, u32[]{:S(2)}) async-start(f32[16,16,128]{2,1,0:T(8,128)} %bitcast.16), calls=%async_computation.3 | async-start | bytes 262144 | tf_op jit(solution)/shard_map/all_to_all | solution.py:558
  98.9 0.4 shard_map.128
  99.3 3.5 %collective-permute-start.8 = (f32[1,32,128]{2,1,0:T(8,128)S(1)}, f32[1,32,128]{2,1,0:T(8,128)S(1)}, u32[]{:S(2)}, u32[]{:S(2)}) collective-permute-start(f32[1,32,128]{2,1,0:T(8,128)S(1)} %get-tuple-element.51), channel_id=1, source_target_pairs={{0,63},{1,2},{2,1},{3,4},{4,3},{5,6},{6,5},{7,8},{8,7},{9,10},{10,... | collective-permute-start | bytes 49160 | tf_op jit(solution)/shard_map/ppermute | solution.py:554
  102.8 4.1 %collective-permute-start.9 = (f32[1,32,128]{2,1,0:T(8,128)S(1)}, f32[1,32,128]{2,1,0:T(8,128)S(1)}, u32[]{:S(2)}, u32[]{:S(2)}) collective-permute-start(f32[1,32,128]{2,1,0:T(8,128)S(1)} %get-tuple-element.52), channel_id=1, source_target_pairs={{0,1},{1,0},{2,3},{3,2},{4,5},{5,4},{6,7},{7,6},{8,9},{9,8},{10,11... | collective-permute-start | bytes 49160 | tf_op jit(solution)/shard_map/ppermute | solution.py:554
  106.9 0.6 slice_reduce_fusion
  107.5 0.2 collective-permute-done.9.refs_3_
  107.7 1.9 %shard_map.129 = f32[256,128]{1,0:T(8,128)} custom-call(s32[8,64]{1,0:T(8,128)S(1)} %copy-done.2, f32[20,48,128]{2,1,0:T(8,128)S(1)} %get-tuple-element.50.refs_1_, f32[1,32,128]{2,1,0:T(8,128)S(1)} %collective-permute-done.8.refs_2_, f32[1,32,128]{2,1,0:T(8,128)S(1)} %collective-permute-done.9.refs_3_), custom_call_target="tpu_custom_call" | custom-call | tf_op jit(solution)/shard_map/pallas_call | solution.py:536
  109.6 1.3 %all-to-all-done.3 = f32[16,16,128]{2,1,0:T(8,128)S(1)} async-done(((f32[16,16,128]{2,1,0:T(8,128)}), f32[16,16,128]{2,1,0:T(8,128)S(1)}, u32[]{:S(2)}, u32[]{:S(2)}) %all-to-all-start.3) | async-done | bytes 131104 | tf_op jit(solution)/shard_map/all_to_all | solution.py:558
  110.9 0.7 shard_map.131
  (19 shorter events, 0.0 us)
Async XLA Ops:
  0.6 28.5 %copy-start = (f32[2,128]{1,0:T(2,128)S(1)}, f32[2,128]{1,0:T(2,128)}, u32[]{:S(2)}) copy-start(f32[2,128]{1,0:T(2,128)} %param.16) | copy-start | bytes 3076
  0.6 0.8 copy-start.3
  1.5 8.2 %copy-start.6 = (f32[3,4,16]{2,1,0:T(4,128)S(1)}, f32[3,4,16]{2,1,0:T(4,128)}, u32[]{:S(2)}) copy-start(f32[3,4,16]{2,1,0:T(4,128)} %param.13) | copy-start | bytes 2308
  1.6 8.3 %collective-permute-start = (f32[12,16,128]{2,1,0:T(8,128)S(1)}, f32[12,16,128]{2,1,0:T(8,128)S(1)}, u32[]{:S(2)}, u32[]{:S(2)}) collective-permute-start(f32[12,16,128]{2,1,0:T(8,128)S(1)} %get-tuple-element.30), channel_id=1, source_target_pairs={{0,448},{64,128},{128,64},{192,256},{256,192},{320,384},{384,320},... | collective-permute-start | bytes 294920 | tf_op jit(solution)/shard_map/ppermute | solution.py:554
  7.8 5.4 %collective-permute-start.1 = (f32[12,16,128]{2,1,0:T(8,128)S(1)}, f32[12,16,128]{2,1,0:T(8,128)S(1)}, u32[]{:S(2)}, u32[]{:S(2)}) collective-permute-start(f32[12,16,128]{2,1,0:T(8,128)S(1)} %get-tuple-element.31), channel_id=1, source_target_pairs={{0,64},{64,0},{128,192},{192,128},{256,320},{320,256},{384,448},{4... | collective-permute-start | bytes 294920 | tf_op jit(solution)/shard_map/ppermute | solution.py:554
  13.3 15.8 %copy-start.7 = (f32[4,2]{0,1:T(2,128)S(1)}, f32[4,2]{0,1:T(2,128)}, u32[]{:S(2)}) copy-start(f32[4,2]{0,1:T(2,128)} %param.10) | copy-start | bytes 100
  13.3 16.2 %collective-permute-start.2 = (f32[2,16,128]{2,1,0:T(8,128)S(1)}, f32[2,16,128]{2,1,0:T(8,128)S(1)}, u32[]{:S(2)}, u32[]{:S(2)}) collective-permute-start(f32[2,16,128]{2,1,0:T(8,128)S(1)} %get-tuple-element.33), channel_id=1, source_target_pairs={{0,63},{1,2},{2,1},{3,4},{4,3},{5,6},{6,5},{7,8},{8,7},{9,10},{10,... | collective-permute-start | bytes 49160 | tf_op jit(solution)/shard_map/ppermute | solution.py:554
  19.9 10.1 %collective-permute-start.3 = (f32[2,16,128]{2,1,0:T(8,128)S(1)}, f32[2,16,128]{2,1,0:T(8,128)S(1)}, u32[]{:S(2)}, u32[]{:S(2)}) collective-permute-start(f32[2,16,128]{2,1,0:T(8,128)S(1)} %get-tuple-element.34), channel_id=1, source_target_pairs={{0,1},{1,0},{2,3},{3,2},{4,5},{5,4},{6,7},{7,6},{8,9},{9,8},{10,11... | collective-permute-start | bytes 49160 | tf_op jit(solution)/shard_map/ppermute | solution.py:554
  29.4 0.7 copy-start.2
  30.1 10.6 %copy-start.1 = (f32[3,16,32]{2,1,0:T(8,128)S(1)}, f32[3,16,32]{2,1,0:T(8,128)}, u32[]{:S(2)}) copy-start(f32[3,16,32]{2,1,0:T(8,128)} %param.14) | copy-start | bytes 18436
  32.2 7.7 %copy-start.8 = (s32[4]{0:T(128)S(1)}, s32[4]{0:T(128)}, u32[]{:S(2)}) copy-start(s32[4]{0:T(128)} %param.11) | copy-start | bytes 52
  32.2 7.7 %collective-permute-start.4 = (f32[1,64,128]{2,1,0:T(8,128)S(1)}, f32[1,64,128]{2,1,0:T(8,128)S(1)}, u32[]{:S(2)}, u32[]{:S(2)}) collective-permute-start(f32[1,64,128]{2,1,0:T(8,128)S(1)} %get-tuple-element.36), channel_id=1, source_target_pairs={{0,63},{1,2},{2,1},{3,4},{4,3},{5,6},{6,5},{7,8},{8,7},{9,10},{10,... | collective-permute-start | bytes 98312 | tf_op jit(solution)/shard_map/ppermute | solution.py:554
  34.1 6.6 %collective-permute-start.5 = (f32[1,64,128]{2,1,0:T(8,128)S(1)}, f32[1,64,128]{2,1,0:T(8,128)S(1)}, u32[]{:S(2)}, u32[]{:S(2)}) collective-permute-start(f32[1,64,128]{2,1,0:T(8,128)S(1)} %get-tuple-element.37), channel_id=1, source_target_pairs={{0,1},{1,0},{2,3},{3,2},{4,5},{5,4},{6,7},{7,6},{8,9},{9,8},{10,11... | collective-permute-start | bytes 98312 | tf_op jit(solution)/shard_map/ppermute | solution.py:554
  43.3 21.3 %all-to-all-start = ((f32[32,1,128]{2,1,0:T(1,128)}), f32[32,1,128]{2,1,0:T(1,128)S(1)}, u32[]{:S(2)}, u32[]{:S(2)}) async-start(f32[32,1,128]{2,1,0:T(1,128)} %bitcast.4), calls=%async_computation | async-start | bytes 32768 | tf_op jit(solution)/shard_map/all_to_all | solution.py:558
  53.4 15.3 %collective-permute-start.6 = (f32[128,128]{1,0:T(8,128)S(1)}, f32[128,128]{1,0:T(8,128)S(1)}, u32[]{:S(2)}, u32[]{:S(2)}) collective-permute-start(f32[128,128]{1,0:T(8,128)S(1)} %get-tuple-element.41), channel_id=1, source_target_pairs={{0,63},{1,2},{2,1},{3,4},{4,3},{5,6},{6,5},{7,8},{8,7},{9,10},{10,... | collective-permute-start | bytes 196616 | tf_op jit(solution)/shard_map/ppermute | solution.py:554
  55.3 13.3 %collective-permute-start.7 = (f32[128,128]{1,0:T(8,128)S(1)}, f32[128,128]{1,0:T(8,128)S(1)}, u32[]{:S(2)}, u32[]{:S(2)}) collective-permute-start(f32[128,128]{1,0:T(8,128)S(1)} %get-tuple-element.42), channel_id=1, source_target_pairs={{0,1},{1,0},{2,3},{3,2},{4,5},{5,4},{6,7},{7,6},{8,9},{9,8},{10,11... | collective-permute-start | bytes 196616 | tf_op jit(solution)/shard_map/ppermute | solution.py:554
  65.2 9.8 %all-to-all-start.1 = ((f32[16,1,128]{2,1,0:T(1,128)}), f32[16,1,128]{2,1,0:T(1,128)S(1)}, u32[]{:S(2)}, u32[]{:S(2)}) async-start(f32[16,1,128]{2,1,0:T(1,128)} %bitcast.7), calls=%async_computation.1 | async-start | bytes 16384 | tf_op jit(solution)/shard_map/all_to_all | solution.py:558
  68.7 0.7 copy-start.5
  69.3 5.6 %copy-start.4 = (f32[32,128]{1,0:T(8,128)S(1)}, f32[32,128]{1,0:T(8,128)}, u32[]{:S(2)}) copy-start(f32[32,128]{1,0:T(8,128)} %refs_3_.1) | copy-start | bytes 49156
  92.4 18.4 %all-to-all-start.3 = ((f32[16,16,128]{2,1,0:T(8,128)}), f32[16,16,128]{2,1,0:T(8,128)S(1)}, u32[]{:S(2)}, u32[]{:S(2)}) async-start(f32[16,16,128]{2,1,0:T(8,128)} %bitcast.16), calls=%async_computation.3 | async-start | bytes 262144 | tf_op jit(solution)/shard_map/all_to_all | solution.py:558
  99.3 8.2 %collective-permute-start.8 = (f32[1,32,128]{2,1,0:T(8,128)S(1)}, f32[1,32,128]{2,1,0:T(8,128)S(1)}, u32[]{:S(2)}, u32[]{:S(2)}) collective-permute-start(f32[1,32,128]{2,1,0:T(8,128)S(1)} %get-tuple-element.51), channel_id=1, source_target_pairs={{0,63},{1,2},{2,1},{3,4},{4,3},{5,6},{6,5},{7,8},{8,7},{9,10},{10,... | collective-permute-start | bytes 49160 | tf_op jit(solution)/shard_map/ppermute | solution.py:554
  102.8 4.9 %collective-permute-start.9 = (f32[1,32,128]{2,1,0:T(8,128)S(1)}, f32[1,32,128]{2,1,0:T(8,128)S(1)}, u32[]{:S(2)}, u32[]{:S(2)}) collective-permute-start(f32[1,32,128]{2,1,0:T(8,128)S(1)} %get-tuple-element.52), channel_id=1, source_target_pairs={{0,1},{1,0},{2,3},{3,2},{4,5},{5,4},{6,7},{7,6},{8,9},{9,8},{10,11... | collective-permute-start | bytes 49160 | tf_op jit(solution)/shard_map/ppermute | solution.py:554

commit v8 on v7

--- a/solution.py
+++ b/solution.py
@@ -278,7 +278,7 @@
         at = slice(256 * place, 256 * (place + 1))
         pre = dot_halves(weights, t_ref[: 3 * CI, at], t_ref[3 * CI :, at])
         decay = jnp.exp(-jnp.abs(pre))
-        act = jnp.maximum(pre, 0.0) + jnp.log(1.0 + decay)
+        act = jnp.maximum(pre, 0.0) + jnp.log1p(decay)
         if -1 <= crow <= CROWS:
             inverse = 1.0 / (1.0 + decay)
             sig = jnp.where(pre >= 0, inverse, decay * inverse)
@@ -332,7 +332,7 @@
         decay = jnp.exp(-jnp.abs(pre))
         inverse = 1.0 / (1.0 + decay)
         sig = jnp.where(pre >= 0, inverse, decay * inverse)
-        act = jnp.maximum(pre[:, :own], 0.0) + jnp.log(1.0 + decay[:, :own])
+        act = jnp.maximum(pre[:, :own], 0.0) + jnp.log1p(decay[:, :own])
         sums.append(sum(act[:, 128 * q : 128 * (q + 1)] for q in range(OWN)))
         for q in range(len(PAIRS)):
             sig_ref[q, CH1 * m : CH1 * (m + 1)] = sig[:, 128 * q : 128 * (q + 1)]
@@ -350,6 +350,7 @@
         ends = jnp.where(lanes(CB) // (2 * SLOT) == q, pick(value, index), ends)
         if q < OWN:
             s_ref[:CB, 128 * q : 128 * (q + 1)], s_ref[CB:, 128 * q : 128 * (q + 1)] = halves(value)
+    ends = jnp.where(lanes(CB // 2) < 64, ends[: CB // 2], roll(ends[CB // 2 :], 64))
     ends_ref[...] = ends
     ends_copy_ref[...] = ends
     grams = [jnp.zeros((CH0, 128), f32) for _ in range(ORDER)]
@@ -370,6 +371,7 @@
     here = Place()
     left = before(far_ref[...], near_ref[...], here.odd_tile)
     right = after(far_ref[...], near_ref[...], here.odd_tile)
+    left, right = (jnp.concatenate([side, roll(side, 64)], axis=0) for side in (left, right))
     for n, row in enumerate(range(-UP2, CROWS + UP2)):
         q, half = WHERE[row]
         value = coarse_row(roll(sig1_ref[q], 64 * half), left, right, 2 * q + half)
@@ -615,7 +617,7 @@
     )
     feats = share(feats, FIRST)
     feats = call(row_again_kernel, shape(lax.axis_size(SECOND), CB), feats)
-    trade = shape(CB, 128)
+    trade = shape(CB // 2, 128)
     far2, near2, grams = call(
         gram_kernel, (trade, trade, shape(ORDER, CH0, 128)), sig1, terms1,
         scratch=[pltpu.VMEM((2 * CB, OWN * 128), bf16)],

time: 113 us -> 114 us (level)
  no operation moved by 1% of the time
where the time goes in v8:
time: 114 us; the launch traced here: 112 us
  starting transfers between devices  64.6 us (57%)
  waiting for transfers between devices  16.2 us (14%)
  blocking collectives  14 us (12%)
  Pallas kernels  13.3 us (12%)
  local copies, waits for them, and re-layouts  2.55 us (2%)
    ppermute x5, starting transfers between devices, exchange(): lax.ppermute(near_value, axis, near)  25 us
    ppermute x5, starting transfers between devices, exchange(): lax.ppermute(far_value, axis, far)  20.2 us
    all_to_all x3, starting transfers between devices, share(): return lax.all_to_all(rows, axes, 0, 0, tiled=True)  19.5 us
    all_to_all x1, blocking collectives, share(): return lax.all_to_all(rows, axes, 0, 0, tiled=True)  14 us
    pallas_call x12, Pallas kernels, call(): pl.pallas_call(kernel, out_shape=outs, in_specs=in_specs, out_specs=jax.t...  13.3 us
    all_to_all x3, waiting for transfers between devices, share(): return lax.all_to_all(rows, axes, 0, 0, tiled=True)  11.5 us
    ppermute x5, waiting for transfers between devices, exchange(): lax.ppermute(near_value, axis, near)  4.69 us
  transfers between devices with their start and end apart: 13, of which 7 were waited for; matrix products, arithmetic and copies ran while one was open for 1% of the time, Pallas kernels for 4%

profile of v8, /device:TPU:1, one launch (start us, length us, event | category | flops | bytes accessed | tf_op | source)
XLA Modules:
  0.0 112.0 jit_solution(3625847667158834633)
XLA Ops:
  0.6 0.0 copy-start
  0.7 0.8 copy-done.3
  1.5 0.1 shard_map.120
  1.6 6.2 %collective-permute-start = (f32[12,16,128]{2,1,0:T(8,128)S(1)}, f32[12,16,128]{2,1,0:T(8,128)S(1)}, u32[]{:S(2)}, u32[]{:S(2)}) collective-permute-start(f32[12,16,128]{2,1,0:T(8,128)S(1)} %get-tuple-element.30), channel_id=1, source_target_pairs={{0,448},{64,128},{128,64},{192,256},{256,192},{320,384},{384,320},... | collective-permute-start | bytes 294920 | tf_op jit(solution)/shard_map/ppermute | solution.py:556
  7.8 1.9 %collective-permute-start.1 = (f32[12,16,128]{2,1,0:T(8,128)S(1)}, f32[12,16,128]{2,1,0:T(8,128)S(1)}, u32[]{:S(2)}, u32[]{:S(2)}) collective-permute-start(f32[12,16,128]{2,1,0:T(8,128)S(1)} %get-tuple-element.31), channel_id=1, source_target_pairs={{0,64},{64,0},{128,192},{192,128},{256,320},{320,256},{384,448},{4... | collective-permute-start | bytes 294920 | tf_op jit(solution)/shard_map/ppermute | solution.py:556
  9.7 0.1 multiply_bitcast_fusion
  9.8 0.0 collective-permute-done.far_ref
  9.8 3.3 %collective-permute-done.1.near_ref = f32[12,16,128]{2,1,0:T(8,128)S(1)} collective-permute-done((f32[12,16,128]{2,1,0:T(8,128)S(1)}, f32[12,16,128]{2,1,0:T(8,128)S(1)}, u32[]{:S(2)}, u32[]{:S(2)}) %collective-permute-start.1) | collective-permute-done | bytes 98336 | tf_op jit(solution)/shard_map/ppermute | solution.py:556
  13.2 0.2 shard_map.121
  13.3 0.0 copy-start.7
  13.3 6.5 %collective-permute-start.2 = (f32[2,16,128]{2,1,0:T(8,128)S(1)}, f32[2,16,128]{2,1,0:T(8,128)S(1)}, u32[]{:S(2)}, u32[]{:S(2)}) collective-permute-start(f32[2,16,128]{2,1,0:T(8,128)S(1)} %get-tuple-element.33), channel_id=1, source_target_pairs={{0,63},{1,2},{2,1},{3,4},{4,3},{5,6},{6,5},{7,8},{8,7},{9,10},{10,... | collective-permute-start | bytes 49160 | tf_op jit(solution)/shard_map/ppermute | solution.py:556
  19.9 9.2 %collective-permute-start.3 = (f32[2,16,128]{2,1,0:T(8,128)S(1)}, f32[2,16,128]{2,1,0:T(8,128)S(1)}, u32[]{:S(2)}, u32[]{:S(2)}) collective-permute-start(f32[2,16,128]{2,1,0:T(8,128)S(1)} %get-tuple-element.34), channel_id=1, source_target_pairs={{0,1},{1,0},{2,3},{3,2},{4,5},{5,4},{6,7},{7,6},{8,9},{9,8},{10,11... | collective-permute-start | bytes 49160 | tf_op jit(solution)/shard_map/ppermute | solution.py:556
  29.1 0.2 fusion.1.shift_ref
  29.3 0.1 reshape.29
  29.4 0.0 copy-start.2
  29.5 0.1 copy.15.w_ref
  29.5 0.4 collective-permute-done.3.near0_ref
  29.9 0.2 copy-done.2
  30.1 2.3 %shard_map.122 = (f32[18,64,128]{2,1,0:T(8,128)S(1)}, f32[20,64,128]{2,1,0:T(8,128)S(1)}, bf16[80,2048]{1,0:T(8,128)(2,1)S(1)}, f32[1,64,128]{2,1,0:T(8,128)S(1)}, f32[1,64,128]{2,1,0:T(8,128)S(1)}) custom-call(s32[8,64]{1,0:T(8,128)S(1)} %copy-done.2, f32[12,16,128]{2,1,0:T(8,128)S(1)} %collective-permute-done.far_ref, ...), custom_call_target="tpu_custom_call" | custom-call | tf_op jit(solution)/shard_map/pallas_call | solution.py:538
  32.4 2.1 %collective-permute-start.4 = (f32[1,64,128]{2,1,0:T(8,128)S(1)}, f32[1,64,128]{2,1,0:T(8,128)S(1)}, u32[]{:S(2)}, u32[]{:S(2)}) collective-permute-start(f32[1,64,128]{2,1,0:T(8,128)S(1)} %get-tuple-element.36), channel_id=1, source_target_pairs={{0,63},{1,2},{2,1},{3,4},{4,3},{5,6},{6,5},{7,8},{8,7},{9,10},{10,... | collective-permute-start | bytes 98312 | tf_op jit(solution)/shard_map/ppermute | solution.py:556
  34.5 5.7 %collective-permute-start.5 = (f32[1,64,128]{2,1,0:T(8,128)S(1)}, f32[1,64,128]{2,1,0:T(8,128)S(1)}, u32[]{:S(2)}, u32[]{:S(2)}) collective-permute-start(f32[1,64,128]{2,1,0:T(8,128)S(1)} %get-tuple-element.37), channel_id=1, source_target_pairs={{0,1},{1,0},{2,3},{3,2},{4,5},{5,4},{6,7},{7,6},{8,9},{9,8},{10,11... | collective-permute-start | bytes 98312 | tf_op jit(solution)/shard_map/ppermute | solution.py:556
  40.2 0.8 collective-permute-done.5.near_ref
  41.0 2.6 %shard_map.123 = (f32[32,128]{1,0:T(8,128)}, f32[7,128,128]{2,1,0:T(8,128)S(1)}, bf16[4,96,896]{2,1,0:T(8,128)(2,1)S(1)}) custom-call(s32[8,64]{1,0:T(8,128)S(1)} %copy-done.2, f32[18,64,128]{2,1,0:T(8,128)S(1)} %get-tuple-element.35.x1_ref, f32[1,64,128]{2,1,0:T(8,128)S(1)} %collective-permute-done.4.far_ref, ...), custom_call_target="tpu_custom_call" | custom-call | tf_op jit(solution)/shard_map/pallas_call | solution.py:538
  43.6 9.6 %all-to-all-start = ((f32[32,1,128]{2,1,0:T(1,128)}), f32[32,1,128]{2,1,0:T(1,128)S(1)}, u32[]{:S(2)}, u32[]{:S(2)}) async-start(f32[32,1,128]{2,1,0:T(1,128)} %bitcast.4), calls=%async_computation | async-start | bytes 32768 | tf_op jit(solution)/shard_map/all_to_all | solution.py:560
  53.2 0.1 pad_maximum_fusion.refs_4_
  53.3 0.5 shard_map.125
  53.8 1.9 %collective-permute-start.6 = (f32[64,128]{1,0:T(8,128)S(1)}, f32[64,128]{1,0:T(8,128)S(1)}, u32[]{:S(2)}, u32[]{:S(2)}) collective-permute-start(f32[64,128]{1,0:T(8,128)S(1)} %get-tuple-element.41), channel_id=1, source_target_pairs={{0,63},{1,2},{2,1},{3,4},{4,3},{5,6},{6,5},{7,8},{8,7},{9,10},{10,... | collective-permute-start | bytes 98312 | tf_op jit(solution)/shard_map/ppermute | solution.py:556
  55.7 4.0 %collective-permute-start.7 = (f32[64,128]{1,0:T(8,128)S(1)}, f32[64,128]{1,0:T(8,128)S(1)}, u32[]{:S(2)}, u32[]{:S(2)}) collective-permute-start(f32[64,128]{1,0:T(8,128)S(1)} %get-tuple-element.42), channel_id=1, source_target_pairs={{0,1},{1,0},{2,3},{3,2},{4,5},{5,4},{6,7},{7,6},{8,9},{9,8},{10,11... | collective-permute-start | bytes 98312 | tf_op jit(solution)/shard_map/ppermute | solution.py:556
  59.7 5.2 %all-to-all-done = f32[32,1,128]{2,1,0:T(1,128)S(1)} async-done(((f32[32,1,128]{2,1,0:T(1,128)}), f32[32,1,128]{2,1,0:T(1,128)S(1)}, u32[]{:S(2)}, u32[]{:S(2)}) %all-to-all-start) | async-done | bytes 16416 | tf_op jit(solution)/shard_map/all_to_all | solution.py:560
  64.9 0.6 shard_map.124
  65.5 3.5 %all-to-all-start.1 = ((f32[16,1,128]{2,1,0:T(1,128)}), f32[16,1,128]{2,1,0:T(1,128)S(1)}, u32[]{:S(2)}, u32[]{:S(2)}) async-start(f32[16,1,128]{2,1,0:T(1,128)} %bitcast.7), calls=%async_computation.1 | async-start | bytes 16384 | tf_op jit(solution)/shard_map/all_to_all | solution.py:560
  69.1 0.0 copy-start.5
  69.1 0.1 broadcast_in_dim.15.labels_ref
  69.1 0.6 copy-done.5
  69.7 0.7 shard_map.126
  70.4 4.9 %all-to-all-done.1 = f32[16,1,128]{2,1,0:T(1,128)S(1)} async-done(((f32[16,1,128]{2,1,0:T(1,128)}), f32[16,1,128]{2,1,0:T(1,128)S(1)}, u32[]{:S(2)}, u32[]{:S(2)}) %all-to-all-start.1) | async-done | bytes 8224 | tf_op jit(solution)/shard_map/all_to_all | solution.py:560
  75.3 2.8 %shard_map.127 = (f32[8,128]{1,0:T(8,128)S(1)}, f32[512,128]{1,0:T(8,128)S(1)}, bf16[128,2560]{1,0:T(8,128)(2,1)S(1)}) custom-call(s32[8,64]{1,0:T(8,128)S(1)} %copy-done.2, f32[16,128]{1,0:T(8,128)S(1)} %bitcast.34, f32[3,8,128]{2,1,0:T(8,128)S(1)} %get-tuple-element.43.refs_2_, f32[32,128]{1,0:T(8,128)S(1)} %copy-done.4, ...), custom_call_target="tpu_custom_call" | custom-call | tf_op jit(solution)/shard_map/pallas_call | solution.py:538
  78.1 14.0 %all_to_all.44 = f32[32,16,128]{2,1,0:T(8,128)S(1)} all-to-all(f32[32,16,128]{2,1,0:T(8,128)S(1)} %bitcast.28), channel_id=1, replica_groups=mesh['x'=4,'y_lo'=2,'z'=16,'y_hi'=2,'core'=2] {'x','y_lo','y_hi','core'}, dimensions={0} | all-to-all | bytes 524288 | tf_op jit(solution)/shard_map/all_to_all | solution.py:560
  92.1 0.7 shard_map.130
  92.8 6.4 %all-to-all-start.3 = ((f32[16,16,128]{2,1,0:T(8,128)}), f32[16,16,128]{2,1,0:T(8,128)S(1)}, u32[]{:S(2)}, u32[]{:S(2)}) async-start(f32[16,16,128]{2,1,0:T(8,128)} %bitcast.16), calls=%async_computation.3 | async-start | bytes 262144 | tf_op jit(solution)/shard_map/all_to_all | solution.py:560
  99.2 0.4 shard_map.128
  99.7 3.5 %collective-permute-start.8 = (f32[1,32,128]{2,1,0:T(8,128)S(1)}, f32[1,32,128]{2,1,0:T(8,128)S(1)}, u32[]{:S(2)}, u32[]{:S(2)}) collective-permute-start(f32[1,32,128]{2,1,0:T(8,128)S(1)} %get-tuple-element.51), channel_id=1, source_target_pairs={{0,63},{1,2},{2,1},{3,4},{4,3},{5,6},{6,5},{7,8},{8,7},{9,10},{10,... | collective-permute-start | bytes 49160 | tf_op jit(solution)/shard_map/ppermute | solution.py:556
  103.1 4.1 %collective-permute-start.9 = (f32[1,32,128]{2,1,0:T(8,128)S(1)}, f32[1,32,128]{2,1,0:T(8,128)S(1)}, u32[]{:S(2)}, u32[]{:S(2)}) collective-permute-start(f32[1,32,128]{2,1,0:T(8,128)S(1)} %get-tuple-element.52), channel_id=1, source_target_pairs={{0,1},{1,0},{2,3},{3,2},{4,5},{5,4},{6,7},{7,6},{8,9},{9,8},{10,11... | collective-permute-start | bytes 49160 | tf_op jit(solution)/shard_map/ppermute | solution.py:556
  107.3 0.6 slice_reduce_fusion
  107.9 0.2 collective-permute-done.9.refs_3_
  108.1 1.9 %shard_map.129 = f32[256,128]{1,0:T(8,128)} custom-call(s32[8,64]{1,0:T(8,128)S(1)} %copy-done.2, f32[20,48,128]{2,1,0:T(8,128)S(1)} %get-tuple-element.50.refs_1_, f32[1,32,128]{2,1,0:T(8,128)S(1)} %collective-permute-done.8.refs_2_, f32[1,32,128]{2,1,0:T(8,128)S(1)} %collective-permute-done.9.refs_3_), custom_call_target="tpu_custom_call" | custom-call | tf_op jit(solution)/shard_map/pallas_call | solution.py:538
  109.9 1.3 %all-to-all-done.3 = f32[16,16,128]{2,1,0:T(8,128)S(1)} async-done(((f32[16,16,128]{2,1,0:T(8,128)}), f32[16,16,128]{2,1,0:T(8,128)S(1)}, u32[]{:S(2)}, u32[]{:S(2)}) %all-to-all-start.3) | async-done | bytes 131104 | tf_op jit(solution)/shard_map/all_to_all | solution.py:560
  111.3 0.7 shard_map.131
  (19 shorter events, 0.0 us)
Async XLA Ops:
  0.6 28.5 %copy-start = (f32[2,128]{1,0:T(2,128)S(1)}, f32[2,128]{1,0:T(2,128)}, u32[]{:S(2)}) copy-start(f32[2,128]{1,0:T(2,128)} %param.16) | copy-start | bytes 3076
  0.6 0.8 copy-start.3
  1.5 8.2 %copy-start.6 = (f32[3,4,16]{2,1,0:T(4,128)S(1)}, f32[3,4,16]{2,1,0:T(4,128)}, u32[]{:S(2)}) copy-start(f32[3,4,16]{2,1,0:T(4,128)} %param.13) | copy-start | bytes 2308
  1.6 8.3 %collective-permute-start = (f32[12,16,128]{2,1,0:T(8,128)S(1)}, f32[12,16,128]{2,1,0:T(8,128)S(1)}, u32[]{:S(2)}, u32[]{:S(2)}) collective-permute-start(f32[12,16,128]{2,1,0:T(8,128)S(1)} %get-tuple-element.30), channel_id=1, source_target_pairs={{0,448},{64,128},{128,64},{192,256},{256,192},{320,384},{384,320},... | collective-permute-start | bytes 294920 | tf_op jit(solution)/shard_map/ppermute | solution.py:556
  7.8 5.4 %collective-permute-start.1 = (f32[12,16,128]{2,1,0:T(8,128)S(1)}, f32[12,16,128]{2,1,0:T(8,128)S(1)}, u32[]{:S(2)}, u32[]{:S(2)}) collective-permute-start(f32[12,16,128]{2,1,0:T(8,128)S(1)} %get-tuple-element.31), channel_id=1, source_target_pairs={{0,64},{64,0},{128,192},{192,128},{256,320},{320,256},{384,448},{4... | collective-permute-start | bytes 294920 | tf_op jit(solution)/shard_map/ppermute | solution.py:556
  13.3 15.8 %copy-start.7 = (f32[4,2]{0,1:T(2,128)S(1)}, f32[4,2]{0,1:T(2,128)}, u32[]{:S(2)}) copy-start(f32[4,2]{0,1:T(2,128)} %param.10) | copy-start | bytes 100
  13.3 16.2 %collective-permute-start.2 = (f32[2,16,128]{2,1,0:T(8,128)S(1)}, f32[2,16,128]{2,1,0:T(8,128)S(1)}, u32[]{:S(2)}, u32[]{:S(2)}) collective-permute-start(f32[2,16,128]{2,1,0:T(8,128)S(1)} %get-tuple-element.33), channel_id=1, source_target_pairs={{0,63},{1,2},{2,1},{3,4},{4,3},{5,6},{6,5},{7,8},{8,7},{9,10},{10,... | collective-permute-start | bytes 49160 | tf_op jit(solution)/shard_map/ppermute | solution.py:556
  19.9 10.1 %collective-permute-start.3 = (f32[2,16,128]{2,1,0:T(8,128)S(1)}, f32[2,16,128]{2,1,0:T(8,128)S(1)}, u32[]{:S(2)}, u32[]{:S(2)}) collective-permute-start(f32[2,16,128]{2,1,0:T(8,128)S(1)} %get-tuple-element.34), channel_id=1, source_target_pairs={{0,1},{1,0},{2,3},{3,2},{4,5},{5,4},{6,7},{7,6},{8,9},{9,8},{10,11... | collective-permute-start | bytes 49160 | tf_op jit(solution)/shard_map/ppermute | solution.py:556
  29.4 0.7 copy-start.2
  30.1 10.9 %copy-start.1 = (f32[3,16,32]{2,1,0:T(8,128)S(1)}, f32[3,16,32]{2,1,0:T(8,128)}, u32[]{:S(2)}) copy-start(f32[3,16,32]{2,1,0:T(8,128)} %param.14) | copy-start | bytes 18436
  32.4 7.8 %copy-start.8 = (s32[4]{0:T(128)S(1)}, s32[4]{0:T(128)}, u32[]{:S(2)}) copy-start(s32[4]{0:T(128)} %param.11) | copy-start | bytes 52
  32.4 7.8 %collective-permute-start.4 = (f32[1,64,128]{2,1,0:T(8,128)S(1)}, f32[1,64,128]{2,1,0:T(8,128)S(1)}, u32[]{:S(2)}, u32[]{:S(2)}) collective-permute-start(f32[1,64,128]{2,1,0:T(8,128)S(1)} %get-tuple-element.36), channel_id=1, source_target_pairs={{0,63},{1,2},{2,1},{3,4},{4,3},{5,6},{6,5},{7,8},{8,7},{9,10},{10,... | collective-permute-start | bytes 98312 | tf_op jit(solution)/shard_map/ppermute | solution.py:556
  34.5 6.6 %collective-permute-start.5 = (f32[1,64,128]{2,1,0:T(8,128)S(1)}, f32[1,64,128]{2,1,0:T(8,128)S(1)}, u32[]{:S(2)}, u32[]{:S(2)}) collective-permute-start(f32[1,64,128]{2,1,0:T(8,128)S(1)} %get-tuple-element.37), channel_id=1, source_target_pairs={{0,1},{1,0},{2,3},{3,2},{4,5},{5,4},{6,7},{7,6},{8,9},{9,8},{10,11... | collective-permute-start | bytes 98312 | tf_op jit(solution)/shard_map/ppermute | solution.py:556
  43.6 21.3 %all-to-all-start = ((f32[32,1,128]{2,1,0:T(1,128)}), f32[32,1,128]{2,1,0:T(1,128)S(1)}, u32[]{:S(2)}, u32[]{:S(2)}) async-start(f32[32,1,128]{2,1,0:T(1,128)} %bitcast.4), calls=%async_computation | async-start | bytes 32768 | tf_op jit(solution)/shard_map/all_to_all | solution.py:560
  53.8 15.3 %collective-permute-start.6 = (f32[64,128]{1,0:T(8,128)S(1)}, f32[64,128]{1,0:T(8,128)S(1)}, u32[]{:S(2)}, u32[]{:S(2)}) collective-permute-start(f32[64,128]{1,0:T(8,128)S(1)} %get-tuple-element.41), channel_id=1, source_target_pairs={{0,63},{1,2},{2,1},{3,4},{4,3},{5,6},{6,5},{7,8},{8,7},{9,10},{10,... | collective-permute-start | bytes 98312 | tf_op jit(solution)/shard_map/ppermute | solution.py:556
  55.7 13.3 %collective-permute-start.7 = (f32[64,128]{1,0:T(8,128)S(1)}, f32[64,128]{1,0:T(8,128)S(1)}, u32[]{:S(2)}, u32[]{:S(2)}) collective-permute-start(f32[64,128]{1,0:T(8,128)S(1)} %get-tuple-element.42), channel_id=1, source_target_pairs={{0,1},{1,0},{2,3},{3,2},{4,5},{5,4},{6,7},{7,6},{8,9},{9,8},{10,11... | collective-permute-start | bytes 98312 | tf_op jit(solution)/shard_map/ppermute | solution.py:556
  65.5 9.8 %all-to-all-start.1 = ((f32[16,1,128]{2,1,0:T(1,128)}), f32[16,1,128]{2,1,0:T(1,128)S(1)}, u32[]{:S(2)}, u32[]{:S(2)}) async-start(f32[16,1,128]{2,1,0:T(1,128)} %bitcast.7), calls=%async_computation.1 | async-start | bytes 16384 | tf_op jit(solution)/shard_map/all_to_all | solution.py:560
  69.1 0.7 copy-start.5
  69.7 5.6 %copy-start.4 = (f32[32,128]{1,0:T(8,128)S(1)}, f32[32,128]{1,0:T(8,128)}, u32[]{:S(2)}) copy-start(f32[32,128]{1,0:T(8,128)} %refs_3_.1) | copy-start | bytes 49156
  92.8 18.5 %all-to-all-start.3 = ((f32[16,16,128]{2,1,0:T(8,128)}), f32[16,16,128]{2,1,0:T(8,128)S(1)}, u32[]{:S(2)}, u32[]{:S(2)}) async-start(f32[16,16,128]{2,1,0:T(8,128)} %bitcast.16), calls=%async_computation.3 | async-start | bytes 262144 | tf_op jit(solution)/shard_map/all_to_all | solution.py:560
  99.7 8.2 %collective-permute-start.8 = (f32[1,32,128]{2,1,0:T(8,128)S(1)}, f32[1,32,128]{2,1,0:T(8,128)S(1)}, u32[]{:S(2)}, u32[]{:S(2)}) collective-permute-start(f32[1,32,128]{2,1,0:T(8,128)S(1)} %get-tuple-element.51), channel_id=1, source_target_pairs={{0,63},{1,2},{2,1},{3,4},{4,3},{5,6},{6,5},{7,8},{8,7},{9,10},{10,... | collective-permute-start | bytes 49160 | tf_op jit(solution)/shard_map/ppermute | solution.py:556
  103.1 4.9 %collective-permute-start.9 = (f32[1,32,128]{2,1,0:T(8,128)S(1)}, f32[1,32,128]{2,1,0:T(8,128)S(1)}, u32[]{:S(2)}, u32[]{:S(2)}) collective-permute-start(f32[1,32,128]{2,1,0:T(8,128)S(1)} %get-tuple-element.52), channel_id=1, source_target_pairs={{0,1},{1,0},{2,3},{3,2},{4,5},{5,4},{6,7},{7,6},{8,9},{9,8},{10,11... | collective-permute-start | bytes 49160 | tf_op jit(solution)/shard_map/ppermute | solution.py:556
